TPU v7x, 512 devices: a whole 4x8x8 slice. The times are simulated.
512 devices in a mesh: group: 8 (over y_lo, x), tp: 64 (over z, y_hi, core).
Axes of the slice: x: 4, y: 8 (y_hi: 4, y_lo: 2; y = y_hi * 2 + y_lo), z: 8, core: 2. Of those that a mesh axis runs over, the one named last changes fastest.
Arguments:
- hidden: bfloat16 [1024, 12288], P('group', 'tp')
- q_weight: bfloat16 [12288, 12288], P('group', 'tp'), may hold values from -0.0546875 to 0.0546875
- kv_weight: bfloat16 [12288, 2048], P('group', 'tp'), may hold values from -0.0546875 to 0.0546875
- o_weight: bfloat16 [12288, 12288], P('group', 'tp'), may hold values from -0.3125 to 0.3125
- k_pool: bfloat16 [12288, 32, 1024], P(('group', 'tp'))
- v_pool: bfloat16 [12288, 32, 1024], P(('group', 'tp')), may hold values from -6 to 6
- page_table: int32 [1024, 12], P(('group', 'tp')), may hold values from 0 to 23, as said below
- lengths: int32 [1024], P(('group', 'tp')), may hold values from 1 to 384, as said below
Outputs:
- attended: bfloat16 [1024, 12288], P('group', 'tp')
- new_kv: bfloat16 [1024, 2048], P(('group', 'tp'))
Inputs may be any that keep to these rules, and one draw needn't show every extreme that they name: `page_table`: the 2 requests of each aligned block name each of that device's 24 page slots exactly once. `lengths`: the first request of each aligned block of 2 requests has exactly 384 cached tokens.
All inputs are finite; a program needn't handle non-finite values.
Results may differ from a plain program's by a relative error of at most 0.01.
Values may be sent and summed in bfloat16 or wider, within the bound.
No kernel may reach another device: no remote copies, remote signals or barrier semaphores. Data moves between devices by JAX's collectives and lax.ppermute only.
A program may use at most 64 MiB of HBM per device.

v0:
```python
import jax
import jax.numpy as jnp
from jax import lax
from jax.sharding import PartitionSpec as P

D = 12288
HD = 128


eps = 1e-05


def attend_rows(q_rows, kv_rows, k_pool, v_pool, page_table, lengths):
    nrows = q_rows.shape[0]
    kv_width = k_pool.shape[2]
    kv_heads = kv_width // HD
    per_group = q_rows.shape[1] // HD // kv_heads
    query = q_rows.reshape(nrows, kv_heads, per_group, HD)
    own_keys = kv_rows[:, :kv_width].reshape(nrows, kv_heads, HD)
    own_values = kv_rows[:, kv_width:].reshape(nrows, kv_heads, HD)
    paged_keys = k_pool[page_table].reshape(nrows, -1, kv_heads, HD)
    paged_values = v_pool[page_table].reshape(nrows, -1, kv_heads, HD)
    scale = 1.0 / jnp.sqrt(jnp.float32(HD))
    cached = (
        jnp.einsum("rgph,rcgh->rgpc", query, paged_keys, preferred_element_type=jnp.float32) * scale
    )
    own = jnp.einsum("rgph,rgh->rgp", query, own_keys, preferred_element_type=jnp.float32) * scale
    context = paged_keys.shape[1]
    valid = jnp.arange(context, dtype=jnp.int32)[None, :] < lengths[:, None]
    cached = jnp.where(valid[:, None, None, :], cached, jnp.float32(-1e30))
    top = jnp.maximum(jnp.max(cached, axis=-1), own)
    exp_cached = jnp.exp(cached - top[..., None])
    exp_own = jnp.exp(own - top)
    total = jnp.sum(exp_cached, axis=-1) + exp_own
    weight_cached = (exp_cached / total[..., None]).astype(jnp.bfloat16)
    weight_own = (exp_own / total).astype(jnp.bfloat16)
    mixed = jnp.einsum(
        "rgpc,rcgh->rgph", weight_cached, paged_values, preferred_element_type=jnp.float32
    )
    mixed = mixed + weight_own[..., None].astype(jnp.float32) * own_values[:, :, None, :].astype(
        jnp.float32
    )
    return mixed.astype(jnp.bfloat16).reshape(nrows, -1)


def per_device(hidden, q_weight, kv_weight, o_weight, k_pool, v_pool, page_table, lengths):
    q_whole, kv_whole = (
        lax.all_gather(q_weight, "group", axis=0, tiled=True),
        lax.all_gather(kv_weight, "group", axis=0, tiled=True),
    )
    o_whole = lax.all_gather(o_weight, "group", axis=0, tiled=True)
    piece = lax.all_gather(hidden, "tp", axis=1, tiled=True)
    widened = piece.astype(jnp.float32)
    q_total = jnp.dot(piece, q_whole, preferred_element_type=jnp.float32)
    kv_total = jnp.dot(piece, kv_whole, preferred_element_type=jnp.float32)
    squares = jnp.sum(widened * widened, axis=1)
    inv_rms = lax.rsqrt(squares / D + eps)[:, None]
    queries = (q_total * inv_rms).astype(jnp.bfloat16)
    fresh = (kv_total * inv_rms).astype(jnp.bfloat16)
    q_rows, kv_rows = (
        lax.all_to_all(queries, "tp", split_axis=0, concat_axis=1, tiled=True),
        lax.all_to_all(fresh, "tp", split_axis=0, concat_axis=1, tiled=True),
    )
    mixed = attend_rows(q_rows, kv_rows, k_pool, v_pool, page_table, lengths)
    by_columns = lax.all_to_all(mixed, "tp", split_axis=1, concat_axis=0, tiled=True)
    attended = jnp.dot(
        lax.all_gather(by_columns, "tp", axis=1, tiled=True),
        o_whole,
        preferred_element_type=jnp.float32,
    )
    return (attended.astype(jnp.bfloat16), kv_rows)


def solution(mesh):
    in_specs = (
        P("group", "tp"),
        P("group", "tp"),
        P("group", "tp"),
        P("group", "tp"),
        P(("group", "tp"), None, None),
        P(("group", "tp"), None, None),
        P(("group", "tp"), None),
        P(("group", "tp")),
    )
    out_specs = (P("group", "tp"), P(("group", "tp"), None))
    return jax.shard_map(
        per_device, mesh=mesh, in_specs=in_specs, out_specs=out_specs, check_vma=False
    )
```

profile of v0, /device:TPU:1, one launch (start us, length us, event | category | flops | bytes accessed | tf_op | source)
XLA Modules:
  0.0 330.4 jit_solution(7475533996092343099)
XLA Ops:
  8.0 0.7 all-gather.7.cloned.1.call-update
  9.4 0.7 compare_select_fusion
  10.2 0.7 iota_compare_fusion
  10.9 24.9 %all_gather.17 = bf16[12288,32]{0,1:T(8,128)(2,1)S(1)} all-gather(bf16[1536,32]{0,1:T(8,128)(2,1)} %param.10), channel_id=1, replica_groups=mesh['group'=8,'tp'=64] {'group'}, dimensions={0}, use_global_device_ids=true | all-gather | bytes 884736 | tf_op jit(solution)/shard_map/all_gather | solution.py:49
  35.8 67.1 %all-gather.5.cloned.1.call-done = bf16[128,12288]{0,1:T(8,128)(2,1)} async-done(((bf16[128,192]{0,1:T(8,128)(2,1)}), bf16[128,12288]{0,1:T(8,128)(2,1)}) %all-gather.5.cloned.1.call-update) | async-done | bytes 3145744 | tf_op jit(solution)/shard_map/all_gather | solution.py:52
  102.9 3.2 multiply_reduce_fusion
  106.7 0.7 copy.24
  107.5 7.1 %all-to-all-start.1 = ((bf16[64,2,32]{2,1,0:T(2,128)(2,1)}), bf16[64,2,32]{2,1,0:T(2,128)(2,1)S(1)}, u32[]{:S(2)}, u32[]{:S(2)}) async-start(bf16[64,2,32]{2,1,0:T(2,128)(2,1)} %bitcast.1), calls=%async_computation.1 | async-start | bytes 65536 | tf_op jit(solution)/shard_map/all_to_all | solution.py:62
  114.6 1.9 gather_fusion
  116.5 1.8 copy.31
  118.3 3.3 gather_fusion.1
  121.6 3.1 copy.32
  124.6 1.6 all-to-all-done.1
  126.4 38.2 %all-gather.7.cloned.1.call-done = bf16[12288,192]{0,1:T(8,128)(2,1)} async-done(((bf16[1536,192]{0,1:T(8,128)(2,1)}), bf16[12288,192]{0,1:T(8,128)(2,1)}) %all-gather.7.cloned.1.call-update) | async-done | bytes 4718608 | tf_op jit(solution)/shard_map/all_gather | solution.py:48
  164.6 4.7 %fusion.16 = bf16[128,192]{0,1:T(8,128)(2,1)S(1)} fusion(bf16[12288,192]{0,1:T(8,128)(2,1)} %all-gather.7.cloned.1.call-done, bf16[128,12288]{0,1:T(8,128)(2,1)} %all-gather.5.cloned.1.call-done, f32[128]{0:T(128)S(1)} %add_rsqrt_fusion), kind=kOutput, calls=%fused_computation.12 | convolution fusion | flops 604028928 | bytes 7913984 | tf_op jit(solution)/shard_map/dot_general | solution.py:54
  170.1 12.4 %all-to-all-start = ((bf16[64,2,192]{2,1,0:T(2,128)(2,1)}), bf16[64,2,192]{2,1,0:T(2,128)(2,1)S(1)}, u32[]{:S(2)}, u32[]{:S(2)}) async-start(bf16[64,2,192]{2,1,0:T(2,128)(2,1)} %all_to_all.40), calls=%async_computation | async-start | bytes 131072 | tf_op jit(solution)/shard_map/all_to_all | solution.py:61
  182.7 13.0 %all-to-all-done = bf16[64,2,192]{2,1,0:T(2,128)(2,1)S(1)} async-done(((bf16[64,2,192]{2,1,0:T(2,128)(2,1)}), bf16[64,2,192]{2,1,0:T(2,128)(2,1)S(1)}, u32[]{:S(2)}, u32[]{:S(2)}) %all-to-all-start) | async-done | bytes 49184 | tf_op jit(solution)/shard_map/all_to_all | solution.py:61
  195.9 0.7 fusion.23
  196.9 1.9 fusion.13
  199.0 16.9 %all_to_all.54 = bf16[2,64,192]{2,0,1:T(2,128)(2,1)S(1)} all-to-all(bf16[2,64,192]{2,0,1:T(2,128)(2,1)S(1)} %copy.27), channel_id=1, replica_groups=mesh['group'=8,'tp'=64] {'tp'}, dimensions={1} | all-to-all | bytes 98304 | tf_op jit(solution)/shard_map/all_to_all | solution.py:65
  215.9 0.7 copy.28
  216.7 13.9 %all-gather.11.cloned.1.call-done = bf16[12288,192]{0,1:T(8,128)(2,1)} async-done(((bf16[1536,192]{0,1:T(8,128)(2,1)}), bf16[12288,192]{0,1:T(8,128)(2,1)}) %all-gather.11.cloned.1.call-update) | async-done | bytes 4718608 | tf_op jit(solution)/shard_map/all_gather | solution.py:51
  230.5 88.0 %all-gather.9.cloned.1.call-done = bf16[128,12288]{0,1:T(8,128)(2,1)} async-done(((bf16[128,192]{0,1:T(8,128)(2,1)}), bf16[128,12288]{0,1:T(8,128)(2,1)}) %all-gather.9.cloned.1.call-update) | async-done | bytes 3145744 | tf_op jit(solution)/shard_map/all_gather | solution.py:67
  318.5 5.3 %convolution_convert_fusion = bf16[128,192]{0,1:T(8,128)(2,1)} fusion(bf16[12288,192]{0,1:T(8,128)(2,1)} %all-gather.11.cloned.1.call-done, bf16[128,12288]{0,1:T(8,128)(2,1)} %all-gather.9.cloned.1.call-done), kind=kOutput, calls=%fused_computation.13 | convolution fusion | flops 604004352 | bytes 7913472 | tf_op jit(solution)/shard_map/dot_general | solution.py:66
  (33 shorter events, 3.9 us)
Async XLA Ops:
  7.2 107.4 %copy-start = (bf16[24,32,1024]{2,1,0:T(8,128)(2,1)S(1)}, bf16[24,32,1024]{2,1,0:T(8,128)(2,1)}, u32[]{:S(2)}) copy-start(bf16[24,32,1024]{2,1,0:T(8,128)(2,1)} %param.12) | copy-start | bytes 4718596
  7.2 95.7 %all-gather.5.cloned.1.call-start = ((), (), s32[]{:S(2)}) async-start(), calls=%async_computation.3 | async-start | bytes 3194880 | tf_op jit(solution)/shard_map/all_gather | solution.py:52
  7.9 156.7 %all-gather.7.cloned.1.call-start = ((), (), s32[]{:S(2)}) async-start(), calls=%async_computation.4 | async-start | bytes 5308416 | tf_op jit(solution)/shard_map/all_gather | solution.py:48
  8.7 221.9 %all-gather.11.cloned.1.call-start = ((), (), s32[]{:S(2)}) async-start(), calls=%async_computation.6 | async-start | bytes 5308416 | tf_op jit(solution)/shard_map/all_gather | solution.py:51
  102.9 3.2 copy-start.1
  107.5 18.8 %all-to-all-start.1 = ((bf16[64,2,32]{2,1,0:T(2,128)(2,1)}), bf16[64,2,32]{2,1,0:T(2,128)(2,1)S(1)}, u32[]{:S(2)}, u32[]{:S(2)}) async-start(bf16[64,2,32]{2,1,0:T(2,128)(2,1)} %bitcast.1), calls=%async_computation.1 | async-start | bytes 65536 | tf_op jit(solution)/shard_map/all_to_all | solution.py:62
  126.4 56.2 %copy-start.2 = (bf16[2,2048]{1,0:T(2,128)(2,1)}, bf16[2,2048]{1,0:T(2,128)(2,1)S(1)}, u32[]{:S(2)}) copy-start(bf16[2,2048]{1,0:T(2,128)(2,1)S(1)} %all_to_all.46) | copy-start | bytes 24580
  170.1 25.5 %all-to-all-start = ((bf16[64,2,192]{2,1,0:T(2,128)(2,1)}), bf16[64,2,192]{2,1,0:T(2,128)(2,1)S(1)}, u32[]{:S(2)}, u32[]{:S(2)}) async-start(bf16[64,2,192]{2,1,0:T(2,128)(2,1)} %all_to_all.40), calls=%async_computation | async-start | bytes 131072 | tf_op jit(solution)/shard_map/all_to_all | solution.py:61
  182.6 135.9 %all-gather.9.cloned.1.call-start = ((), (), s32[]{:S(2)}) async-start(), calls=%async_computation.5 | async-start | bytes 3194880 | tf_op jit(solution)/shard_map/all_gather | solution.py:67
Sparse Core Ops, SparseCore 0:
  11.4 91.5 all-gather.4
  105.0 59.5 all-gather.6
  166.7 63.7 all-gather.10
  234.3 84.1 all-gather.8
where the time goes:
time: 331 us; the launch traced here: 330 us
  waiting for transfers between devices  224 us (68%)
  blocking collectives  41.8 us (13%)
  starting transfers between devices  19.7 us (6%)
  between operations  13.9 us (4%)
  matrix products  13.4 us (4%)
  local copies, waits for them, and re-layouts  12.9 us (4%)
  other arithmetic  4.89 us (1%)
    all_gather x1, waiting for transfers between devices, per_device(): lax.all_gather(by_columns, 'tp', axis=1, tiled=True)  88 us
    all_gather x1, waiting for transfers between devices, per_device(): piece = lax.all_gather(hidden, 'tp', axis=1, tiled=True)  67.1 us
    all_gather x1, waiting for transfers between devices, per_device(): lax.all_gather(q_weight, 'group', axis=0, tiled=True)  38.2 us
    all_gather x1, blocking collectives, per_device(): lax.all_gather(kv_weight, 'group', axis=0, tiled=True)  24.9 us
    all_to_all x1, blocking collectives, per_device(): lax.all_to_all(mixed, 'tp', split_axis=1, concat_axis=0, tiled=True)  16.9 us
    all_gather x1, waiting for transfers between devices, per_device(): o_whole = lax.all_gather(o_weight, 'group', axis=0, tiled=True)  13.9 us
    all_to_all x1, waiting for transfers between devices, per_device(): lax.all_to_all(queries, 'tp', split_axis=0, concat_axis=1, tiled=True)  13 us
    all_to_all x1, starting transfers between devices, per_device(): lax.all_to_all(queries, 'tp', split_axis=0, concat_axis=1, tiled=True)  12.4 us
  transfers between devices with their start and end apart: 6, of which 6 were waited for; matrix products, arithmetic and copies ran while one was open for 8% of the time, Pallas kernels for 0%

commit v1 on v0

v1 whole, which is shorter than its diff:
```python
import jax
import jax.numpy as jnp
from jax import lax
from jax.experimental import pallas as pl
from jax.experimental.pallas import tpu as pltpu
from jax.sharding import Mesh, PartitionSpec as P

D = 12288
HD = 128

eps = 1e-05

G = ("yl", "x")
T = ("zq", "zp", "yh", "c")


def attend_rows(q_rows, kv_rows, k_pool, v_pool, page_table, lengths):
    nrows = q_rows.shape[0]
    kv_width = k_pool.shape[2]
    kv_heads = kv_width // HD
    per_group = q_rows.shape[1] // HD // kv_heads
    query = q_rows.reshape(nrows, kv_heads, per_group, HD)
    own_keys = kv_rows[:, :kv_width].reshape(nrows, kv_heads, HD)
    own_values = kv_rows[:, kv_width:].reshape(nrows, kv_heads, HD)
    paged_keys = k_pool[page_table].reshape(nrows, -1, kv_heads, HD)
    paged_values = v_pool[page_table].reshape(nrows, -1, kv_heads, HD)
    scale = 1.0 / jnp.sqrt(jnp.float32(HD))
    cached = (
        jnp.einsum("rgph,rcgh->rgpc", query, paged_keys, preferred_element_type=jnp.float32) * scale
    )
    own = jnp.einsum("rgph,rgh->rgp", query, own_keys, preferred_element_type=jnp.float32) * scale
    context = paged_keys.shape[1]
    valid = jnp.arange(context, dtype=jnp.int32)[None, :] < lengths[:, None]
    cached = jnp.where(valid[:, None, None, :], cached, jnp.float32(-1e30))
    top = jnp.maximum(jnp.max(cached, axis=-1), own)
    exp_cached = jnp.exp(cached - top[..., None])
    exp_own = jnp.exp(own - top)
    total = jnp.sum(exp_cached, axis=-1) + exp_own
    weight_cached = (exp_cached / total[..., None]).astype(jnp.bfloat16)
    weight_own = (exp_own / total).astype(jnp.bfloat16)
    mixed = jnp.einsum(
        "rgpc,rcgh->rgph", weight_cached, paged_values, preferred_element_type=jnp.float32
    )
    mixed = mixed + weight_own[..., None].astype(jnp.float32) * own_values[:, :, None, :].astype(
        jnp.float32
    )
    return mixed.astype(jnp.bfloat16).reshape(nrows, -1)


def a2a(a, axes):
    return lax.all_to_all(a, axes, split_axis=0, concat_axis=0, tiled=True)


NT = (((1,), (1,)), ((), ()))
VMEM = pl.BlockSpec(memory_space=pltpu.VMEM)
SMEM = pl.BlockSpec(memory_space=pltpu.SMEM)


def limit(mib):
    return pltpu.CompilerParams(vmem_limit_bytes=mib * 2**20)


def split_kernel(place, hidden, *out):
    row = lax.broadcasted_iota(jnp.int32, (128, 128), 0)
    col = lax.broadcasted_iota(jnp.int32, (128, 128), 1)
    zp = (place[2] + row // 64) % 2
    core = (place[1] + row // 32) % 2
    goes = ((row // 8) % 4) * 32 + zp * 16 + ((row // 2) % 4) * 4 + core * 2 + row % 2
    pick = jnp.where(goes == col, 1.0, 0.0).astype(jnp.bfloat16)
    rows = lax.dot_general(pick, hidden[...], NT, preferred_element_type=jnp.float32)
    rows = rows.astype(jnp.bfloat16)
    for k in range(4):
        out[k][...] = rows[k * 32 : k * 32 + 32]


def split(place, hidden):
    return pl.pallas_call(
        split_kernel,
        in_specs=[SMEM, VMEM],
        out_specs=[VMEM] * 4,
        compiler_params=limit(4),
        out_shape=[jax.ShapeDtypeStruct((32, 192), jnp.bfloat16)] * 4,
    )(place, hidden)


def copies_kernel(place, same, core, zp, both, out):
    flip_core, flip_zp = place[1] == 1, place[0] == 1
    blocks = []
    for straight, crossed in ((same, core), (zp, both)):
        first = jnp.where(flip_core, crossed[...], straight[...])
        second = jnp.where(flip_core, straight[...], crossed[...])
        blocks.append(jnp.concatenate([first, second], axis=1))
    first = jnp.where(flip_zp, blocks[1], blocks[0])
    second = jnp.where(flip_zp, blocks[0], blocks[1])
    for to in range(16):
        out[to, :32] = first
        out[to, 32:] = second


def copies(place, parts):
    return pl.pallas_call(
        copies_kernel,
        in_specs=[SMEM] + [VMEM] * 4,
        out_specs=VMEM,
        compiler_params=limit(4),
        out_shape=pltpu.HBM((16, 64, 384), jnp.bfloat16),
    )(place, *parts)


def join_kernel(q, kv, out):
    out[:192] = q[...]
    out[192:] = kv[...]


def join(q, kv):
    return pl.pallas_call(
        join_kernel,
        in_specs=[VMEM] * 2,
        out_specs=VMEM,
        compiler_params=limit(4),
        out_shape=jax.ShapeDtypeStruct((224, 1536), jnp.bfloat16),
    )(q, kv)


def gather_kernel(place, own, near, own_other, near_other, weight):
    zp, core = place[0], place[1]
    for piece, z, c in (
        (own, zp, core),
        (near, 1 - zp, core),
        (own_other, zp, 1 - core),
        (near_other, 1 - zp, 1 - core),
    ):
        at = z * 2 + c
        weight[pl.ds(pl.multiple_of(at * 192, 64), 192), :] = piece[:192]
        weight[pl.ds(pl.multiple_of(768 + at * 32, 32), 32), :] = piece[192:]


def gather(place, pieces):
    return pl.pallas_call(
        gather_kernel,
        in_specs=[SMEM] + [VMEM] * 4,
        out_specs=VMEM,
        out_shape=pltpu.HBM((896, 1536), jnp.bfloat16),
        compiler_params=limit(8),
    )(place, *pieces)


def project_kernel(rows, weight, out):
    total = squares = 0
    for y in range(4):
        a = rows[:, y].reshape(128, 384)
        total += lax.dot_general(
            a, weight[:, y * 384 : y * 384 + 384], NT, preferred_element_type=jnp.float32
        )
        wide = a.astype(jnp.float32)
        squares += jnp.sum(wide * wide, axis=1, keepdims=True)
    out[:, :896] = total.astype(jnp.bfloat16)
    high = squares.astype(jnp.bfloat16).astype(jnp.float32)
    lane = lax.broadcasted_iota(jnp.int32, (128, 128), 1)
    extra = jnp.where(lane == 0, high, jnp.where(lane == 1, squares - high, 0.0))
    out[:, 896:] = extra.astype(jnp.bfloat16)


def project(rows, weight):
    return pl.pallas_call(
        project_kernel,
        grid=(2,),
        in_specs=[
            pl.BlockSpec((2, 4, 64, 384), lambda i: (i, 0, 0, 0)),
            pl.BlockSpec((896, 1536), lambda i: (0, 0)),
        ],
        out_specs=pl.BlockSpec((128, 1024), lambda i: (i, 0)),
        out_shape=pltpu.HBM((256, 1024), jnp.bfloat16),
        compiler_params=limit(12),
        cost_estimate=pl.CostEstimate(
            flops=2 * 256 * 1536 * 896, bytes_accessed=4 * 2**20, transcendentals=0
        ),
    )(rows, weight)


def add_kernel(parts, touch, out):
    del touch
    total = jnp.sum(parts[...].astype(jnp.float32), axis=0)
    squares = jnp.sum(total[:, 896:], axis=1, keepdims=True)
    normed = total[:, :896] * lax.rsqrt(squares / D + eps)
    for r in range(8):
        out[r] = normed[2 * r : 2 * r + 2].astype(jnp.bfloat16)


def add(parts, touch):
    return pl.pallas_call(
        add_kernel,
        grid=(2,),
        in_specs=[
            pl.BlockSpec((8, 16, 1024), lambda i: (0, i, 0)),
            pl.BlockSpec((16, 128), lambda i: (0, 0)),
        ],
        out_specs=pl.BlockSpec((8, 2, 896), lambda i: (i, 0, 0)),
        compiler_params=limit(4),
        out_shape=pltpu.HBM((16, 2, 896), jnp.bfloat16),
    )(parts, touch)


def order_kernel(parts, touch, q, kv):
    del touch
    for z in range(8):
        zq, zp = z // 2, z % 2
        for y in range(4):
            q[z, :, y * 384 : y * 384 + 384] = parts[zq * 4 + y, :, zp * 384 : zp * 384 + 384]
        at = 768 + zp * 64
        for y in range(0, 4, 2):
            pair = [parts[zq * 4 + y + k, :, at : at + 64].astype(jnp.float32) for k in range(2)]
            kv[z, :, y * 64 : y * 64 + 128] = jnp.concatenate(pair, axis=1).astype(jnp.bfloat16)


def order(parts, touch):
    return pl.pallas_call(
        order_kernel,
        in_specs=[VMEM] * 2,
        out_specs=[VMEM] * 2,
        compiler_params=limit(4),
        out_shape=[
            jax.ShapeDtypeStruct((8, 2, 1536), jnp.bfloat16),
            jax.ShapeDtypeStruct((8, 2, 256), jnp.bfloat16),
        ],
    )(parts, touch)


def spread_kernel(place, mine, theirs, own, near_a, near_b, out):
    near = jnp.concatenate([near_a[...], near_b[...]], axis=0)
    for weight, to in ((own[...], place[0]), (near, 1 - place[0])):
        first = lax.dot_general(mine[...], weight, NT, preferred_element_type=jnp.float32)
        second = lax.dot_general(theirs[...], weight, NT, preferred_element_type=jnp.float32)
        first, second = first.astype(jnp.bfloat16), second.astype(jnp.bfloat16)
        last = jnp.concatenate([first[:, 128:], second[:, 128:]], axis=1)
        for g in range(8):
            at = slice(g * 32, g * 32 + 32)
            out[g, to, 0:32, :] = first[at, :128]
            out[g, to, 32:64, :] = second[at, :128]
            out[g, to, 64:96, :] = last[at]


def spread(place, mine, theirs, pieces):
    return pl.pallas_call(
        spread_kernel,
        in_specs=[SMEM] + [VMEM] * 5,
        out_specs=VMEM,
        out_shape=jax.ShapeDtypeStruct((8, 2, 96, 128), jnp.bfloat16),
        compiler_params=limit(16),
        cost_estimate=pl.CostEstimate(
            flops=2 * 512 * 1536 * 384, bytes_accessed=4 * 2**20, transcendentals=0
        ),
    )(place, mine, theirs, *pieces)


def collect_kernel(place, parts, out):
    total = jnp.sum(parts[...].astype(jnp.float32), axis=0).astype(jnp.bfloat16)
    rows = []
    for z in range(2):
        rows.append(jnp.concatenate([total[z, 0:32], total[z, 64:96, :64]], axis=1))
        rows.append(jnp.concatenate([total[z, 32:64], total[z, 64:96, 64:]], axis=1))
    rows = jnp.concatenate(rows, axis=0)
    at = lax.broadcasted_iota(jnp.int32, (128, 128), 0)
    to = lax.broadcasted_iota(jnp.int32, (128, 128), 1)
    core = (place[1] + at // 32) % 2
    goes = ((at // 8) % 4) * 32 + (at // 64) * 16 + ((at // 2) % 4) * 4 + core * 2 + at % 2
    pick = jnp.where(goes == to, 1.0, 0.0).astype(jnp.bfloat16)
    out[...] = lax.dot_general(
        rows, pick, (((0,), (0,)), ((), ())), preferred_element_type=jnp.float32
    ).astype(jnp.bfloat16)


def collect(place, parts):
    return pl.pallas_call(
        collect_kernel,
        in_specs=[SMEM, VMEM],
        out_specs=VMEM,
        compiler_params=limit(4),
        out_shape=jax.ShapeDtypeStruct((192, 128), jnp.bfloat16),
    )(place, parts)


OTHER = [(0, 1), (1, 0)]


def per_device(hidden, q_weight, kv_weight, o_weight, k_pool, v_pool, page_table, lengths):
    place = jnp.stack([lax.axis_index("zp"), lax.axis_index("c"), lax.axis_index("x") % 2])
    place = place.astype(jnp.int32)

    parts = split(place, hidden.T)
    parts = [
        lax.ppermute(
            part,
            G + ("zq", "zp", "c"),
            [
                ((g * 8 + z) * 2 + c, (z * 8 + (g ^ (k // 2))) * 2 + (c ^ (k % 2)))
                for g in range(8)
                for z in range(8)
                for c in range(2)
            ],
        )
        for k, part in enumerate(parts)
    ]

    own = join(q_weight.T, kv_weight.T)
    near = lax.ppermute(own, "zp", OTHER)
    pieces = (own, near, lax.ppermute(own, "c", OTHER), lax.ppermute(near, "c", OTHER))

    rows = a2a(copies(place, parts), ("zq", "yh")).reshape(4, 4, 64, 384)
    o_own = o_weight.T
    o_near = [lax.ppermute(half, "zp", OTHER) for half in (o_own[:96], o_own[96:])]

    parts = a2a(project(rows, gather(place, pieces)).reshape(8, 32, 1024), G)
    parts = a2a(add(parts, o_near[0][:16, :128]), ("zq", "yh"))
    q_rows, kv_rows = order(parts, o_near[1][:16, :128])
    q_rows = q_rows.transpose(1, 0, 2).reshape(2, 12288)
    kv_rows = kv_rows.transpose(1, 0, 2).reshape(2, 2048)

    mixed = attend_rows(q_rows, kv_rows, k_pool, v_pool, page_table, lengths)

    chunks = mixed.reshape(2, 8, 1536).transpose(1, 0, 2)
    send = jnp.broadcast_to(chunks[:, None], (8, 16, 2, 1536)).reshape(128, 2, 1536)
    mine = a2a(send, G + ("zq", "yh")).reshape(256, 1536)
    theirs = lax.ppermute(mine, "c", OTHER)
    out = spread(place, mine, theirs, (o_own, *o_near))
    back = a2a(out.reshape(16, 96, 128), G + ("zp",)).reshape(8, 2, 96, 128)
    return (collect(place, back).T, kv_rows)


def solution(mesh):
    parts = Mesh(mesh.devices.reshape(2, 4, 4, 2, 4, 2), G + T)
    in_specs = (
        P(G, T),
        P(G, T),
        P(G, T),
        P(G, T),
        P(G + T, None, None),
        P(G + T, None, None),
        P(G + T, None),
        P(G + T),
    )
    out_specs = (P(G, T), P(G + T, None))
    return jax.shard_map(
        per_device, mesh=parts, in_specs=in_specs, out_specs=out_specs, check_vma=False
    )
```

time: 331 us -> 202 us (0.61)
  waiting for transfers between devices: 224 us -> 40.8 us
  starting transfers between devices: 19.7 us -> 75.7 us
  between operations: 13.9 us -> 0.94 us
  Pallas kernels: 0 us -> 11.8 us
  matrix products: 13.4 us -> 2.85 us
  blocking collectives: 41.8 us -> 50.5 us
  local copies, waits for them, and re-layouts: 12.9 us -> 17.6 us
  other arithmetic: 4.89 us -> 1.12 us
    all_gather x4 -> x0, waiting for transfers between devices: 207 us -> none  [the longest x1 88 us: per_device(): lax.all_gather(by_columns, 'tp', axis=1, tiled=True)]
    ppermute x0 -> x10, waiting for transfers between devices: none -> 40.6 us  [the longest x1 29.3 us: per_device(): near = lax.ppermute(own, 'zp', OTHER)]
    ppermute x0 -> x10, starting transfers between devices: none -> 34 us  [the longest x4 13.8 us: per_device(): lax.ppermute(part, G + ('zq', 'zp', 'c'), [((g * 8 + z) * 2 + c, (z * 8 +...]
    all_to_all x1 -> x2, blocking collectives: 16.9 us -> 50.5 us  [a2a(): return lax.all_to_all(a, axes, split_axis=0, concat_axis=0, tiled=True)]
    all_gather x1 -> x0, blocking collectives: 24.9 us -> none  [per_device(): lax.all_gather(kv_weight, 'group', axis=0, tiled=True)]
    all_to_all x2 -> x3, starting transfers between devices: 19.5 us -> 41.7 us  [a2a(): return lax.all_to_all(a, axes, split_axis=0, concat_axis=0, tiled=True)]
    all_to_all x2 -> x3, waiting for transfers between devices: 14.6 us -> 0.22 us  [a2a(): return lax.all_to_all(a, axes, split_axis=0, concat_axis=0, tiled=True)]
    pallas_call x0 -> x9, Pallas kernels: none -> 11.8 us  [the longest x1 2.63 us: project(): pl.pallas_call(project_kernel, grid=(2,), in_specs=[pl.BlockSpec((2, 4, 6...]
  transfers between devices with their start and end apart: 6 -> 13, of which waited for: 6 -> 7; matrix products, arithmetic and copies ran while one was open for 8% -> 6% of each run, Pallas kernels for 0% -> 2%
where the time goes in v1:
time: 202 us; the launch traced here: 201 us
  starting transfers between devices  75.7 us (37%)
  blocking collectives  50.5 us (25%)
  waiting for transfers between devices  40.8 us (20%)
  local copies, waits for them, and re-layouts  17.6 us (9%)
  Pallas kernels  11.8 us (6%)
  matrix products  2.85 us (1%)
    all_to_all x2, blocking collectives, a2a(): return lax.all_to_all(a, axes, split_axis=0, concat_axis=0, tiled=True)  50.5 us
    all_to_all x3, starting transfers between devices, a2a(): return lax.all_to_all(a, axes, split_axis=0, concat_axis=0, tiled=True)  41.7 us
    ppermute x1, waiting for transfers between devices, per_device(): near = lax.ppermute(own, 'zp', OTHER)  29.3 us
    ppermute x4, starting transfers between devices, per_device(): lax.ppermute(part, G + ('zq', 'zp', 'c'), [((g * 8 + z) * 2 + c, (z * 8 +...  13.8 us
    unnamed x21, local copies, waits for them, and re-layouts  8.79 us
    ppermute x1, starting transfers between devices, per_device(): theirs = lax.ppermute(mine, 'c', OTHER)  7.11 us
    ppermute x2, starting transfers between devices, per_device(): lax.ppermute(half, 'zp', OTHER)  5.27 us
    ppermute x2, waiting for transfers between devices, per_device(): lax.ppermute(half, 'zp', OTHER)  4.52 us
  transfers between devices with their start and end apart: 13, of which 7 were waited for; matrix products, arithmetic and copies ran while one was open for 6% of the time, Pallas kernels for 2%

profile of v1, /device:TPU:1, one launch (start us, length us, event | category | flops | bytes accessed | tf_op | source)
XLA Modules:
  0.0 201.4 jit_solution(702754254864683735)
XLA Ops:
  3.1 8.8 %collective-permute-start.1 = (bf16[32,192]{1,0:T(8,128)(2,1)S(1)}, bf16[32,192]{1,0:T(8,128)(2,1)S(1)}, u32[]{:S(2)}, u32[]{:S(2)}) collective-permute-start(bf16[32,192]{1,0:T(8,128)(2,1)S(1)} %get-tuple-element.9), channel_id=1, source_target_pairs={{0,1},{1,0},{8,65},{9,64},{16,129},{17,128},{24,193},{25,192},{32,... | collective-permute-start | bytes 36872 | tf_op jit(solution)/shard_map/ppermute | solution.py:292
  11.9 2.4 %collective-permute-start.2 = (bf16[32,192]{1,0:T(8,128)(2,1)S(1)}, bf16[32,192]{1,0:T(8,128)(2,1)S(1)}, u32[]{:S(2)}, u32[]{:S(2)}) collective-permute-start(bf16[32,192]{1,0:T(8,128)(2,1)S(1)} %get-tuple-element.10), channel_id=1, source_target_pairs={{0,8},{1,9},{8,72},{9,73},{16,136},{17,137},{24,200},{25,201},{32,... | collective-permute-start | bytes 36872 | tf_op jit(solution)/shard_map/ppermute | solution.py:292
  14.3 1.9 collective-permute-start.3
  16.4 3.0 %collective-permute-done.3.both = bf16[32,192]{1,0:T(8,128)(2,1)S(1)} collective-permute-done((bf16[32,192]{1,0:T(8,128)(2,1)S(1)}, bf16[32,192]{1,0:T(8,128)(2,1)S(1)}, u32[]{:S(2)}, u32[]{:S(2)}) %collective-permute-start.3) | collective-permute-done | bytes 12320 | tf_op jit(solution)/shard_map/ppermute | solution.py:292
  20.9 24.0 %all-to-all-start = ((bf16[16,64,384]{2,1,0:T(8,128)(2,1)}), bf16[16,64,384]{2,1,0:T(8,128)(2,1)S(1)}, u32[]{:S(2)}, u32[]{:S(2)}) async-start(bf16[16,64,384]{2,1,0:T(8,128)(2,1)} %shard_map.96), calls=%async_computation | async-start | bytes 1572864 | tf_op jit(solution)/shard_map/all_to_all | solution.py:51
  45.0 2.4 %collective-permute-start.4 = (bf16[224,1536]{1,0:T(8,128)(2,1)S(1)}, bf16[224,1536]{1,0:T(8,128)(2,1)S(1)}, u32[]{:S(2)}, u32[]{:S(2)}) collective-permute-start(bf16[224,1536]{1,0:T(8,128)(2,1)S(1)} %shard_map.97.own), channel_id=1, source_target_pairs={{0,8},{8,0},{1,9},{9,1},{2,10},{10,2},{3,11},{11,3},{4,12},{12,4},... | collective-permute-start | bytes 2064392 | tf_op jit(solution)/shard_map/ppermute | solution.py:306
  47.4 3.1 %collective-permute-start.5 = (bf16[224,1536]{1,0:T(8,128)(2,1)S(1)}, bf16[224,1536]{1,0:T(8,128)(2,1)S(1)}, u32[]{:S(2)}, u32[]{:S(2)}) collective-permute-start(bf16[224,1536]{1,0:T(8,128)(2,1)S(1)} %shard_map.97.own), channel_id=1, source_target_pairs={{0,1},{1,0},{2,3},{3,2},{4,5},{5,4},{6,7},{7,6},{8,9},{9,8},{10,11... | collective-permute-start | bytes 2064392 | tf_op jit(solution)/shard_map/ppermute | solution.py:307
  50.6 29.3 %collective-permute-done.4.near = bf16[224,1536]{1,0:T(8,128)(2,1)S(1)} collective-permute-done((bf16[224,1536]{1,0:T(8,128)(2,1)S(1)}, bf16[224,1536]{1,0:T(8,128)(2,1)S(1)}, u32[]{:S(2)}, u32[]{:S(2)}) %collective-permute-start.4) | collective-permute-done | bytes 688160 | tf_op jit(solution)/shard_map/ppermute | solution.py:306
  79.9 2.4 %collective-permute-start.6 = (bf16[224,1536]{1,0:T(8,128)(2,1)S(1)}, bf16[224,1536]{1,0:T(8,128)(2,1)S(1)}, u32[]{:S(2)}, u32[]{:S(2)}) collective-permute-start(bf16[224,1536]{1,0:T(8,128)(2,1)S(1)} %collective-permute-done.4.near), channel_id=1, source_target_pairs={{0,1},{1,0},{2,3},{3,2},{4,5},{5,4},{6,7},{7,6},{8,9},{9,8},{10,11... | collective-permute-start | bytes 2064392 | tf_op jit(solution)/shard_map/ppermute | solution.py:307
  84.0 2.3 %shard_map.98.weight = bf16[896,1536]{1,0:T(8,128)(2,1)} custom-call(s32[3]{0:T(128)S(1)} %pad_add_fusion.place, bf16[224,1536]{1,0:T(8,128)(2,1)S(1)} %shard_map.97.own, bf16[224,1536]{1,0:T(8,128)(2,1)S(1)} %collective-permute-done.4.near, bf16[224,1536]{1,0:T(8,128)(2,1)S(1)} %collective-permute-done.5.own_other, ...), custom_call_target="tpu_custom_call" | custom-call | tf_op jit(solution)/shard_map/pallas_call | solution.py:139
  88.1 2.6 %shard_map.99 = bf16[256,1024]{1,0:T(8,128)(2,1)} custom-call(bf16[4,4,64,384]{3,2,1,0:T(8,128)(2,1)S(1)} %bitcast.37, bf16[896,1536]{1,0:T(8,128)(2,1)S(1)} %copy-done.1), custom_call_target="tpu_custom_call" | custom-call | flops 704643072 | bytes 4194304 | tf_op jit(solution)/shard_map/pallas_call | solution.py:165
  90.7 4.6 %all-to-all-start.1 = ((bf16[8,32,1024]{2,1,0:T(8,128)(2,1)}), bf16[8,32,1024]{2,1,0:T(8,128)(2,1)S(1)}, u32[]{:S(2)}, u32[]{:S(2)}) async-start(bf16[8,32,1024]{2,1,0:T(8,128)(2,1)} %bitcast.50), calls=%async_computation.1 | async-start | bytes 1048576 | tf_op jit(solution)/shard_map/all_to_all | solution.py:51
  96.1 3.1 %collective-permute-start.7 = (bf16[96,1536]{1,0:T(8,128)(2,1)}, bf16[96,1536]{1,0:T(8,128)(2,1)S(1)}, u32[]{:S(2)}, u32[]{:S(2)}) collective-permute-start(bf16[96,1536]{1,0:T(8,128)(2,1)} %get-tuple-element.15), channel_id=1, source_target_pairs={{0,8},{8,0},{1,9},{9,1},{2,10},{10,2},{3,11},{11,3},{4,12},{12,4},... | collective-permute-start | bytes 884744 | tf_op jit(solution)/shard_map/ppermute | solution.py:311
  99.2 2.2 %collective-permute-start.8 = (bf16[96,1536]{1,0:T(8,128)(2,1)}, bf16[96,1536]{1,0:T(8,128)(2,1)S(1)}, u32[]{:S(2)}, u32[]{:S(2)}) collective-permute-start(bf16[96,1536]{1,0:T(8,128)(2,1)} %get-tuple-element.14), channel_id=1, source_target_pairs={{0,8},{8,0},{1,9},{9,1},{2,10},{10,2},{3,11},{11,3},{4,12},{12,4},... | collective-permute-start | bytes 884744 | tf_op jit(solution)/shard_map/ppermute | solution.py:311
  101.6 4.5 %collective-permute-done.7.near_a = bf16[96,1536]{1,0:T(8,128)(2,1)S(1)} collective-permute-done((bf16[96,1536]{1,0:T(8,128)(2,1)}, bf16[96,1536]{1,0:T(8,128)(2,1)S(1)}, u32[]{:S(2)}, u32[]{:S(2)}) %collective-permute-start.7) | collective-permute-done | bytes 294944 | tf_op jit(solution)/shard_map/ppermute | solution.py:311
  107.0 13.1 %all-to-all-start.2 = ((bf16[16,2,896]{2,1,0:T(2,128)(2,1)}), bf16[16,2,896]{2,1,0:T(2,128)(2,1)S(1)}, u32[]{:S(2)}, u32[]{:S(2)}) async-start(bf16[16,2,896]{2,1,0:T(2,128)(2,1)} %shard_map.100), calls=%async_computation.2 | async-start | bytes 114688 | tf_op jit(solution)/shard_map/all_to_all | solution.py:51
  122.0 3.0 %copy.21 = bf16[96,8,8,128]{3,2,1,0:T(8,128)(2,1)} copy(bf16[96,8,8,128]{3,1,2,0:T(8,128)(2,1)} %bitcast.48) | data formatting | bytes 3145728
  125.0 3.3 %gather_fusion.1 = bf16[24,32,1024]{2,1,0:T(8,128)(2,1)} fusion(bf16[24,32,1024]{2,1,0:T(8,128)(2,1)} %param.13, s32[1024]{0:T(1024)S(1)} %pad_clamp_fusion), kind=kCustom, calls=%fused_computation.1 | custom fusion | bytes 3145824 | tf_op jit(solution)/shard_map/gather | solution.py:26
  128.3 3.0 %copy.22 = bf16[96,8,8,128]{3,2,1,0:T(8,128)(2,1)} copy(bf16[96,8,8,128]{3,1,2,0:T(8,128)(2,1)} %bitcast.47) | data formatting | bytes 3145728
  133.1 2.2 %fusion.25 = (f32[2,8,12]{2,1,0:T(8,128)S(1)}, f32[2,8,12,384]{3,2,1,0:T(8,128)S(1)}) fusion(bf16[2,384,8,128]{3,2,1,0:T(8,128)(2,1)} %bitcast.46, bf16[2,8,12,128]{3,1,2,0:T(8,128)(2,1)S(1)} %bitcast.53, pred[2,384]{1,0:T(4,128)(4,1)S(1)} %iota_compare_fusion), kind=kOutput, calls=%fused_computation.31 | convolution fusion | flops 19095360 | bytes 1918464 | tf_op jit(solution)/shard_map/rgph,rcgh->rgpc/dot_general | solution.py:29
  136.6 36.9 %all_to_all.25 = bf16[128,2,1536]{2,1,0:T(2,128)(2,1)} all-to-all(bf16[128,2,1536]{2,1,0:T(2,128)(2,1)S(1)} %bitcast.49), channel_id=1, replica_groups=mesh['yl'=2,'x'=4,'zq'=4,'zp'=2,'yh'=4,'c'=2] {'yl','x','zq','yh'}, dimensions={0} | all-to-all | bytes 1572864 | tf_op jit(solution)/shard_map/all_to_all | solution.py:51
  173.5 2.3 %reshape.72.mine = bf16[256,1536]{1,0:T(8,128)(2,1)S(1)} reshape(bf16[128,2,1536]{2,1,0:T(2,128)(2,1)} %all_to_all.25) | data formatting | bytes 1572864 | tf_op jit(solution)/shard_map/reshape | solution.py:323
  175.8 7.1 %collective-permute-start.9 = (bf16[256,1536]{1,0:T(8,128)(2,1)S(1)}, bf16[256,1536]{1,0:T(8,128)(2,1)S(1)}, u32[]{:S(2)}, u32[]{:S(2)}) collective-permute-start(bf16[256,1536]{1,0:T(8,128)(2,1)S(1)} %reshape.72.mine), channel_id=1, source_target_pairs={{0,1},{1,0},{2,3},{3,2},{4,5},{5,4},{6,7},{7,6},{8,9},{9,8},{10,11... | collective-permute-start | bytes 2359304 | tf_op jit(solution)/shard_map/ppermute | solution.py:324
  186.4 13.6 %all_to_all.26 = bf16[16,96,128]{2,1,0:T(8,128)(2,1)S(1)} all-to-all(bf16[16,96,128]{2,1,0:T(8,128)(2,1)S(1)} %bitcast.41), channel_id=1, replica_groups=mesh['yl'=2,'x'=4,'zq'=4,'zp'=2,'yh'=4,'c'=2] {'yl','x','zp'}, dimensions={0} | all-to-all | bytes 786432 | tf_op jit(solution)/shard_map/all_to_all | solution.py:51
  (57 shorter events, 19.3 us)
Async XLA Ops:
  0.6 119.5 %copy-start = (bf16[24,32,1024]{2,1,0:T(8,128)(2,1)S(1)}, bf16[24,32,1024]{2,1,0:T(8,128)(2,1)}, u32[]{:S(2)}) copy-start(bf16[24,32,1024]{2,1,0:T(8,128)(2,1)} %param.12) | copy-start | bytes 4718596
  0.6 44.3 %copy-start.3 = (bf16[1536,192]{0,1:T(8,128)(2,1)S(1)}, bf16[1536,192]{0,1:T(8,128)(2,1)}, u32[]{:S(2)}) copy-start(bf16[1536,192]{0,1:T(8,128)(2,1)} %param.9) | copy-start | bytes 1769476
  0.7 44.3 %copy-start.4 = (bf16[1536,32]{0,1:T(8,128)(2,1)S(1)}, bf16[1536,32]{0,1:T(8,128)(2,1)}, u32[]{:S(2)}) copy-start(bf16[1536,32]{0,1:T(8,128)(2,1)} %param.10) | copy-start | bytes 294916
  0.8 0.9 copy-start.5
  2.4 13.8 %collective-permute-start = (bf16[32,192]{1,0:T(8,128)(2,1)S(1)}, bf16[32,192]{1,0:T(8,128)(2,1)S(1)}, u32[]{:S(2)}, u32[]{:S(2)}) collective-permute-start(bf16[32,192]{1,0:T(8,128)(2,1)S(1)} %get-tuple-element.8), channel_id=1, source_target_pairs={{0,0},{1,1},{8,64},{9,65},{16,128},{17,129},{24,192},{25,193},{32,... | collective-permute-start | bytes 36872 | tf_op jit(solution)/shard_map/ppermute | solution.py:292
  3.1 13.1 %collective-permute-start.1 = (bf16[32,192]{1,0:T(8,128)(2,1)S(1)}, bf16[32,192]{1,0:T(8,128)(2,1)S(1)}, u32[]{:S(2)}, u32[]{:S(2)}) collective-permute-start(bf16[32,192]{1,0:T(8,128)(2,1)S(1)} %get-tuple-element.9), channel_id=1, source_target_pairs={{0,1},{1,0},{8,65},{9,64},{16,129},{17,128},{24,193},{25,192},{32,... | collective-permute-start | bytes 36872 | tf_op jit(solution)/shard_map/ppermute | solution.py:292
  11.9 4.5 %collective-permute-start.2 = (bf16[32,192]{1,0:T(8,128)(2,1)S(1)}, bf16[32,192]{1,0:T(8,128)(2,1)S(1)}, u32[]{:S(2)}, u32[]{:S(2)}) collective-permute-start(bf16[32,192]{1,0:T(8,128)(2,1)S(1)} %get-tuple-element.10), channel_id=1, source_target_pairs={{0,8},{1,9},{8,72},{9,73},{16,136},{17,137},{24,200},{25,201},{32,... | collective-permute-start | bytes 36872 | tf_op jit(solution)/shard_map/ppermute | solution.py:292
  14.3 5.1 %collective-permute-start.3 = (bf16[32,192]{1,0:T(8,128)(2,1)S(1)}, bf16[32,192]{1,0:T(8,128)(2,1)S(1)}, u32[]{:S(2)}, u32[]{:S(2)}) collective-permute-start(bf16[32,192]{1,0:T(8,128)(2,1)S(1)} %get-tuple-element.11), channel_id=1, source_target_pairs={{0,9},{1,8},{8,73},{9,72},{16,137},{17,136},{24,201},{25,200},{32,... | collective-permute-start | bytes 36872 | tf_op jit(solution)/shard_map/ppermute | solution.py:292
  20.9 65.4 %all-to-all-start = ((bf16[16,64,384]{2,1,0:T(8,128)(2,1)}), bf16[16,64,384]{2,1,0:T(8,128)(2,1)S(1)}, u32[]{:S(2)}, u32[]{:S(2)}) async-start(bf16[16,64,384]{2,1,0:T(8,128)(2,1)} %shard_map.96), calls=%async_computation | async-start | bytes 1572864 | tf_op jit(solution)/shard_map/all_to_all | solution.py:51
  45.0 34.8 %collective-permute-start.4 = (bf16[224,1536]{1,0:T(8,128)(2,1)S(1)}, bf16[224,1536]{1,0:T(8,128)(2,1)S(1)}, u32[]{:S(2)}, u32[]{:S(2)}) collective-permute-start(bf16[224,1536]{1,0:T(8,128)(2,1)S(1)} %shard_map.97.own), channel_id=1, source_target_pairs={{0,8},{8,0},{1,9},{9,1},{2,10},{10,2},{3,11},{11,3},{4,12},{12,4},... | collective-permute-start | bytes 2064392 | tf_op jit(solution)/shard_map/ppermute | solution.py:306
  47.4 34.9 %collective-permute-start.5 = (bf16[224,1536]{1,0:T(8,128)(2,1)S(1)}, bf16[224,1536]{1,0:T(8,128)(2,1)S(1)}, u32[]{:S(2)}, u32[]{:S(2)}) collective-permute-start(bf16[224,1536]{1,0:T(8,128)(2,1)S(1)} %shard_map.97.own), channel_id=1, source_target_pairs={{0,1},{1,0},{2,3},{3,2},{4,5},{5,4},{6,7},{7,6},{8,9},{9,8},{10,11... | collective-permute-start | bytes 2064392 | tf_op jit(solution)/shard_map/ppermute | solution.py:307
  79.9 4.2 %collective-permute-start.6 = (bf16[224,1536]{1,0:T(8,128)(2,1)S(1)}, bf16[224,1536]{1,0:T(8,128)(2,1)S(1)}, u32[]{:S(2)}, u32[]{:S(2)}) collective-permute-start(bf16[224,1536]{1,0:T(8,128)(2,1)S(1)} %collective-permute-done.4.near), channel_id=1, source_target_pairs={{0,1},{1,0},{2,3},{3,2},{4,5},{5,4},{6,7},{7,6},{8,9},{9,8},{10,11... | collective-permute-start | bytes 2064392 | tf_op jit(solution)/shard_map/ppermute | solution.py:307
  86.3 1.8 copy-start.1
  88.1 7.2 %copy-start.2 = (bf16[1536,192]{0,1:T(8,128)(2,1)S(1)}, bf16[1536,192]{0,1:T(8,128)(2,1)}, u32[]{:S(2)}) copy-start(bf16[1536,192]{0,1:T(8,128)(2,1)} %param.11) | copy-start | bytes 1769476
  90.7 10.7 %copy-start.7 = (s32[2,12]{1,0:T(2,128)S(1)}, s32[2,12]{1,0:T(2,128)}, u32[]{:S(2)}) copy-start(s32[2,12]{1,0:T(2,128)} %param.14) | copy-start | bytes 292
  90.7 10.8 %copy-start.8 = (s32[2]{0:T(128)S(1)}, s32[2]{0:T(128)}, u32[]{:S(2)}) copy-start(s32[2]{0:T(128)} %param.15) | copy-start | bytes 28
  90.7 15.4 %all-to-all-start.1 = ((bf16[8,32,1024]{2,1,0:T(8,128)(2,1)}), bf16[8,32,1024]{2,1,0:T(8,128)(2,1)S(1)}, u32[]{:S(2)}, u32[]{:S(2)}) async-start(bf16[8,32,1024]{2,1,0:T(8,128)(2,1)} %bitcast.50), calls=%async_computation.1 | async-start | bytes 1048576 | tf_op jit(solution)/shard_map/all_to_all | solution.py:51
  96.1 10.0 %collective-permute-start.7 = (bf16[96,1536]{1,0:T(8,128)(2,1)}, bf16[96,1536]{1,0:T(8,128)(2,1)S(1)}, u32[]{:S(2)}, u32[]{:S(2)}) collective-permute-start(bf16[96,1536]{1,0:T(8,128)(2,1)} %get-tuple-element.15), channel_id=1, source_target_pairs={{0,8},{8,0},{1,9},{9,1},{2,10},{10,2},{3,11},{11,3},{4,12},{12,4},... | collective-permute-start | bytes 884744 | tf_op jit(solution)/shard_map/ppermute | solution.py:311
  99.2 32.1 %collective-permute-start.8 = (bf16[96,1536]{1,0:T(8,128)(2,1)}, bf16[96,1536]{1,0:T(8,128)(2,1)S(1)}, u32[]{:S(2)}, u32[]{:S(2)}) collective-permute-start(bf16[96,1536]{1,0:T(8,128)(2,1)} %get-tuple-element.14), channel_id=1, source_target_pairs={{0,8},{8,0},{1,9},{9,1},{2,10},{10,2},{3,11},{11,3},{4,12},{12,4},... | collective-permute-start | bytes 884744 | tf_op jit(solution)/shard_map/ppermute | solution.py:311
  107.0 24.5 %all-to-all-start.2 = ((bf16[16,2,896]{2,1,0:T(2,128)(2,1)}), bf16[16,2,896]{2,1,0:T(2,128)(2,1)S(1)}, u32[]{:S(2)}, u32[]{:S(2)}) async-start(bf16[16,2,896]{2,1,0:T(2,128)(2,1)} %shard_map.100), calls=%async_computation.2 | async-start | bytes 114688 | tf_op jit(solution)/shard_map/all_to_all | solution.py:51
  132.9 2.7 %copy-start.6 = (bf16[96,8,8,128]{3,2,1,0:T(8,128)(2,1)S(1)}, bf16[96,8,8,128]{3,2,1,0:T(8,128)(2,1)}, u32[]{:S(2)}) copy-start(bf16[96,8,8,128]{3,2,1,0:T(8,128)(2,1)} %copy.22) | copy-start | bytes 4718596
  175.8 9.0 %collective-permute-start.9 = (bf16[256,1536]{1,0:T(8,128)(2,1)S(1)}, bf16[256,1536]{1,0:T(8,128)(2,1)S(1)}, u32[]{:S(2)}, u32[]{:S(2)}) collective-permute-start(bf16[256,1536]{1,0:T(8,128)(2,1)S(1)} %reshape.72.mine), channel_id=1, source_target_pairs={{0,1},{1,0},{2,3},{3,2},{4,5},{5,4},{6,7},{7,6},{8,9},{9,8},{10,11... | collective-permute-start | bytes 2359304 | tf_op jit(solution)/shard_map/ppermute | solution.py:324

commit v2 on v1

--- a/solution.py
+++ b/solution.py
@@ -14,39 +14,6 @@
 T = ("zq", "zp", "yh", "c")
 
 
-def attend_rows(q_rows, kv_rows, k_pool, v_pool, page_table, lengths):
-    nrows = q_rows.shape[0]
-    kv_width = k_pool.shape[2]
-    kv_heads = kv_width // HD
-    per_group = q_rows.shape[1] // HD // kv_heads
-    query = q_rows.reshape(nrows, kv_heads, per_group, HD)
-    own_keys = kv_rows[:, :kv_width].reshape(nrows, kv_heads, HD)
-    own_values = kv_rows[:, kv_width:].reshape(nrows, kv_heads, HD)
-    paged_keys = k_pool[page_table].reshape(nrows, -1, kv_heads, HD)
-    paged_values = v_pool[page_table].reshape(nrows, -1, kv_heads, HD)
-    scale = 1.0 / jnp.sqrt(jnp.float32(HD))
-    cached = (
-        jnp.einsum("rgph,rcgh->rgpc", query, paged_keys, preferred_element_type=jnp.float32) * scale
-    )
-    own = jnp.einsum("rgph,rgh->rgp", query, own_keys, preferred_element_type=jnp.float32) * scale
-    context = paged_keys.shape[1]
-    valid = jnp.arange(context, dtype=jnp.int32)[None, :] < lengths[:, None]
-    cached = jnp.where(valid[:, None, None, :], cached, jnp.float32(-1e30))
-    top = jnp.maximum(jnp.max(cached, axis=-1), own)
-    exp_cached = jnp.exp(cached - top[..., None])
-    exp_own = jnp.exp(own - top)
-    total = jnp.sum(exp_cached, axis=-1) + exp_own
-    weight_cached = (exp_cached / total[..., None]).astype(jnp.bfloat16)
-    weight_own = (exp_own / total).astype(jnp.bfloat16)
-    mixed = jnp.einsum(
-        "rgpc,rcgh->rgph", weight_cached, paged_values, preferred_element_type=jnp.float32
-    )
-    mixed = mixed + weight_own[..., None].astype(jnp.float32) * own_values[:, :, None, :].astype(
-        jnp.float32
-    )
-    return mixed.astype(jnp.bfloat16).reshape(nrows, -1)
-
-
 def a2a(a, axes):
     return lax.all_to_all(a, axes, split_axis=0, concat_axis=0, tiled=True)
 
@@ -60,51 +27,47 @@
     return pltpu.CompilerParams(vmem_limit_bytes=mib * 2**20)
 
 
-def split_kernel(place, hidden, *out):
-    row = lax.broadcasted_iota(jnp.int32, (128, 128), 0)
-    col = lax.broadcasted_iota(jnp.int32, (128, 128), 1)
-    zp = (place[2] + row // 64) % 2
-    core = (place[1] + row // 32) % 2
-    goes = ((row // 8) % 4) * 32 + zp * 16 + ((row // 2) % 4) * 4 + core * 2 + row % 2
-    pick = jnp.where(goes == col, 1.0, 0.0).astype(jnp.bfloat16)
-    rows = lax.dot_general(pick, hidden[...], NT, preferred_element_type=jnp.float32)
-    rows = rows.astype(jnp.bfloat16)
-    for k in range(4):
-        out[k][...] = rows[k * 32 : k * 32 + 32]
+def split_kernel(place, hidden, own, other):
+    row = lax.broadcasted_iota(jnp.int32, (64, 128), 0)
+    col = lax.broadcasted_iota(jnp.int32, (64, 128), 1)
+    for out, core in ((own, place[1]), (other, 1 - place[1])):
+        goes = ((row // 8) % 4) * 32 + (row // 32) * 16 + ((row // 2) % 4) * 4 + core * 2 + row % 2
+        pick = jnp.where(goes == col, 1.0, 0.0).astype(jnp.bfloat16)
+        out[...] = lax.dot_general(
+            pick, hidden[...], NT, preferred_element_type=jnp.float32
+        ).astype(jnp.bfloat16)
 
 
 def split(place, hidden):
     return pl.pallas_call(
         split_kernel,
         in_specs=[SMEM, VMEM],
-        out_specs=[VMEM] * 4,
-        compiler_params=limit(4),
-        out_shape=[jax.ShapeDtypeStruct((32, 192), jnp.bfloat16)] * 4,
+        out_specs=[VMEM, VMEM],
+        compiler_params=limit(4),
+        out_shape=[jax.ShapeDtypeStruct((64, 192), jnp.bfloat16)] * 2,
     )(place, hidden)
 
 
-def copies_kernel(place, same, core, zp, both, out):
-    flip_core, flip_zp = place[1] == 1, place[0] == 1
-    blocks = []
-    for straight, crossed in ((same, core), (zp, both)):
-        first = jnp.where(flip_core, crossed[...], straight[...])
-        second = jnp.where(flip_core, straight[...], crossed[...])
-        blocks.append(jnp.concatenate([first, second], axis=1))
-    first = jnp.where(flip_zp, blocks[1], blocks[0])
-    second = jnp.where(flip_zp, blocks[0], blocks[1])
-    for to in range(16):
-        out[to, :32] = first
-        out[to, 32:] = second
-
-
-def copies(place, parts):
+def copies_kernel(place, own, other, touch, out):
+    del touch
+    flip = place[1] == 1
+    first = jnp.where(flip, other[...], own[...])
+    second = jnp.where(flip, own[...], other[...])
+    both = jnp.concatenate([first, second], axis=1)
+    for zq in range(4):
+        for zp in range(2):
+            for y in range(4):
+                out[zq * 8 + zp * 4 + y] = both[zp * 32 : zp * 32 + 32]
+
+
+def copies(place, own, other, touch):
     return pl.pallas_call(
         copies_kernel,
-        in_specs=[SMEM] + [VMEM] * 4,
-        out_specs=VMEM,
-        compiler_params=limit(4),
-        out_shape=pltpu.HBM((16, 64, 384), jnp.bfloat16),
-    )(place, *parts)
+        in_specs=[SMEM] + [VMEM] * 3,
+        out_specs=VMEM,
+        compiler_params=limit(4),
+        out_shape=pltpu.HBM((32, 32, 384), jnp.bfloat16),
+    )(place, own, other, touch)
 
 
 def join_kernel(q, kv, out):
@@ -166,7 +129,7 @@
         project_kernel,
         grid=(2,),
         in_specs=[
-            pl.BlockSpec((2, 4, 64, 384), lambda i: (i, 0, 0, 0)),
+            pl.BlockSpec((4, 4, 32, 384), lambda i: (i, 0, 0, 0)),
             pl.BlockSpec((896, 1536), lambda i: (0, 0)),
         ],
         out_specs=pl.BlockSpec((128, 1024), lambda i: (i, 0)),
@@ -201,29 +164,88 @@
     )(parts, touch)
 
 
-def order_kernel(parts, touch, q, kv):
+def attend_kernel(table, lengths, parts, k_pool, v_pool, touch, new_kv, send, query, mixed, sem):
     del touch
+    row = lax.broadcasted_iota(jnp.int32, (24, 768), 0) % 2
+    lane = lax.broadcasted_iota(jnp.int32, (1, 768), 1)
+    masks = []
+    for r in range(2):
+        mask = jnp.zeros((1, 768), jnp.int32)
+        for page in range(12):
+            start = table[r, page] * 32
+            end = start + jnp.clip(lengths[r] - page * 32, 0, 32)
+            mask = jnp.where((lane >= start) & (lane < end), 1, mask)
+        masks.append(mask)
+    valid = jnp.where(row == 0, masks[0], masks[1]) == 1
+
     for z in range(8):
         zq, zp = z // 2, z % 2
         for y in range(4):
-            q[z, :, y * 384 : y * 384 + 384] = parts[zq * 4 + y, :, zp * 384 : zp * 384 + 384]
-        at = 768 + zp * 64
+            for k in range(3):
+                at, h = zp * 384 + k * 128, y * 3 + k
+                query[z, 2 * h : 2 * h + 2, :] = parts[zq * 4 + y, :, at : at + 128].astype(
+                    jnp.float32
+                )
+    fresh = []
+    for z in range(8):
+        at = 768 + (z % 2) * 64
         for y in range(0, 4, 2):
-            pair = [parts[zq * 4 + y + k, :, at : at + 64].astype(jnp.float32) for k in range(2)]
-            kv[z, :, y * 64 : y * 64 + 128] = jnp.concatenate(pair, axis=1).astype(jnp.bfloat16)
-
-
-def order(parts, touch):
-    return pl.pallas_call(
-        order_kernel,
-        in_specs=[VMEM] * 2,
-        out_specs=[VMEM] * 2,
-        compiler_params=limit(4),
+            pair = [
+                parts[(z // 2) * 4 + y + k, :, at : at + 64].astype(jnp.float32) for k in range(2)
+            ]
+            fresh.append(jnp.concatenate(pair, axis=1))
+            to = z * 256 + y * 64
+            new_kv[:, to : to + 128] = fresh[-1].astype(jnp.bfloat16)
+
+    scale = 1.0 / jnp.sqrt(jnp.float32(HD))
+    odd = lax.broadcasted_iota(jnp.int32, (24, 128), 0) % 2 == 1
+    for g in range(8):
+        heads = slice(g * 128, g * 128 + 128)
+        keys = k_pool[:, :, heads].reshape(768, 128)
+        values = v_pool[:, :, heads].reshape(768, 128)
+        own_key = jnp.where(odd, fresh[g][1:2], fresh[g][0:1])
+        own_value = jnp.where(odd, fresh[8 + g][1:2], fresh[8 + g][0:1])
+        q = query[g]
+        scores = lax.dot_general(
+            q.astype(jnp.bfloat16), keys, NT, preferred_element_type=jnp.float32
+        )
+        scores = jnp.where(valid, scores * scale, jnp.float32(-1e30))
+        own = jnp.sum(q * own_key, axis=1, keepdims=True) * scale
+        top = jnp.maximum(jnp.max(scores, axis=1, keepdims=True), own)
+        scores = jnp.exp(scores - top)
+        own = jnp.exp(own - top)
+        total = jnp.sum(scores, axis=1, keepdims=True) + own
+        weights = (scores / total).astype(jnp.bfloat16)
+        own = (own / total).astype(jnp.bfloat16).astype(jnp.float32)
+        out = lax.dot_general(
+            weights, values, (((1,), (0,)), ((), ())), preferred_element_type=jnp.float32
+        )
+        out = out + own * own_value
+        for h in range(12):
+            mixed[g, :, h * 128 : h * 128 + 128] = out[2 * h : 2 * h + 2].astype(jnp.bfloat16)
+    copies = [pltpu.make_async_copy(mixed, send.at[:, k], sem.at[k]) for k in range(16)]
+    for copy in copies:
+        copy.start()
+    for copy in copies:
+        copy.wait()
+
+
+def attend(table, lengths, parts, k_pool, v_pool, touch):
+    return pl.pallas_call(
+        attend_kernel,
+        in_specs=[SMEM] * 2 + [VMEM] * 4,
+        out_specs=[VMEM, pl.BlockSpec(memory_space=pl.ANY)],
         out_shape=[
-            jax.ShapeDtypeStruct((8, 2, 1536), jnp.bfloat16),
-            jax.ShapeDtypeStruct((8, 2, 256), jnp.bfloat16),
+            jax.ShapeDtypeStruct((2, 2048), jnp.bfloat16),
+            pltpu.HBM((8, 16, 2, 1536), jnp.bfloat16),
         ],
-    )(parts, touch)
+        scratch_shapes=[
+            pltpu.VMEM((8, 24, 128), jnp.float32),
+            pltpu.VMEM((8, 2, 1536), jnp.bfloat16),
+            pltpu.SemaphoreType.DMA((16,)),
+        ],
+        compiler_params=limit(16),
+    )(table, lengths, parts, k_pool, v_pool, touch)
 
 
 def spread_kernel(place, mine, theirs, own, near_a, near_b, out):
@@ -284,43 +306,35 @@
 
 
 def per_device(hidden, q_weight, kv_weight, o_weight, k_pool, v_pool, page_table, lengths):
-    place = jnp.stack([lax.axis_index("zp"), lax.axis_index("c"), lax.axis_index("x") % 2])
+    place = jnp.stack([lax.axis_index("zp"), lax.axis_index("c")])
     place = place.astype(jnp.int32)
 
-    parts = split(place, hidden.T)
-    parts = [
+    own = join(q_weight.T, kv_weight.T)
+    near = lax.ppermute(own, "zp", OTHER)
+    pieces = (own, near, lax.ppermute(own, "c", OTHER), lax.ppermute(near, "c", OTHER))
+
+    rows = [
         lax.ppermute(
             part,
             G + ("zq", "zp", "c"),
             [
-                ((g * 8 + z) * 2 + c, (z * 8 + (g ^ (k // 2))) * 2 + (c ^ (k % 2)))
+                ((g * 8 + z) * 2 + c, (z * 8 + g) * 2 + (c ^ flip))
                 for g in range(8)
                 for z in range(8)
                 for c in range(2)
             ],
         )
-        for k, part in enumerate(parts)
+        for flip, part in enumerate(split(place, hidden.T))
     ]
-
-    own = join(q_weight.T, kv_weight.T)
-    near = lax.ppermute(own, "zp", OTHER)
-    pieces = (own, near, lax.ppermute(own, "c", OTHER), lax.ppermute(near, "c", OTHER))
-
-    rows = a2a(copies(place, parts), ("zq", "yh")).reshape(4, 4, 64, 384)
+    rows = a2a(copies(place, *rows, near[:16, :128]), ("zq", "zp", "yh")).reshape(8, 4, 32, 384)
     o_own = o_weight.T
     o_near = [lax.ppermute(half, "zp", OTHER) for half in (o_own[:96], o_own[96:])]
 
     parts = a2a(project(rows, gather(place, pieces)).reshape(8, 32, 1024), G)
     parts = a2a(add(parts, o_near[0][:16, :128]), ("zq", "yh"))
-    q_rows, kv_rows = order(parts, o_near[1][:16, :128])
-    q_rows = q_rows.transpose(1, 0, 2).reshape(2, 12288)
-    kv_rows = kv_rows.transpose(1, 0, 2).reshape(2, 2048)
-
-    mixed = attend_rows(q_rows, kv_rows, k_pool, v_pool, page_table, lengths)
-
-    chunks = mixed.reshape(2, 8, 1536).transpose(1, 0, 2)
-    send = jnp.broadcast_to(chunks[:, None], (8, 16, 2, 1536)).reshape(128, 2, 1536)
-    mine = a2a(send, G + ("zq", "yh")).reshape(256, 1536)
+    kv_rows, send = attend(page_table, lengths, parts, k_pool, v_pool, o_near[1][:16, :128])
+
+    mine = a2a(send.reshape(128, 2, 1536), G + ("zq", "yh")).reshape(256, 1536)
     theirs = lax.ppermute(mine, "c", OTHER)
     out = spread(place, mine, theirs, (o_own, *o_near))
     back = a2a(out.reshape(16, 96, 128), G + ("zp",)).reshape(8, 2, 96, 128)

time: 202 us -> 169 us (0.84)
  local copies, waits for them, and re-layouts: 17.6 us -> 6.99 us
  blocking collectives: 50.5 us -> 40.1 us
  waiting for transfers between devices: 40.8 us -> 31.5 us
  Pallas kernels: 11.8 us -> 16.6 us
  starting transfers between devices: 75.7 us -> 71.7 us
  matrix products: 2.85 us -> 0 us
    ppermute x1, waiting for transfers between devices: 29.3 us -> 2.86 us  [per_device(): near = lax.ppermute(own, 'zp', OTHER)]
    all_to_all x3, waiting for transfers between devices: 0.22 us -> 18.5 us  [a2a(): return lax.all_to_all(a, axes, split_axis=0, concat_axis=0, tiled=True)]
    all_to_all x2, blocking collectives: 50.5 us -> 40.1 us  [a2a(): return lax.all_to_all(a, axes, split_axis=0, concat_axis=0, tiled=True)]
    ppermute x4 -> x2, starting transfers between devices: 13.8 us -> 6.54 us  [per_device(): lax.ppermute(part, G + ('zq', 'zp', 'c'), [((g * 8 + z) * 2 + c, (z * 8 +...]
    gather x2 -> x0, local copies, waits for them, and re-layouts: 5.11 us -> none  [the longest x1 3.27 us: attend_rows(): paged_values = v_pool[page_table].reshape(nrows, -1, kv_heads, HD)]
    pallas_call x4, Pallas kernels: 5.62 us -> 10.4 us  [the longest x1 5.5 us: attend(): pl.pallas_call(attend_kernel, in_specs=[SMEM] * 2 + [VMEM] * 4, out_specs...]
    ppermute x4 -> x2, waiting for transfers between devices: 3.11 us -> 0.01 us  [per_device(): lax.ppermute(part, G + ('zq', 'zp', 'c'), [((g * 8 + z) * 2 + c, (z * 8 +...]
    unnamed x21 -> x18, local copies, waits for them, and re-layouts: 8.79 us -> 5.94 us
  transfers between devices with their start and end apart: 13 -> 11, of which waited for: 7 -> 7; matrix products, arithmetic and copies ran while one was open for 6% -> 0% of each run, Pallas kernels for 2% -> 2%
where the time goes in v2:
time: 169 us; the launch traced here: 168 us
  starting transfers between devices  71.7 us (42%)
  blocking collectives  40.1 us (24%)
  waiting for transfers between devices  31.5 us (19%)
  Pallas kernels  16.6 us (10%)
  local copies, waits for them, and re-layouts  6.99 us (4%)
    all_to_all x3, starting transfers between devices, a2a(): return lax.all_to_all(a, axes, split_axis=0, concat_axis=0, tiled=True)  40.7 us
    all_to_all x2, blocking collectives, a2a(): return lax.all_to_all(a, axes, split_axis=0, concat_axis=0, tiled=True)  40.1 us
    all_to_all x3, waiting for transfers between devices, a2a(): return lax.all_to_all(a, axes, split_axis=0, concat_axis=0, tiled=True)  18.5 us
    ppermute x1, starting transfers between devices, per_device(): theirs = lax.ppermute(mine, 'c', OTHER)  8.66 us
    ppermute x2, starting transfers between devices, per_device(): lax.ppermute(part, G + ('zq', 'zp', 'c'), [((g * 8 + z) * 2 + c, (z * 8 +...  6.54 us
    ppermute x2, waiting for transfers between devices, per_device(): lax.ppermute(half, 'zp', OTHER)  6.17 us
    unnamed x18, local copies, waits for them, and re-layouts  5.94 us
    pallas_call x1, Pallas kernels, attend(): pl.pallas_call(attend_kernel, in_specs=[SMEM] * 2 + [VMEM] * 4, out_specs...  5.5 us
  transfers between devices with their start and end apart: 11, of which 7 were waited for; matrix products, arithmetic and copies ran while one was open for 0% of the time, Pallas kernels for 2%

profile of v2, /device:TPU:1, one launch (start us, length us, event | category | flops | bytes accessed | tf_op | source)
XLA Modules:
  0.0 167.8 jit_solution(932417319828867240)
XLA Ops:
  2.6 4.8 %collective-permute-start.2 = (bf16[224,1536]{1,0:T(8,128)(2,1)S(1)}, bf16[224,1536]{1,0:T(8,128)(2,1)S(1)}, u32[]{:S(2)}, u32[]{:S(2)}) collective-permute-start(bf16[224,1536]{1,0:T(8,128)(2,1)S(1)} %shard_map.96.own), channel_id=1, source_target_pairs={{0,8},{8,0},{1,9},{9,1},{2,10},{10,2},{3,11},{11,3},{4,12},{12,4},... | collective-permute-start | bytes 2064392 | tf_op jit(solution)/shard_map/ppermute | solution.py:313
  9.7 5.9 %collective-permute-start.1 = (bf16[64,192]{1,0:T(8,128)(2,1)S(1)}, bf16[64,192]{1,0:T(8,128)(2,1)S(1)}, u32[]{:S(2)}, u32[]{:S(2)}) collective-permute-start(bf16[64,192]{1,0:T(8,128)(2,1)S(1)} %get-tuple-element.7), channel_id=1, source_target_pairs={{0,1},{1,0},{8,65},{9,64},{16,129},{17,128},{24,193},{25,192},{32,... | collective-permute-start | bytes 73736 | tf_op jit(solution)/shard_map/ppermute | solution.py:317
  15.6 2.9 %collective-permute-done.2.near = bf16[224,1536]{1,0:T(8,128)(2,1)S(1)} collective-permute-done((bf16[224,1536]{1,0:T(8,128)(2,1)S(1)}, bf16[224,1536]{1,0:T(8,128)(2,1)S(1)}, u32[]{:S(2)}, u32[]{:S(2)}) %collective-permute-start.2) | collective-permute-done | bytes 688160 | tf_op jit(solution)/shard_map/ppermute | solution.py:313
  20.1 20.0 %all-to-all-start = ((bf16[32,32,384]{2,1,0:T(8,128)(2,1)}), bf16[32,32,384]{2,1,0:T(8,128)(2,1)S(1)}, u32[]{:S(2)}, u32[]{:S(2)}) async-start(bf16[32,32,384]{2,1,0:T(8,128)(2,1)} %shard_map.97), calls=%async_computation | async-start | bytes 1572864 | tf_op jit(solution)/shard_map/all_to_all | solution.py:18
  40.1 3.7 %collective-permute-start.3 = (bf16[224,1536]{1,0:T(8,128)(2,1)S(1)}, bf16[224,1536]{1,0:T(8,128)(2,1)S(1)}, u32[]{:S(2)}, u32[]{:S(2)}) collective-permute-start(bf16[224,1536]{1,0:T(8,128)(2,1)S(1)} %shard_map.96.own), channel_id=1, source_target_pairs={{0,1},{1,0},{2,3},{3,2},{4,5},{5,4},{6,7},{7,6},{8,9},{9,8},{10,11... | collective-permute-start | bytes 2064392 | tf_op jit(solution)/shard_map/ppermute | solution.py:314
  43.8 1.9 %collective-permute-start.4 = (bf16[224,1536]{1,0:T(8,128)(2,1)S(1)}, bf16[224,1536]{1,0:T(8,128)(2,1)S(1)}, u32[]{:S(2)}, u32[]{:S(2)}) collective-permute-start(bf16[224,1536]{1,0:T(8,128)(2,1)S(1)} %collective-permute-done.2.near), channel_id=1, source_target_pairs={{0,1},{1,0},{2,3},{3,2},{4,5},{5,4},{6,7},{7,6},{8,9},{9,8},{10,11... | collective-permute-start | bytes 2064392 | tf_op jit(solution)/shard_map/ppermute | solution.py:314
  45.8 2.1 %collective-permute-done.4.near_other = bf16[224,1536]{1,0:T(8,128)(2,1)S(1)} collective-permute-done((bf16[224,1536]{1,0:T(8,128)(2,1)S(1)}, bf16[224,1536]{1,0:T(8,128)(2,1)S(1)}, u32[]{:S(2)}, u32[]{:S(2)}) %collective-permute-start.4) | collective-permute-done | bytes 688160 | tf_op jit(solution)/shard_map/ppermute | solution.py:314
  47.9 2.3 %shard_map.98.weight = bf16[896,1536]{1,0:T(8,128)(2,1)} custom-call(s32[2]{0:T(128)S(1)} %pad_add_fusion.place, bf16[224,1536]{1,0:T(8,128)(2,1)S(1)} %shard_map.96.own, bf16[224,1536]{1,0:T(8,128)(2,1)S(1)} %collective-permute-done.2.near, bf16[224,1536]{1,0:T(8,128)(2,1)S(1)} %collective-permute-done.3.own_other, ...), custom_call_target="tpu_custom_call" | custom-call | tf_op jit(solution)/shard_map/pallas_call | solution.py:102
  50.1 9.1 %all-to-all-done = bf16[32,32,384]{2,1,0:T(8,128)(2,1)S(1)} async-done(((bf16[32,32,384]{2,1,0:T(8,128)(2,1)}), bf16[32,32,384]{2,1,0:T(8,128)(2,1)S(1)}, u32[]{:S(2)}, u32[]{:S(2)}) %all-to-all-start) | async-done | bytes 786464 | tf_op jit(solution)/shard_map/all_to_all | solution.py:18
  59.2 1.8 %copy-done = bf16[896,1536]{1,0:T(8,128)(2,1)S(1)} copy-done((bf16[896,1536]{1,0:T(8,128)(2,1)S(1)}, bf16[896,1536]{1,0:T(8,128)(2,1)}, u32[]{:S(2)}) %copy-start) | copy-done | bytes 2752536
  61.0 2.6 %shard_map.99 = bf16[256,1024]{1,0:T(8,128)(2,1)} custom-call(bf16[8,4,32,384]{3,2,1,0:T(8,128)(2,1)S(1)} %bitcast.12, bf16[896,1536]{1,0:T(8,128)(2,1)S(1)} %copy-done), custom_call_target="tpu_custom_call" | custom-call | flops 704643072 | bytes 4194304 | tf_op jit(solution)/shard_map/pallas_call | solution.py:128
  63.6 17.2 %all-to-all-start.1 = ((bf16[8,32,1024]{2,1,0:T(8,128)(2,1)}), bf16[8,32,1024]{2,1,0:T(8,128)(2,1)S(1)}, u32[]{:S(2)}, u32[]{:S(2)}) async-start(bf16[8,32,1024]{2,1,0:T(8,128)(2,1)} %bitcast.20), calls=%async_computation.1 | async-start | bytes 1048576 | tf_op jit(solution)/shard_map/all_to_all | solution.py:18
  81.6 1.9 %collective-permute-start.5 = (bf16[96,1536]{1,0:T(8,128)(2,1)S(1)}, bf16[96,1536]{1,0:T(8,128)(2,1)S(1)}, u32[]{:S(2)}, u32[]{:S(2)}) collective-permute-start(bf16[96,1536]{1,0:T(8,128)(2,1)S(1)} %get-tuple-element.11), channel_id=1, source_target_pairs={{0,8},{8,0},{1,9},{9,1},{2,10},{10,2},{3,11},{11,3},{4,12},{12,4},... | collective-permute-start | bytes 884744 | tf_op jit(solution)/shard_map/ppermute | solution.py:331
  83.5 3.4 %collective-permute-start.6 = (bf16[96,1536]{1,0:T(8,128)(2,1)}, bf16[96,1536]{1,0:T(8,128)(2,1)S(1)}, u32[]{:S(2)}, u32[]{:S(2)}) collective-permute-start(bf16[96,1536]{1,0:T(8,128)(2,1)} %get-tuple-element.10), channel_id=1, source_target_pairs={{0,8},{8,0},{1,9},{9,1},{2,10},{10,2},{3,11},{11,3},{4,12},{12,4},... | collective-permute-start | bytes 884744 | tf_op jit(solution)/shard_map/ppermute | solution.py:331
  86.9 4.2 %collective-permute-done.5.near_a = bf16[96,1536]{1,0:T(8,128)(2,1)S(1)} collective-permute-done((bf16[96,1536]{1,0:T(8,128)(2,1)S(1)}, bf16[96,1536]{1,0:T(8,128)(2,1)S(1)}, u32[]{:S(2)}, u32[]{:S(2)}) %collective-permute-start.5) | collective-permute-done | bytes 294944 | tf_op jit(solution)/shard_map/ppermute | solution.py:331
  92.0 3.5 %all-to-all-start.2 = ((bf16[16,2,896]{2,1,0:T(2,128)(2,1)}), bf16[16,2,896]{2,1,0:T(2,128)(2,1)S(1)}, u32[]{:S(2)}, u32[]{:S(2)}) async-start(bf16[16,2,896]{2,1,0:T(2,128)(2,1)} %shard_map.100), calls=%async_computation.2 | async-start | bytes 114688 | tf_op jit(solution)/shard_map/all_to_all | solution.py:18
  95.5 1.9 %collective-permute-done.6.near_b = bf16[96,1536]{1,0:T(8,128)(2,1)S(1)} collective-permute-done((bf16[96,1536]{1,0:T(8,128)(2,1)}, bf16[96,1536]{1,0:T(8,128)(2,1)S(1)}, u32[]{:S(2)}, u32[]{:S(2)}) %collective-permute-start.6) | collective-permute-done | bytes 294944 | tf_op jit(solution)/shard_map/ppermute | solution.py:331
  97.4 9.4 %all-to-all-done.2.parts = bf16[16,2,896]{2,1,0:T(2,128)(2,1)S(1)} async-done(((bf16[16,2,896]{2,1,0:T(2,128)(2,1)}), bf16[16,2,896]{2,1,0:T(2,128)(2,1)S(1)}, u32[]{:S(2)}, u32[]{:S(2)}) %all-to-all-start.2) | async-done | bytes 57376 | tf_op jit(solution)/shard_map/all_to_all | solution.py:18
  108.3 5.5 %shard_map.101 = (bf16[2,2048]{1,0:T(2,128)(2,1)}, bf16[8,16,2,1536]{3,2,1,0:T(2,128)(2,1)}) custom-call(s32[2,12]{1,0:T(2,128)S(1)} %copy-done.7, s32[2]{0:T(128)S(1)} %copy-done.8, bf16[16,2,896]{2,1,0:T(2,128)(2,1)S(1)} %all-to-all-done.2.parts, bf16[24,32,1024]{2,1,0:T(8,128)(2,1)S(1)} %copy-done.2, bf16[24,32,1024]{2,1,0:T(8,128)(2,1)S(1)} %copy-done.3, ...), custom_call_target="tpu_custom_call" | custom-call | tf_op jit(solution)/shard_map/pallas_call | solution.py:234
  113.8 27.3 %all_to_all.25 = bf16[128,2,1536]{2,1,0:T(2,128)(2,1)S(1)} all-to-all(bf16[128,2,1536]{2,1,0:T(2,128)(2,1)} %bitcast.21), channel_id=1, replica_groups=mesh['yl'=2,'x'=4,'zq'=4,'zp'=2,'yh'=4,'c'=2] {'yl','x','zq','yh'}, dimensions={0} | all-to-all | bytes 1572864 | tf_op jit(solution)/shard_map/all_to_all | solution.py:18
  141.4 8.7 %collective-permute-start.7 = (bf16[256,1536]{1,0:T(8,128)(2,1)S(1)}, bf16[256,1536]{1,0:T(8,128)(2,1)S(1)}, u32[]{:S(2)}, u32[]{:S(2)}) collective-permute-start(bf16[256,1536]{1,0:T(8,128)(2,1)S(1)} %reshape.25.mine), channel_id=1, source_target_pairs={{0,1},{1,0},{2,3},{3,2},{4,5},{5,4},{6,7},{7,6},{8,9},{9,8},{10,11... | collective-permute-start | bytes 2359304 | tf_op jit(solution)/shard_map/ppermute | solution.py:338
  150.1 1.9 %collective-permute-done.7.theirs = bf16[256,1536]{1,0:T(8,128)(2,1)S(1)} collective-permute-done((bf16[256,1536]{1,0:T(8,128)(2,1)S(1)}, bf16[256,1536]{1,0:T(8,128)(2,1)S(1)}, u32[]{:S(2)}, u32[]{:S(2)}) %collective-permute-start.7) | collective-permute-done | bytes 786464 | tf_op jit(solution)/shard_map/ppermute | solution.py:338
  152.0 1.6 shard_map.102
  153.6 12.8 %all_to_all.26 = bf16[16,96,128]{2,1,0:T(8,128)(2,1)S(1)} all-to-all(bf16[16,96,128]{2,1,0:T(8,128)(2,1)S(1)} %bitcast.16), channel_id=1, replica_groups=mesh['yl'=2,'x'=4,'zq'=4,'zp'=2,'yh'=4,'c'=2] {'yl','x','zp'}, dimensions={0} | all-to-all | bytes 786432 | tf_op jit(solution)/shard_map/all_to_all | solution.py:18
  (33 shorter events, 10.6 us)
Async XLA Ops:
  0.6 1.1 copy-start.4
  1.7 0.9 copy-start.5
  2.6 15.9 %collective-permute-start.2 = (bf16[224,1536]{1,0:T(8,128)(2,1)S(1)}, bf16[224,1536]{1,0:T(8,128)(2,1)S(1)}, u32[]{:S(2)}, u32[]{:S(2)}) collective-permute-start(bf16[224,1536]{1,0:T(8,128)(2,1)S(1)} %shard_map.96.own), channel_id=1, source_target_pairs={{0,8},{8,0},{1,9},{9,1},{2,10},{10,2},{3,11},{11,3},{4,12},{12,4},... | collective-permute-start | bytes 2064392 | tf_op jit(solution)/shard_map/ppermute | solution.py:313
  7.6 0.8 copy-start.6
  9.1 9.4 %collective-permute-start = (bf16[64,192]{1,0:T(8,128)(2,1)S(1)}, bf16[64,192]{1,0:T(8,128)(2,1)S(1)}, u32[]{:S(2)}, u32[]{:S(2)}) collective-permute-start(bf16[64,192]{1,0:T(8,128)(2,1)S(1)} %get-tuple-element.6), channel_id=1, source_target_pairs={{0,0},{1,1},{8,64},{9,65},{16,128},{17,129},{24,192},{25,193},{32,... | collective-permute-start | bytes 73736 | tf_op jit(solution)/shard_map/ppermute | solution.py:317
  9.7 8.8 %collective-permute-start.1 = (bf16[64,192]{1,0:T(8,128)(2,1)S(1)}, bf16[64,192]{1,0:T(8,128)(2,1)S(1)}, u32[]{:S(2)}, u32[]{:S(2)}) collective-permute-start(bf16[64,192]{1,0:T(8,128)(2,1)S(1)} %get-tuple-element.7), channel_id=1, source_target_pairs={{0,1},{1,0},{8,65},{9,64},{16,129},{17,128},{24,193},{25,192},{32,... | collective-permute-start | bytes 73736 | tf_op jit(solution)/shard_map/ppermute | solution.py:317
  20.1 39.2 %all-to-all-start = ((bf16[32,32,384]{2,1,0:T(8,128)(2,1)}), bf16[32,32,384]{2,1,0:T(8,128)(2,1)S(1)}, u32[]{:S(2)}, u32[]{:S(2)}) async-start(bf16[32,32,384]{2,1,0:T(8,128)(2,1)} %shard_map.97), calls=%async_computation | async-start | bytes 1572864 | tf_op jit(solution)/shard_map/all_to_all | solution.py:18
  40.1 5.7 %collective-permute-start.3 = (bf16[224,1536]{1,0:T(8,128)(2,1)S(1)}, bf16[224,1536]{1,0:T(8,128)(2,1)S(1)}, u32[]{:S(2)}, u32[]{:S(2)}) collective-permute-start(bf16[224,1536]{1,0:T(8,128)(2,1)S(1)} %shard_map.96.own), channel_id=1, source_target_pairs={{0,1},{1,0},{2,3},{3,2},{4,5},{5,4},{6,7},{7,6},{8,9},{9,8},{10,11... | collective-permute-start | bytes 2064392 | tf_op jit(solution)/shard_map/ppermute | solution.py:314
  43.8 4.0 %collective-permute-start.4 = (bf16[224,1536]{1,0:T(8,128)(2,1)S(1)}, bf16[224,1536]{1,0:T(8,128)(2,1)S(1)}, u32[]{:S(2)}, u32[]{:S(2)}) collective-permute-start(bf16[224,1536]{1,0:T(8,128)(2,1)S(1)} %collective-permute-done.2.near), channel_id=1, source_target_pairs={{0,1},{1,0},{2,3},{3,2},{4,5},{5,4},{6,7},{7,6},{8,9},{9,8},{10,11... | collective-permute-start | bytes 2064392 | tf_op jit(solution)/shard_map/ppermute | solution.py:314
  59.2 1.8 %copy-start = (bf16[896,1536]{1,0:T(8,128)(2,1)S(1)}, bf16[896,1536]{1,0:T(8,128)(2,1)}, u32[]{:S(2)}) copy-start(bf16[896,1536]{1,0:T(8,128)(2,1)} %shard_map.98.weight) | copy-start | bytes 8257540
  61.0 19.8 %copy-start.1 = (bf16[1536,192]{0,1:T(8,128)(2,1)S(1)}, bf16[1536,192]{0,1:T(8,128)(2,1)}, u32[]{:S(2)}) copy-start(bf16[1536,192]{0,1:T(8,128)(2,1)} %param.11) | copy-start | bytes 1769476
  63.6 43.2 %copy-start.2 = (bf16[24,32,1024]{2,1,0:T(8,128)(2,1)S(1)}, bf16[24,32,1024]{2,1,0:T(8,128)(2,1)}, u32[]{:S(2)}) copy-start(bf16[24,32,1024]{2,1,0:T(8,128)(2,1)} %k_pool.1) | copy-start | bytes 4718596
  63.6 43.2 %copy-start.7 = (s32[2,12]{1,0:T(2,128)S(1)}, s32[2,12]{1,0:T(2,128)}, u32[]{:S(2)}) copy-start(s32[2,12]{1,0:T(2,128)} %table.1) | copy-start | bytes 292
  63.6 43.2 %copy-start.8 = (s32[2]{0:T(128)S(1)}, s32[2]{0:T(128)}, u32[]{:S(2)}) copy-start(s32[2]{0:T(128)} %lengths.1) | copy-start | bytes 28
  63.6 27.5 %all-to-all-start.1 = ((bf16[8,32,1024]{2,1,0:T(8,128)(2,1)}), bf16[8,32,1024]{2,1,0:T(8,128)(2,1)S(1)}, u32[]{:S(2)}, u32[]{:S(2)}) async-start(bf16[8,32,1024]{2,1,0:T(8,128)(2,1)} %bitcast.20), calls=%async_computation.1 | async-start | bytes 1048576 | tf_op jit(solution)/shard_map/all_to_all | solution.py:18
  81.6 9.5 %collective-permute-start.5 = (bf16[96,1536]{1,0:T(8,128)(2,1)S(1)}, bf16[96,1536]{1,0:T(8,128)(2,1)S(1)}, u32[]{:S(2)}, u32[]{:S(2)}) collective-permute-start(bf16[96,1536]{1,0:T(8,128)(2,1)S(1)} %get-tuple-element.11), channel_id=1, source_target_pairs={{0,8},{8,0},{1,9},{9,1},{2,10},{10,2},{3,11},{11,3},{4,12},{12,4},... | collective-permute-start | bytes 884744 | tf_op jit(solution)/shard_map/ppermute | solution.py:331
  83.5 13.9 %collective-permute-start.6 = (bf16[96,1536]{1,0:T(8,128)(2,1)}, bf16[96,1536]{1,0:T(8,128)(2,1)S(1)}, u32[]{:S(2)}, u32[]{:S(2)}) collective-permute-start(bf16[96,1536]{1,0:T(8,128)(2,1)} %get-tuple-element.10), channel_id=1, source_target_pairs={{0,8},{8,0},{1,9},{9,1},{2,10},{10,2},{3,11},{11,3},{4,12},{12,4},... | collective-permute-start | bytes 884744 | tf_op jit(solution)/shard_map/ppermute | solution.py:331
  92.0 14.8 %all-to-all-start.2 = ((bf16[16,2,896]{2,1,0:T(2,128)(2,1)}), bf16[16,2,896]{2,1,0:T(2,128)(2,1)S(1)}, u32[]{:S(2)}, u32[]{:S(2)}) async-start(bf16[16,2,896]{2,1,0:T(2,128)(2,1)} %shard_map.100), calls=%async_computation.2 | async-start | bytes 114688 | tf_op jit(solution)/shard_map/all_to_all | solution.py:18
  106.8 1.4 copy-start.3
  141.4 10.6 %collective-permute-start.7 = (bf16[256,1536]{1,0:T(8,128)(2,1)S(1)}, bf16[256,1536]{1,0:T(8,128)(2,1)S(1)}, u32[]{:S(2)}, u32[]{:S(2)}) collective-permute-start(bf16[256,1536]{1,0:T(8,128)(2,1)S(1)} %reshape.25.mine), channel_id=1, source_target_pairs={{0,1},{1,0},{2,3},{3,2},{4,5},{5,4},{6,7},{7,6},{8,9},{9,8},{10,11... | collective-permute-start | bytes 2359304 | tf_op jit(solution)/shard_map/ppermute | solution.py:338

commit v3 on v2

v3 whole, which is shorter than its diff:
```python
import jax
import jax.numpy as jnp
from jax import lax
from jax.experimental import pallas as pl
from jax.experimental.pallas import tpu as pltpu
from jax.sharding import Mesh, PartitionSpec as P

D = 12288
HD = 128

eps = 1e-05

G = ("yl", "x")
T = ("zq", "zp", "yh", "c")


def a2a(a, axes):
    return lax.all_to_all(a, axes, split_axis=0, concat_axis=0, tiled=True)


NT = (((1,), (1,)), ((), ()))
VMEM = pl.BlockSpec(memory_space=pltpu.VMEM)
SMEM = pl.BlockSpec(memory_space=pltpu.SMEM)


def in_hbm(a):
    return pltpu.with_memory_space_constraint(a, pltpu.HBM)


def limit(mib):
    return pltpu.CompilerParams(vmem_limit_bytes=mib * 2**20)


def split_kernel(place, hidden, own, other):
    row = lax.broadcasted_iota(jnp.int32, (64, 128), 0)
    col = lax.broadcasted_iota(jnp.int32, (64, 128), 1)
    for out, core in ((own, place[1]), (other, 1 - place[1])):
        goes = ((row // 8) % 4) * 32 + (row // 32) * 16 + ((row // 2) % 4) * 4 + core * 2 + row % 2
        pick = jnp.where(goes == col, 1.0, 0.0).astype(jnp.bfloat16)
        out[...] = lax.dot_general(
            pick, hidden[...], NT, preferred_element_type=jnp.float32
        ).astype(jnp.bfloat16)


def split(place, hidden):
    return pl.pallas_call(
        split_kernel,
        in_specs=[SMEM, VMEM],
        out_specs=[VMEM, VMEM],
        compiler_params=limit(4),
        out_shape=[jax.ShapeDtypeStruct((64, 192), jnp.bfloat16)] * 2,
    )(place, in_hbm(hidden))


def copies_kernel(place, own, other, touch, out):
    del touch
    flip = place[1] == 1
    first = jnp.where(flip, other[...], own[...])
    second = jnp.where(flip, own[...], other[...])
    both = jnp.concatenate([first, second], axis=1)
    for zq in range(4):
        for zp in range(2):
            for y in range(4):
                out[zq * 8 + zp * 4 + y] = both[zp * 32 : zp * 32 + 32]


def copies(place, own, other, touch):
    return pl.pallas_call(
        copies_kernel,
        in_specs=[SMEM] + [VMEM] * 3,
        out_specs=VMEM,
        compiler_params=limit(4),
        out_shape=pltpu.HBM((32, 32, 384), jnp.bfloat16),
    )(place, own, other, touch)


def join_kernel(q, kv, first, second):
    first[...] = q[:112]
    second[:80] = q[112:]
    second[80:] = kv[...]


def join(q, kv):
    return pl.pallas_call(
        join_kernel,
        in_specs=[VMEM] * 2,
        out_specs=[VMEM] * 2,
        compiler_params=limit(4),
        out_shape=[jax.ShapeDtypeStruct((112, 1536), jnp.bfloat16)] * 2,
    )(in_hbm(q), in_hbm(kv))


def gather_kernel(place, *refs):
    zp, core = place[0], place[1]
    weight = refs[8]
    for k, (z, c) in enumerate(((zp, core), (1 - zp, core), (zp, 1 - core), (1 - zp, 1 - core))):
        first, second = refs[2 * k], refs[2 * k + 1]
        at = pl.multiple_of((z * 2 + c) * 192, 64)
        weight[pl.ds(at, 112), :] = first[...]
        weight[pl.ds(pl.multiple_of(at + 112, 16), 80), :] = second[:80]
        at = 768 + (z * 2 + c) * 32
        weight[pl.ds(pl.multiple_of(at, 32), 32), :] = second[80:]


def gather(place, pieces):
    return pl.pallas_call(
        gather_kernel,
        in_specs=[SMEM] + [VMEM] * 8,
        out_specs=VMEM,
        out_shape=pltpu.HBM((896, 1536), jnp.bfloat16),
        compiler_params=limit(8),
    )(place, *pieces)


def project_kernel(rows, weight, out, total, squares):
    step = pl.program_id(0)

    @pl.when(step == 0)
    def _():
        total[...] = jnp.zeros_like(total)
        squares[...] = jnp.zeros_like(squares)

    a = rows[:, 0].reshape(256, 384)
    total[...] += lax.dot_general(a, weight[...], NT, preferred_element_type=jnp.float32)
    wide = a.astype(jnp.float32)
    wide = wide * wide
    squares[...] += wide[:, :128] + wide[:, 128:256] + wide[:, 256:]

    @pl.when(step == 3)
    def _():
        out[:, :896] = total[...].astype(jnp.bfloat16)
        sums = jnp.sum(squares[...], axis=1, keepdims=True)
        high = sums.astype(jnp.bfloat16).astype(jnp.float32)
        lane = lax.broadcasted_iota(jnp.int32, (256, 128), 1)
        extra = jnp.where(lane == 0, high, jnp.where(lane == 1, sums - high, 0.0))
        out[:, 896:] = extra.astype(jnp.bfloat16)


def project(rows, weight):
    return pl.pallas_call(
        project_kernel,
        grid=(4,),
        in_specs=[
            pl.BlockSpec((8, 1, 32, 384), lambda i: (0, i, 0, 0)),
            pl.BlockSpec((896, 384), lambda i: (0, i)),
        ],
        out_specs=pl.BlockSpec((256, 1024), lambda i: (0, 0)),
        out_shape=pltpu.HBM((256, 1024), jnp.bfloat16),
        scratch_shapes=[pltpu.VMEM((256, 896), jnp.float32), pltpu.VMEM((256, 128), jnp.float32)],
        compiler_params=limit(12),
        cost_estimate=pl.CostEstimate(
            flops=2 * 256 * 1536 * 896, bytes_accessed=4 * 2**20, transcendentals=0
        ),
    )(rows, in_hbm(weight))


def add_kernel(parts, out):
    total = jnp.sum(parts[...].astype(jnp.float32), axis=0)
    squares = jnp.sum(total[:, 896:], axis=1, keepdims=True)
    normed = total[:, :896] * lax.rsqrt(squares / D + eps)
    for r in range(8):
        out[r] = normed[2 * r : 2 * r + 2].astype(jnp.bfloat16)


def add(parts):
    return pl.pallas_call(
        add_kernel,
        grid=(2,),
        in_specs=[
            pl.BlockSpec((8, 16, 1024), lambda i: (0, i, 0)),
        ],
        out_specs=pl.BlockSpec((8, 2, 896), lambda i: (i, 0, 0)),
        compiler_params=limit(4),
        out_shape=pltpu.HBM((16, 2, 896), jnp.bfloat16),
    )(parts)


def attend_kernel(table, lengths, parts, k_pool, v_pool, touch, new_kv, send, query, mixed, v_held, sem, v_sem):
    del touch
    fetch = pltpu.make_async_copy(v_pool, v_held, v_sem)
    fetch.start()
    row = lax.broadcasted_iota(jnp.int32, (24, 768), 0) % 2
    lane = lax.broadcasted_iota(jnp.int32, (1, 768), 1)
    masks = []
    for r in range(2):
        mask = jnp.zeros((1, 768), jnp.int32)
        for page in range(12):
            start = table[r, page] * 32
            end = start + jnp.clip(lengths[r] - page * 32, 0, 32)
            mask = jnp.where((lane >= start) & (lane < end), 1, mask)
        masks.append(mask)
    valid = jnp.where(row == 0, masks[0], masks[1]) == 1

    for z in range(8):
        zq, zp = z // 2, z % 2
        for y in range(4):
            for k in range(3):
                at, h = zp * 384 + k * 128, y * 3 + k
                query[z, 2 * h : 2 * h + 2, :] = parts[zq * 4 + y, :, at : at + 128].astype(
                    jnp.float32
                )
    fresh = []
    for z in range(8):
        at = 768 + (z % 2) * 64
        for y in range(0, 4, 2):
            pair = [
                parts[(z // 2) * 4 + y + k, :, at : at + 64].astype(jnp.float32) for k in range(2)
            ]
            fresh.append(jnp.concatenate(pair, axis=1))
            to = z * 256 + y * 64
            new_kv[:, to : to + 128] = fresh[-1].astype(jnp.bfloat16)

    scale = 1.0 / jnp.sqrt(jnp.float32(HD))
    odd = lax.broadcasted_iota(jnp.int32, (24, 128), 0) % 2 == 1
    found = []
    for g in range(8):
        keys = k_pool[:, :, g * 128 : g * 128 + 128].reshape(768, 128)
        own_key = jnp.where(odd, fresh[g][1:2], fresh[g][0:1])
        q = query[g]
        scores = lax.dot_general(
            q.astype(jnp.bfloat16), keys, NT, preferred_element_type=jnp.float32
        )
        scores = jnp.where(valid, scores * scale, jnp.float32(-1e30))
        own = jnp.sum(q * own_key, axis=1, keepdims=True) * scale
        top = jnp.maximum(jnp.max(scores, axis=1, keepdims=True), own)
        scores = jnp.exp(scores - top)
        own = jnp.exp(own - top)
        total = jnp.sum(scores, axis=1, keepdims=True) + own
        weights = (scores / total).astype(jnp.bfloat16)
        found.append((weights, (own / total).astype(jnp.bfloat16).astype(jnp.float32)))
    fetch.wait()
    for g, (weights, own) in enumerate(found):
        values = v_held[:, :, g * 128 : g * 128 + 128].reshape(768, 128)
        own_value = jnp.where(odd, fresh[8 + g][1:2], fresh[8 + g][0:1])
        out = lax.dot_general(
            weights, values, (((1,), (0,)), ((), ())), preferred_element_type=jnp.float32
        )
        out = out + own * own_value
        for h in range(12):
            mixed[g, :, h * 128 : h * 128 + 128] = out[2 * h : 2 * h + 2].astype(jnp.bfloat16)
    copies = [pltpu.make_async_copy(mixed, send.at[:, k], sem.at[k]) for k in range(16)]
    for copy in copies:
        copy.start()
    for copy in copies:
        copy.wait()


def attend(table, lengths, parts, k_pool, v_pool, touch):
    return pl.pallas_call(
        attend_kernel,
        in_specs=[SMEM] * 2 + [VMEM] * 2 + [pl.BlockSpec(memory_space=pl.ANY), VMEM],
        out_specs=[VMEM, pl.BlockSpec(memory_space=pl.ANY)],
        out_shape=[
            jax.ShapeDtypeStruct((2, 2048), jnp.bfloat16),
            pltpu.HBM((8, 16, 2, 1536), jnp.bfloat16),
        ],
        scratch_shapes=[
            pltpu.VMEM((8, 24, 128), jnp.float32),
            pltpu.VMEM((8, 2, 1536), jnp.bfloat16),
            pltpu.VMEM((24, 32, 1024), jnp.bfloat16),
            pltpu.SemaphoreType.DMA((16,)),
            pltpu.SemaphoreType.DMA,
        ],
        compiler_params=limit(16),
    )(table, lengths, parts, k_pool, in_hbm(v_pool), touch)


def spread_kernel(place, rows, *refs):
    zp, core = place[0], place[1]
    out = refs[6]
    pieces = [refs[0][...], jnp.concatenate([refs[1][...], refs[2][...]], axis=0)]
    pieces += [refs[3][...], jnp.concatenate([refs[4][...], refs[5][...]], axis=0)]
    for k, weight in enumerate(pieces):
        z = zp if k % 2 == 0 else 1 - zp
        c = core if k < 2 else 1 - core
        part = lax.dot_general(rows[...], weight, NT, preferred_element_type=jnp.float32)
        part = part.astype(jnp.bfloat16)
        for g in range(8):
            at = g * 32
            out[g, z * 2 + c, 0:32, :] = part[at : at + 32, :128]
            out[g, z * 2 + c, 32:48, :] = jnp.concatenate(
                [part[at : at + 16, 128:], part[at + 16 : at + 32, 128:]], axis=1
            )


def spread(place, rows, pieces):
    return pl.pallas_call(
        spread_kernel,
        in_specs=[SMEM] + [VMEM] * 7,
        out_specs=VMEM,
        out_shape=jax.ShapeDtypeStruct((8, 4, 48, 128), jnp.bfloat16),
        compiler_params=limit(16),
        cost_estimate=pl.CostEstimate(
            flops=2 * 256 * 1536 * 768, bytes_accessed=4 * 2**20, transcendentals=0
        ),
    )(place, rows, *pieces)


def collect_kernel(parts, out):
    total = jnp.sum(parts[...].astype(jnp.float32), axis=0).astype(jnp.bfloat16)
    rows = []
    for k in range(4):
        last = jnp.concatenate([total[k, 32:48, :64], total[k, 32:48, 64:]], axis=0)
        rows.append(jnp.concatenate([total[k, 0:32], last], axis=1))
    rows = jnp.concatenate(rows, axis=0)
    at = lax.broadcasted_iota(jnp.int32, (128, 128), 0)
    to = lax.broadcasted_iota(jnp.int32, (128, 128), 1)
    goes = ((at // 8) % 4) * 32 + (at // 64) * 16 + ((at // 2) % 4) * 4 + ((at // 32) % 2) * 2 + at % 2
    pick = jnp.where(goes == to, 1.0, 0.0).astype(jnp.bfloat16)
    out[...] = lax.dot_general(
        rows, pick, (((0,), (0,)), ((), ())), preferred_element_type=jnp.float32
    ).astype(jnp.bfloat16)


def collect(parts):
    return pl.pallas_call(
        collect_kernel,
        in_specs=[VMEM],
        out_specs=VMEM,
        compiler_params=limit(4),
        out_shape=jax.ShapeDtypeStruct((192, 128), jnp.bfloat16),
    )(parts)


OTHER = [(0, 1), (1, 0)]


def per_device(hidden, q_weight, kv_weight, o_weight, k_pool, v_pool, page_table, lengths):
    place = jnp.stack([lax.axis_index("zp"), lax.axis_index("c")])
    place = place.astype(jnp.int32)

    own = join(q_weight.T, kv_weight.T)
    near = [lax.ppermute(part, "zp", OTHER) for part in own]
    pieces = (*own, *near, *(lax.ppermute(part, "c", OTHER) for part in (*own, *near)))

    rows = [
        lax.ppermute(
            part,
            G + ("zq", "zp", "c"),
            [
                ((g * 8 + z) * 2 + c, (z * 8 + g) * 2 + (c ^ flip))
                for g in range(8)
                for z in range(8)
                for c in range(2)
            ],
        )
        for flip, part in enumerate(split(place, hidden.T))
    ]
    rows = a2a(copies(place, *rows, near[0][:16, :128]), ("zq", "zp", "yh")).reshape(8, 4, 32, 384)
    o_own = o_weight.T
    o_near = [lax.ppermute(half, "zp", OTHER) for half in (o_own[:96], o_own[96:])]
    o_pieces = (o_own, *o_near)

    parts = a2a(project(rows, gather(place, pieces)).reshape(8, 32, 1024), G)
    parts = a2a(add(parts), ("zq", "yh"))
    kv_rows, send = attend(page_table, lengths, parts, k_pool, v_pool, o_near[0][:16, :128])

    mine = a2a(send.reshape(128, 2, 1536), G + ("zq", "yh")).reshape(256, 1536)
    out = spread(place, mine, (*o_pieces, *(lax.ppermute(part, "c", OTHER) for part in o_pieces)))
    back = a2a(out.reshape(32, 48, 128), G + ("zp", "c")).reshape(8, 4, 48, 128)
    return (collect(back).T, kv_rows)


def solution(mesh):
    parts = Mesh(mesh.devices.reshape(2, 4, 4, 2, 4, 2), G + T)
    in_specs = (
        P(G, T),
        P(G, T),
        P(G, T),
        P(G, T),
        P(G + T, None, None),
        P(G + T, None, None),
        P(G + T, None),
        P(G + T),
    )
    out_specs = (P(G, T), P(G + T, None))
    return jax.shard_map(
        per_device, mesh=parts, in_specs=in_specs, out_specs=out_specs, check_vma=False
    )
```

time: 169 us -> 174 us (1.030)
  blocking collectives: 40.1 us -> 15.1 us
  waiting for transfers between devices: 31.5 us -> 50.6 us
  starting transfers between devices: 71.7 us -> 84.5 us
  local copies, waits for them, and re-layouts: 6.99 us -> 3.06 us
  Pallas kernels: 16.6 us -> 19 us
    all_to_all x2 -> x1, blocking collectives: 40.1 us -> 15.1 us  [a2a(): return lax.all_to_all(a, axes, split_axis=0, concat_axis=0, tiled=True)]
    ppermute x4 -> x9, waiting for transfers between devices: 6.85 us -> 18.1 us  [the longest x2 16.8 us: per_device(): near = [lax.ppermute(part, 'zp', OTHER) for part in own]]
    ppermute x2, waiting for transfers between devices: 6.17 us -> 15.4 us  [per_device(): lax.ppermute(half, 'zp', OTHER)]
    ppermute x4 -> x9, starting transfers between devices: 19.1 us -> 26.6 us  [the longest x7 18.6 us: per_device(): lax.ppermute(part, 'c', OTHER)]
    unnamed x18 -> x8, local copies, waits for them, and re-layouts: 5.94 us -> 0.01 us
    all_to_all x3 -> x4, starting transfers between devices: 40.7 us -> 45.9 us  [a2a(): return lax.all_to_all(a, axes, split_axis=0, concat_axis=0, tiled=True)]
    all_to_all x3 -> x4, waiting for transfers between devices: 18.5 us -> 16.3 us  [a2a(): return lax.all_to_all(a, axes, split_axis=0, concat_axis=0, tiled=True)]
    pallas_call x6, Pallas kernels: 13.4 us -> 15.5 us  [the longest x1 4.95 us: attend(): pl.pallas_call(attend_kernel, in_specs=[SMEM] * 2 + [VMEM] * 2 + [pl.Bloc...]
  transfers between devices with their start and end apart: 11 -> 17, of which waited for: 7 -> 6; matrix products, arithmetic and copies ran while one was open for 0% -> 2% of each run, Pallas kernels for 2% -> 2%
where the time goes in v3:
time: 174 us; the launch traced here: 173 us
  starting transfers between devices  84.5 us (49%)
  waiting for transfers between devices  50.6 us (29%)
  Pallas kernels  19 us (11%)
  blocking collectives  15.1 us (9%)
  local copies, waits for them, and re-layouts  3.06 us (2%)
    all_to_all x4, starting transfers between devices, a2a(): return lax.all_to_all(a, axes, split_axis=0, concat_axis=0, tiled=True)  45.9 us
    ppermute x7, starting transfers between devices, per_device(): lax.ppermute(part, 'c', OTHER)  18.6 us
    ppermute x2, waiting for transfers between devices, per_device(): near = [lax.ppermute(part, 'zp', OTHER) for part in own]  16.8 us
    all_to_all x4, waiting for transfers between devices, a2a(): return lax.all_to_all(a, axes, split_axis=0, concat_axis=0, tiled=True)  16.3 us
    ppermute x2, waiting for transfers between devices, per_device(): lax.ppermute(half, 'zp', OTHER)  15.4 us
    all_to_all x1, blocking collectives, a2a(): return lax.all_to_all(a, axes, split_axis=0, concat_axis=0, tiled=True)  15.1 us
    ppermute x2, starting transfers between devices, per_device(): near = [lax.ppermute(part, 'zp', OTHER) for part in own]  7.97 us
    ppermute x2, starting transfers between devices, per_device(): lax.ppermute(part, G + ('zq', 'zp', 'c'), [((g * 8 + z) * 2 + c, (z * 8 +...  6.54 us
  transfers between devices with their start and end apart: 17, of which 6 were waited for; matrix products, arithmetic and copies ran while one was open for 2% of the time, Pallas kernels for 2%

profile of v3, /device:TPU:1, one launch (start us, length us, event | category | flops | bytes accessed | tf_op | source)
XLA Modules:
  0.0 173.3 jit_solution(6172296548712566073)
XLA Ops:
  1.7 4.8 %collective-permute-start.2 = (bf16[112,1536]{1,0:T(8,128)(2,1)S(1)}, bf16[112,1536]{1,0:T(8,128)(2,1)S(1)}, u32[]{:S(2)}, u32[]{:S(2)}) collective-permute-start(bf16[112,1536]{1,0:T(8,128)(2,1)S(1)} %get-tuple-element.10.refs_0_), channel_id=1, source_target_pairs={{0,8},{8,0},{1,9},{9,1},{2,10},{10,2},{3,11},{11,3},{4,12},{12,4},... | collective-permute-start | bytes 1032200 | tf_op jit(solution)/shard_map/ppermute | solution.py:333
  8.3 5.9 %collective-permute-start.1 = (bf16[64,192]{1,0:T(8,128)(2,1)S(1)}, bf16[64,192]{1,0:T(8,128)(2,1)S(1)}, u32[]{:S(2)}, u32[]{:S(2)}) collective-permute-start(bf16[64,192]{1,0:T(8,128)(2,1)S(1)} %get-tuple-element.9), channel_id=1, source_target_pairs={{0,1},{1,0},{8,65},{9,64},{16,129},{17,128},{24,193},{25,192},{32,... | collective-permute-start | bytes 73736 | tf_op jit(solution)/shard_map/ppermute | solution.py:337
  16.6 21.4 %all-to-all-start = ((bf16[32,32,384]{2,1,0:T(8,128)(2,1)}), bf16[32,32,384]{2,1,0:T(8,128)(2,1)S(1)}, u32[]{:S(2)}, u32[]{:S(2)}) async-start(bf16[32,32,384]{2,1,0:T(8,128)(2,1)} %shard_map.97), calls=%async_computation | async-start | bytes 1572864 | tf_op jit(solution)/shard_map/all_to_all | solution.py:18
  38.0 3.1 %collective-permute-start.3 = (bf16[112,1536]{1,0:T(8,128)(2,1)S(1)}, bf16[112,1536]{1,0:T(8,128)(2,1)S(1)}, u32[]{:S(2)}, u32[]{:S(2)}) collective-permute-start(bf16[112,1536]{1,0:T(8,128)(2,1)S(1)} %get-tuple-element.11.refs_1_), channel_id=1, source_target_pairs={{0,8},{8,0},{1,9},{9,1},{2,10},{10,2},{3,11},{11,3},{4,12},{12,4},... | collective-permute-start | bytes 1032200 | tf_op jit(solution)/shard_map/ppermute | solution.py:333
  41.1 2.4 %collective-permute-start.4 = (bf16[112,1536]{1,0:T(8,128)(2,1)S(1)}, bf16[112,1536]{1,0:T(8,128)(2,1)S(1)}, u32[]{:S(2)}, u32[]{:S(2)}) collective-permute-start(bf16[112,1536]{1,0:T(8,128)(2,1)S(1)} %get-tuple-element.10.refs_0_), channel_id=1, source_target_pairs={{0,1},{1,0},{2,3},{3,2},{4,5},{5,4},{6,7},{7,6},{8,9},{9,8},{10,11... | collective-permute-start | bytes 1032200 | tf_op jit(solution)/shard_map/ppermute | solution.py:334
  43.5 1.9 %collective-permute-start.5 = (bf16[112,1536]{1,0:T(8,128)(2,1)S(1)}, bf16[112,1536]{1,0:T(8,128)(2,1)S(1)}, u32[]{:S(2)}, u32[]{:S(2)}) collective-permute-start(bf16[112,1536]{1,0:T(8,128)(2,1)S(1)} %get-tuple-element.11.refs_1_), channel_id=1, source_target_pairs={{0,1},{1,0},{2,3},{3,2},{4,5},{5,4},{6,7},{7,6},{8,9},{9,8},{10,11... | collective-permute-start | bytes 1032200 | tf_op jit(solution)/shard_map/ppermute | solution.py:334
  45.5 2.4 %collective-permute-start.6 = (bf16[112,1536]{1,0:T(8,128)(2,1)S(1)}, bf16[112,1536]{1,0:T(8,128)(2,1)S(1)}, u32[]{:S(2)}, u32[]{:S(2)}) collective-permute-start(bf16[112,1536]{1,0:T(8,128)(2,1)S(1)} %collective-permute-done.2.refs_2_), channel_id=1, source_target_pairs={{0,1},{1,0},{2,3},{3,2},{4,5},{5,4},{6,7},{7,6},{8,9},{9,8},{10,11... | collective-permute-start | bytes 1032200 | tf_op jit(solution)/shard_map/ppermute | solution.py:334
  47.9 16.8 %collective-permute-done.3.refs_3_ = bf16[112,1536]{1,0:T(8,128)(2,1)S(1)} collective-permute-done((bf16[112,1536]{1,0:T(8,128)(2,1)S(1)}, bf16[112,1536]{1,0:T(8,128)(2,1)S(1)}, u32[]{:S(2)}, u32[]{:S(2)}) %collective-permute-start.3) | collective-permute-done | bytes 344096 | tf_op jit(solution)/shard_map/ppermute | solution.py:333
  64.7 2.6 %collective-permute-start.7 = (bf16[112,1536]{1,0:T(8,128)(2,1)S(1)}, bf16[112,1536]{1,0:T(8,128)(2,1)S(1)}, u32[]{:S(2)}, u32[]{:S(2)}) collective-permute-start(bf16[112,1536]{1,0:T(8,128)(2,1)S(1)} %collective-permute-done.3.refs_3_), channel_id=1, source_target_pairs={{0,1},{1,0},{2,3},{3,2},{4,5},{5,4},{6,7},{7,6},{8,9},{9,8},{10,11... | collective-permute-start | bytes 1032200 | tf_op jit(solution)/shard_map/ppermute | solution.py:334
  68.6 2.2 %shard_map.98.weight = bf16[896,1536]{1,0:T(8,128)(2,1)} custom-call(s32[2]{0:T(128)S(1)} %pad_add_fusion.place, bf16[112,1536]{1,0:T(8,128)(2,1)S(1)} %get-tuple-element.10.refs_0_, bf16[112,1536]{1,0:T(8,128)(2,1)S(1)} %get-tuple-element.11.refs_1_, bf16[112,1536]{1,0:T(8,128)(2,1)S(1)} %collective-permute-done.2.refs_2_, ...), custom_call_target="tpu_custom_call" | custom-call | tf_op jit(solution)/shard_map/pallas_call | solution.py:106
  70.8 4.7 %shard_map.99 = bf16[256,1024]{1,0:T(8,128)(2,1)} custom-call(bf16[8,4,32,384]{3,2,1,0:T(8,128)(2,1)S(1)} %bitcast.12, bf16[896,1536]{1,0:T(8,128)(2,1)} %shard_map.98.weight), custom_call_target="tpu_custom_call" | custom-call | flops 704643072 | bytes 4194304 | tf_op jit(solution)/shard_map/pallas_call | solution.py:140
  75.6 6.3 %all-to-all-start.1 = ((bf16[8,32,1024]{2,1,0:T(8,128)(2,1)}), bf16[8,32,1024]{2,1,0:T(8,128)(2,1)S(1)}, u32[]{:S(2)}, u32[]{:S(2)}) async-start(bf16[8,32,1024]{2,1,0:T(8,128)(2,1)} %bitcast.18), calls=%async_computation.1 | async-start | bytes 1048576 | tf_op jit(solution)/shard_map/all_to_all | solution.py:18
  82.6 2.4 %collective-permute-start.8 = (bf16[96,1536]{1,0:T(8,128)(2,1)}, bf16[96,1536]{1,0:T(8,128)(2,1)S(1)}, u32[]{:S(2)}, u32[]{:S(2)}) collective-permute-start(bf16[96,1536]{1,0:T(8,128)(2,1)} %get-tuple-element.15), channel_id=1, source_target_pairs={{0,8},{8,0},{1,9},{9,1},{2,10},{10,2},{3,11},{11,3},{4,12},{12,4},... | collective-permute-start | bytes 884744 | tf_op jit(solution)/shard_map/ppermute | solution.py:351
  85.1 5.0 %all-to-all-done.1.parts = bf16[8,32,1024]{2,1,0:T(8,128)(2,1)S(1)} async-done(((bf16[8,32,1024]{2,1,0:T(8,128)(2,1)}), bf16[8,32,1024]{2,1,0:T(8,128)(2,1)S(1)}, u32[]{:S(2)}, u32[]{:S(2)}) %all-to-all-start.1) | async-done | bytes 524320 | tf_op jit(solution)/shard_map/all_to_all | solution.py:18
  90.9 10.0 %all-to-all-start.2 = ((bf16[16,2,896]{2,1,0:T(2,128)(2,1)}), bf16[16,2,896]{2,1,0:T(2,128)(2,1)S(1)}, u32[]{:S(2)}, u32[]{:S(2)}) async-start(bf16[16,2,896]{2,1,0:T(2,128)(2,1)} %shard_map.100), calls=%async_computation.2 | async-start | bytes 114688 | tf_op jit(solution)/shard_map/all_to_all | solution.py:18
  100.9 11.3 %all-to-all-done.2.parts = bf16[16,2,896]{2,1,0:T(2,128)(2,1)S(1)} async-done(((bf16[16,2,896]{2,1,0:T(2,128)(2,1)}), bf16[16,2,896]{2,1,0:T(2,128)(2,1)S(1)}, u32[]{:S(2)}, u32[]{:S(2)}) %all-to-all-start.2) | async-done | bytes 57376 | tf_op jit(solution)/shard_map/all_to_all | solution.py:18
  112.3 5.0 %shard_map.101 = (bf16[2,2048]{1,0:T(2,128)(2,1)}, bf16[8,16,2,1536]{3,2,1,0:T(2,128)(2,1)}) custom-call(s32[2,12]{1,0:T(2,128)S(1)} %copy-done.2, s32[2]{0:T(128)S(1)} %copy-done.3, bf16[16,2,896]{2,1,0:T(2,128)(2,1)S(1)} %all-to-all-done.2.parts, bf16[24,32,1024]{2,1,0:T(8,128)(2,1)S(1)} %copy-done.1, bf16[24,32,1024]{2,1,0:T(8,128)(2,1)} %v_pool.1, ...), custom_call_target="tpu_custom_call" | custom-call | tf_op jit(solution)/shard_map/pallas_call | solution.py:249
  117.2 8.3 %all-to-all-start.3 = ((bf16[128,2,1536]{2,1,0:T(2,128)(2,1)}), bf16[128,2,1536]{2,1,0:T(2,128)(2,1)}, u32[]{:S(2)}, u32[]{:S(2)}) async-start(bf16[128,2,1536]{2,1,0:T(2,128)(2,1)} %bitcast.19), calls=%async_computation.3 | async-start | bytes 1572864 | tf_op jit(solution)/shard_map/all_to_all | solution.py:18
  125.5 3.1 %collective-permute-start.9 = (bf16[96,1536]{1,0:T(8,128)(2,1)S(1)}, bf16[96,1536]{1,0:T(8,128)(2,1)S(1)}, u32[]{:S(2)}, u32[]{:S(2)}) collective-permute-start(bf16[96,1536]{1,0:T(8,128)(2,1)S(1)} %get-tuple-element.14), channel_id=1, source_target_pairs={{0,8},{8,0},{1,9},{9,1},{2,10},{10,2},{3,11},{11,3},{4,12},{12,4},... | collective-permute-start | bytes 884744 | tf_op jit(solution)/shard_map/ppermute | solution.py:351
  128.6 4.7 %collective-permute-start.10 = (bf16[192,1536]{1,0:T(8,128)(2,1)S(1)}, bf16[192,1536]{1,0:T(8,128)(2,1)S(1)}, u32[]{:S(2)}, u32[]{:S(2)}) collective-permute-start(bf16[192,1536]{1,0:T(8,128)(2,1)S(1)} %bitcast.14), channel_id=1, source_target_pairs={{0,1},{1,0},{2,3},{3,2},{4,5},{5,4},{6,7},{7,6},{8,9},{9,8},{10,11... | collective-permute-start | bytes 1769480 | tf_op jit(solution)/shard_map/ppermute | solution.py:359
  135.3 15.4 %collective-permute-done.9.refs_2_ = bf16[96,1536]{1,0:T(8,128)(2,1)S(1)} collective-permute-done((bf16[96,1536]{1,0:T(8,128)(2,1)S(1)}, bf16[96,1536]{1,0:T(8,128)(2,1)S(1)}, u32[]{:S(2)}, u32[]{:S(2)}) %collective-permute-start.9) | collective-permute-done | bytes 294944 | tf_op jit(solution)/shard_map/ppermute | solution.py:351
  150.7 2.6 %collective-permute-start.12 = (bf16[96,1536]{1,0:T(8,128)(2,1)S(1)}, bf16[96,1536]{1,0:T(8,128)(2,1)S(1)}, u32[]{:S(2)}, u32[]{:S(2)}) collective-permute-start(bf16[96,1536]{1,0:T(8,128)(2,1)S(1)} %collective-permute-done.9.refs_2_), channel_id=1, source_target_pairs={{0,1},{1,0},{2,3},{3,2},{4,5},{5,4},{6,7},{7,6},{8,9},{9,8},{10,11... | collective-permute-start | bytes 884744 | tf_op jit(solution)/shard_map/ppermute | solution.py:359
  153.4 2.3 %reshape.25.rows = bf16[256,1536]{1,0:T(8,128)(2,1)S(1)} reshape(bf16[128,2,1536]{2,1,0:T(2,128)(2,1)} %all-to-all-done.3) | data formatting | bytes 1572864 | tf_op jit(solution)/shard_map/reshape | solution.py:358
  157.3 15.1 %all_to_all.25 = bf16[32,48,128]{2,1,0:T(8,128)(2,1)S(1)} all-to-all(bf16[32,48,128]{2,1,0:T(8,128)(2,1)S(1)} %bitcast.17), channel_id=1, replica_groups=mesh['yl'=2,'x'=4,'zq'=4,'zp'=2,'yh'=4,'c'=2] {'yl','x','zp','c'}, dimensions={0} | all-to-all | bytes 786432 | tf_op jit(solution)/shard_map/all_to_all | solution.py:18
  (33 shorter events, 12.5 us)
Async XLA Ops:
  1.7 12.5 %collective-permute-start.2 = (bf16[112,1536]{1,0:T(8,128)(2,1)S(1)}, bf16[112,1536]{1,0:T(8,128)(2,1)S(1)}, u32[]{:S(2)}, u32[]{:S(2)}) collective-permute-start(bf16[112,1536]{1,0:T(8,128)(2,1)S(1)} %get-tuple-element.10.refs_0_), channel_id=1, source_target_pairs={{0,8},{8,0},{1,9},{9,1},{2,10},{10,2},{3,11},{11,3},{4,12},{12,4},... | collective-permute-start | bytes 1032200 | tf_op jit(solution)/shard_map/ppermute | solution.py:333
  7.7 6.6 %collective-permute-start = (bf16[64,192]{1,0:T(8,128)(2,1)S(1)}, bf16[64,192]{1,0:T(8,128)(2,1)S(1)}, u32[]{:S(2)}, u32[]{:S(2)}) collective-permute-start(bf16[64,192]{1,0:T(8,128)(2,1)S(1)} %get-tuple-element.8), channel_id=1, source_target_pairs={{0,0},{1,1},{8,64},{9,65},{16,128},{17,129},{24,192},{25,193},{32,... | collective-permute-start | bytes 73736 | tf_op jit(solution)/shard_map/ppermute | solution.py:337
  8.3 6.7 %collective-permute-start.1 = (bf16[64,192]{1,0:T(8,128)(2,1)S(1)}, bf16[64,192]{1,0:T(8,128)(2,1)S(1)}, u32[]{:S(2)}, u32[]{:S(2)}) collective-permute-start(bf16[64,192]{1,0:T(8,128)(2,1)S(1)} %get-tuple-element.9), channel_id=1, source_target_pairs={{0,1},{1,0},{8,65},{9,64},{16,129},{17,128},{24,193},{25,192},{32,... | collective-permute-start | bytes 73736 | tf_op jit(solution)/shard_map/ppermute | solution.py:337
  16.6 54.2 %all-to-all-start = ((bf16[32,32,384]{2,1,0:T(8,128)(2,1)}), bf16[32,32,384]{2,1,0:T(8,128)(2,1)S(1)}, u32[]{:S(2)}, u32[]{:S(2)}) async-start(bf16[32,32,384]{2,1,0:T(8,128)(2,1)} %shard_map.97), calls=%async_computation | async-start | bytes 1572864 | tf_op jit(solution)/shard_map/all_to_all | solution.py:18
  38.0 26.7 %collective-permute-start.3 = (bf16[112,1536]{1,0:T(8,128)(2,1)S(1)}, bf16[112,1536]{1,0:T(8,128)(2,1)S(1)}, u32[]{:S(2)}, u32[]{:S(2)}) collective-permute-start(bf16[112,1536]{1,0:T(8,128)(2,1)S(1)} %get-tuple-element.11.refs_1_), channel_id=1, source_target_pairs={{0,8},{8,0},{1,9},{9,1},{2,10},{10,2},{3,11},{11,3},{4,12},{12,4},... | collective-permute-start | bytes 1032200 | tf_op jit(solution)/shard_map/ppermute | solution.py:333
  41.1 26.2 %collective-permute-start.4 = (bf16[112,1536]{1,0:T(8,128)(2,1)S(1)}, bf16[112,1536]{1,0:T(8,128)(2,1)S(1)}, u32[]{:S(2)}, u32[]{:S(2)}) collective-permute-start(bf16[112,1536]{1,0:T(8,128)(2,1)S(1)} %get-tuple-element.10.refs_0_), channel_id=1, source_target_pairs={{0,1},{1,0},{2,3},{3,2},{4,5},{5,4},{6,7},{7,6},{8,9},{9,8},{10,11... | collective-permute-start | bytes 1032200 | tf_op jit(solution)/shard_map/ppermute | solution.py:334
  43.5 23.8 %collective-permute-start.5 = (bf16[112,1536]{1,0:T(8,128)(2,1)S(1)}, bf16[112,1536]{1,0:T(8,128)(2,1)S(1)}, u32[]{:S(2)}, u32[]{:S(2)}) collective-permute-start(bf16[112,1536]{1,0:T(8,128)(2,1)S(1)} %get-tuple-element.11.refs_1_), channel_id=1, source_target_pairs={{0,1},{1,0},{2,3},{3,2},{4,5},{5,4},{6,7},{7,6},{8,9},{9,8},{10,11... | collective-permute-start | bytes 1032200 | tf_op jit(solution)/shard_map/ppermute | solution.py:334
  45.5 21.9 %collective-permute-start.6 = (bf16[112,1536]{1,0:T(8,128)(2,1)S(1)}, bf16[112,1536]{1,0:T(8,128)(2,1)S(1)}, u32[]{:S(2)}, u32[]{:S(2)}) collective-permute-start(bf16[112,1536]{1,0:T(8,128)(2,1)S(1)} %collective-permute-done.2.refs_2_), channel_id=1, source_target_pairs={{0,1},{1,0},{2,3},{3,2},{4,5},{5,4},{6,7},{7,6},{8,9},{9,8},{10,11... | collective-permute-start | bytes 1032200 | tf_op jit(solution)/shard_map/ppermute | solution.py:334
  64.7 3.9 %collective-permute-start.7 = (bf16[112,1536]{1,0:T(8,128)(2,1)S(1)}, bf16[112,1536]{1,0:T(8,128)(2,1)S(1)}, u32[]{:S(2)}, u32[]{:S(2)}) collective-permute-start(bf16[112,1536]{1,0:T(8,128)(2,1)S(1)} %collective-permute-done.3.refs_3_), channel_id=1, source_target_pairs={{0,1},{1,0},{2,3},{3,2},{4,5},{5,4},{6,7},{7,6},{8,9},{9,8},{10,11... | collective-permute-start | bytes 1032200 | tf_op jit(solution)/shard_map/ppermute | solution.py:334
  70.8 11.1 %copy-start = (bf16[1536,192]{0,1:T(8,128)(2,1)S(1)}, bf16[1536,192]{0,1:T(8,128)(2,1)}, u32[]{:S(2)}) copy-start(bf16[1536,192]{0,1:T(8,128)(2,1)} %param.11) | copy-start | bytes 1769476
  75.6 36.7 %copy-start.1 = (bf16[24,32,1024]{2,1,0:T(8,128)(2,1)S(1)}, bf16[24,32,1024]{2,1,0:T(8,128)(2,1)}, u32[]{:S(2)}) copy-start(bf16[24,32,1024]{2,1,0:T(8,128)(2,1)} %k_pool.1) | copy-start | bytes 4718596
  75.6 36.7 %copy-start.2 = (s32[2,12]{1,0:T(2,128)S(1)}, s32[2,12]{1,0:T(2,128)}, u32[]{:S(2)}) copy-start(s32[2,12]{1,0:T(2,128)} %table.1) | copy-start | bytes 292
  75.6 36.7 %copy-start.3 = (s32[2]{0:T(128)S(1)}, s32[2]{0:T(128)}, u32[]{:S(2)}) copy-start(s32[2]{0:T(128)} %lengths.1) | copy-start | bytes 28
  75.6 14.5 %all-to-all-start.1 = ((bf16[8,32,1024]{2,1,0:T(8,128)(2,1)}), bf16[8,32,1024]{2,1,0:T(8,128)(2,1)S(1)}, u32[]{:S(2)}, u32[]{:S(2)}) async-start(bf16[8,32,1024]{2,1,0:T(8,128)(2,1)} %bitcast.18), calls=%async_computation.1 | async-start | bytes 1048576 | tf_op jit(solution)/shard_map/all_to_all | solution.py:18
  82.6 18.3 %collective-permute-start.8 = (bf16[96,1536]{1,0:T(8,128)(2,1)}, bf16[96,1536]{1,0:T(8,128)(2,1)S(1)}, u32[]{:S(2)}, u32[]{:S(2)}) collective-permute-start(bf16[96,1536]{1,0:T(8,128)(2,1)} %get-tuple-element.15), channel_id=1, source_target_pairs={{0,8},{8,0},{1,9},{9,1},{2,10},{10,2},{3,11},{11,3},{4,12},{12,4},... | collective-permute-start | bytes 884744 | tf_op jit(solution)/shard_map/ppermute | solution.py:351
  90.9 21.3 %all-to-all-start.2 = ((bf16[16,2,896]{2,1,0:T(2,128)(2,1)}), bf16[16,2,896]{2,1,0:T(2,128)(2,1)S(1)}, u32[]{:S(2)}, u32[]{:S(2)}) async-start(bf16[16,2,896]{2,1,0:T(2,128)(2,1)} %shard_map.100), calls=%async_computation.2 | async-start | bytes 114688 | tf_op jit(solution)/shard_map/all_to_all | solution.py:18
  117.2 36.1 %all-to-all-start.3 = ((bf16[128,2,1536]{2,1,0:T(2,128)(2,1)}), bf16[128,2,1536]{2,1,0:T(2,128)(2,1)}, u32[]{:S(2)}, u32[]{:S(2)}) async-start(bf16[128,2,1536]{2,1,0:T(2,128)(2,1)} %bitcast.19), calls=%async_computation.3 | async-start | bytes 1572864 | tf_op jit(solution)/shard_map/all_to_all | solution.py:18
  125.5 25.2 %collective-permute-start.9 = (bf16[96,1536]{1,0:T(8,128)(2,1)S(1)}, bf16[96,1536]{1,0:T(8,128)(2,1)S(1)}, u32[]{:S(2)}, u32[]{:S(2)}) collective-permute-start(bf16[96,1536]{1,0:T(8,128)(2,1)S(1)} %get-tuple-element.14), channel_id=1, source_target_pairs={{0,8},{8,0},{1,9},{9,1},{2,10},{10,2},{3,11},{11,3},{4,12},{12,4},... | collective-permute-start | bytes 884744 | tf_op jit(solution)/shard_map/ppermute | solution.py:351
  128.6 27.0 %collective-permute-start.10 = (bf16[192,1536]{1,0:T(8,128)(2,1)S(1)}, bf16[192,1536]{1,0:T(8,128)(2,1)S(1)}, u32[]{:S(2)}, u32[]{:S(2)}) collective-permute-start(bf16[192,1536]{1,0:T(8,128)(2,1)S(1)} %bitcast.14), channel_id=1, source_target_pairs={{0,1},{1,0},{2,3},{3,2},{4,5},{5,4},{6,7},{7,6},{8,9},{9,8},{10,11... | collective-permute-start | bytes 1769480 | tf_op jit(solution)/shard_map/ppermute | solution.py:359
  133.3 22.3 %collective-permute-start.11 = (bf16[96,1536]{1,0:T(8,128)(2,1)S(1)}, bf16[96,1536]{1,0:T(8,128)(2,1)S(1)}, u32[]{:S(2)}, u32[]{:S(2)}) collective-permute-start(bf16[96,1536]{1,0:T(8,128)(2,1)S(1)} %collective-permute-done.8.refs_1_), channel_id=1, source_target_pairs={{0,1},{1,0},{2,3},{3,2},{4,5},{5,4},{6,7},{7,6},{8,9},{9,8},{10,11... | collective-permute-start | bytes 884744 | tf_op jit(solution)/shard_map/ppermute | solution.py:359
  150.7 4.9 %collective-permute-start.12 = (bf16[96,1536]{1,0:T(8,128)(2,1)S(1)}, bf16[96,1536]{1,0:T(8,128)(2,1)S(1)}, u32[]{:S(2)}, u32[]{:S(2)}) collective-permute-start(bf16[96,1536]{1,0:T(8,128)(2,1)S(1)} %collective-permute-done.9.refs_2_), channel_id=1, source_target_pairs={{0,1},{1,0},{2,3},{3,2},{4,5},{5,4},{6,7},{7,6},{8,9},{9,8},{10,11... | collective-permute-start | bytes 884744 | tf_op jit(solution)/shard_map/ppermute | solution.py:359

commit v4 on v2

--- a/solution.py
+++ b/solution.py
@@ -21,6 +21,10 @@
 NT = (((1,), (1,)), ((), ()))
 VMEM = pl.BlockSpec(memory_space=pltpu.VMEM)
 SMEM = pl.BlockSpec(memory_space=pltpu.SMEM)
+
+
+def in_hbm(a):
+    return pltpu.with_memory_space_constraint(a, pltpu.HBM)
 
 
 def limit(mib):
@@ -81,91 +85,76 @@
         in_specs=[VMEM] * 2,
         out_specs=VMEM,
         compiler_params=limit(4),
-        out_shape=jax.ShapeDtypeStruct((224, 1536), jnp.bfloat16),
-    )(q, kv)
-
-
-def gather_kernel(place, own, near, own_other, near_other, weight):
+        out_shape=pltpu.HBM((224, 1536), jnp.bfloat16),
+    )(in_hbm(q), in_hbm(kv))
+
+
+def project_kernel(place, rows, own, near, own_other, near_other, out, weight, sem):
     zp, core = place[0], place[1]
-    for piece, z, c in (
-        (own, zp, core),
-        (near, 1 - zp, core),
-        (own_other, zp, 1 - core),
-        (near_other, 1 - zp, 1 - core),
+    fetches = []
+    for k, (piece, z, c) in enumerate(
+        (
+            (own, zp, core),
+            (near, 1 - zp, core),
+            (own_other, zp, 1 - core),
+            (near_other, 1 - zp, 1 - core),
+        )
     ):
         at = z * 2 + c
-        weight[pl.ds(pl.multiple_of(at * 192, 64), 192), :] = piece[:192]
-        weight[pl.ds(pl.multiple_of(768 + at * 32, 32), 32), :] = piece[192:]
-
-
-def gather(place, pieces):
-    return pl.pallas_call(
-        gather_kernel,
-        in_specs=[SMEM] + [VMEM] * 4,
-        out_specs=VMEM,
-        out_shape=pltpu.HBM((896, 1536), jnp.bfloat16),
-        compiler_params=limit(8),
-    )(place, *pieces)
-
-
-def project_kernel(rows, weight, out):
-    total = squares = 0
-    for y in range(4):
-        a = rows[:, y].reshape(128, 384)
-        total += lax.dot_general(
-            a, weight[:, y * 384 : y * 384 + 384], NT, preferred_element_type=jnp.float32
+        q_rows = pl.ds(pl.multiple_of(at * 192, 64), 192)
+        kv_rows = pl.ds(pl.multiple_of(768 + at * 32, 32), 32)
+        fetches.append(pltpu.make_async_copy(piece.at[:192], weight.at[q_rows], sem.at[2 * k]))
+        fetches.append(
+            pltpu.make_async_copy(piece.at[192:], weight.at[kv_rows], sem.at[2 * k + 1])
         )
-        wide = a.astype(jnp.float32)
-        squares += jnp.sum(wide * wide, axis=1, keepdims=True)
-    out[:, :896] = total.astype(jnp.bfloat16)
-    high = squares.astype(jnp.bfloat16).astype(jnp.float32)
+    for fetch in fetches:
+        fetch.start()
     lane = lax.broadcasted_iota(jnp.int32, (128, 128), 1)
-    extra = jnp.where(lane == 0, high, jnp.where(lane == 1, squares - high, 0.0))
-    out[:, 896:] = extra.astype(jnp.bfloat16)
-
-
-def project(rows, weight):
+    extras = []
+    for half in range(2):
+        wide = 0
+        for y in range(4):
+            a = rows[half * 4 : half * 4 + 4, y].reshape(128, 384).astype(jnp.float32)
+            a = a * a
+            wide += a[:, :128] + a[:, 128:256] + a[:, 256:]
+        sums = jnp.sum(wide, axis=1, keepdims=True)
+        high = sums.astype(jnp.bfloat16).astype(jnp.float32)
+        extras.append(jnp.where(lane == 0, high, jnp.where(lane == 1, sums - high, 0.0)))
+    for fetch in fetches:
+        fetch.wait()
+    for half in range(2):
+        total = 0
+        for y in range(4):
+            total += lax.dot_general(
+                rows[half * 4 : half * 4 + 4, y].reshape(128, 384),
+                weight[:, y * 384 : y * 384 + 384],
+                NT,
+                preferred_element_type=jnp.float32,
+            )
+        for r in range(64):
+            at = slice(2 * r, 2 * r + 2)
+            out[half * 64 + r, :, :896] = total[at].astype(jnp.bfloat16)
+            out[half * 64 + r, :, 896:] = extras[half][at].astype(jnp.bfloat16)
+
+
+def project(place, rows, pieces):
     return pl.pallas_call(
         project_kernel,
-        grid=(2,),
-        in_specs=[
-            pl.BlockSpec((4, 4, 32, 384), lambda i: (i, 0, 0, 0)),
-            pl.BlockSpec((896, 1536), lambda i: (0, 0)),
-        ],
-        out_specs=pl.BlockSpec((128, 1024), lambda i: (i, 0)),
-        out_shape=pltpu.HBM((256, 1024), jnp.bfloat16),
-        compiler_params=limit(12),
+        in_specs=[SMEM, VMEM] + [pl.BlockSpec(memory_space=pl.ANY)] * 4,
+        out_specs=VMEM,
+        out_shape=pltpu.HBM((128, 2, 1024), jnp.bfloat16),
+        scratch_shapes=[pltpu.VMEM((896, 1536), jnp.bfloat16), pltpu.SemaphoreType.DMA((8,))],
+        compiler_params=limit(16),
         cost_estimate=pl.CostEstimate(
             flops=2 * 256 * 1536 * 896, bytes_accessed=4 * 2**20, transcendentals=0
         ),
-    )(rows, weight)
-
-
-def add_kernel(parts, touch, out):
+    )(place, rows, *(in_hbm(piece) for piece in pieces))
+
+
+def attend_kernel(table, lengths, parts, k_pool, v_pool, touch, new_kv, send, query, mixed, v_held, sem, v_sem):
     del touch
-    total = jnp.sum(parts[...].astype(jnp.float32), axis=0)
-    squares = jnp.sum(total[:, 896:], axis=1, keepdims=True)
-    normed = total[:, :896] * lax.rsqrt(squares / D + eps)
-    for r in range(8):
-        out[r] = normed[2 * r : 2 * r + 2].astype(jnp.bfloat16)
-
-
-def add(parts, touch):
-    return pl.pallas_call(
-        add_kernel,
-        grid=(2,),
-        in_specs=[
-            pl.BlockSpec((8, 16, 1024), lambda i: (0, i, 0)),
-            pl.BlockSpec((16, 128), lambda i: (0, 0)),
-        ],
-        out_specs=pl.BlockSpec((8, 2, 896), lambda i: (i, 0, 0)),
-        compiler_params=limit(4),
-        out_shape=pltpu.HBM((16, 2, 896), jnp.bfloat16),
-    )(parts, touch)
-
-
-def attend_kernel(table, lengths, parts, k_pool, v_pool, touch, new_kv, send, query, mixed, sem):
-    del touch
+    fetch = pltpu.make_async_copy(v_pool, v_held, v_sem)
+    fetch.start()
     row = lax.broadcasted_iota(jnp.int32, (24, 768), 0) % 2
     lane = lax.broadcasted_iota(jnp.int32, (1, 768), 1)
     masks = []
@@ -178,33 +167,34 @@
         masks.append(mask)
     valid = jnp.where(row == 0, masks[0], masks[1]) == 1
 
+    normed = []
+    for k in range(16):
+        total = jnp.sum(parts[:, k].astype(jnp.float32), axis=0)
+        if k == 0:
+            squares = jnp.sum(total[:, 896:], axis=1, keepdims=True)
+            inv_rms = lax.rsqrt(squares / D + eps)
+        normed.append((total[:, :896] * inv_rms).astype(jnp.bfloat16).astype(jnp.float32))
     for z in range(8):
         zq, zp = z // 2, z % 2
         for y in range(4):
             for k in range(3):
                 at, h = zp * 384 + k * 128, y * 3 + k
-                query[z, 2 * h : 2 * h + 2, :] = parts[zq * 4 + y, :, at : at + 128].astype(
-                    jnp.float32
-                )
+                query[z, 2 * h : 2 * h + 2, :] = normed[zq * 4 + y][:, at : at + 128]
     fresh = []
     for z in range(8):
         at = 768 + (z % 2) * 64
         for y in range(0, 4, 2):
-            pair = [
-                parts[(z // 2) * 4 + y + k, :, at : at + 64].astype(jnp.float32) for k in range(2)
-            ]
+            pair = [normed[(z // 2) * 4 + y + k][:, at : at + 64] for k in range(2)]
             fresh.append(jnp.concatenate(pair, axis=1))
             to = z * 256 + y * 64
             new_kv[:, to : to + 128] = fresh[-1].astype(jnp.bfloat16)
 
     scale = 1.0 / jnp.sqrt(jnp.float32(HD))
     odd = lax.broadcasted_iota(jnp.int32, (24, 128), 0) % 2 == 1
+    found = []
     for g in range(8):
-        heads = slice(g * 128, g * 128 + 128)
-        keys = k_pool[:, :, heads].reshape(768, 128)
-        values = v_pool[:, :, heads].reshape(768, 128)
+        keys = k_pool[:, :, g * 128 : g * 128 + 128].reshape(768, 128)
         own_key = jnp.where(odd, fresh[g][1:2], fresh[g][0:1])
-        own_value = jnp.where(odd, fresh[8 + g][1:2], fresh[8 + g][0:1])
         q = query[g]
         scores = lax.dot_general(
             q.astype(jnp.bfloat16), keys, NT, preferred_element_type=jnp.float32
@@ -216,7 +206,11 @@
         own = jnp.exp(own - top)
         total = jnp.sum(scores, axis=1, keepdims=True) + own
         weights = (scores / total).astype(jnp.bfloat16)
-        own = (own / total).astype(jnp.bfloat16).astype(jnp.float32)
+        found.append((weights, (own / total).astype(jnp.bfloat16).astype(jnp.float32)))
+    fetch.wait()
+    for g, (weights, own) in enumerate(found):
+        values = v_held[:, :, g * 128 : g * 128 + 128].reshape(768, 128)
+        own_value = jnp.where(odd, fresh[8 + g][1:2], fresh[8 + g][0:1])
         out = lax.dot_general(
             weights, values, (((1,), (0,)), ((), ())), preferred_element_type=jnp.float32
         )
@@ -233,7 +227,7 @@
 def attend(table, lengths, parts, k_pool, v_pool, touch):
     return pl.pallas_call(
         attend_kernel,
-        in_specs=[SMEM] * 2 + [VMEM] * 4,
+        in_specs=[SMEM] * 2 + [VMEM] * 2 + [pl.BlockSpec(memory_space=pl.ANY), VMEM],
         out_specs=[VMEM, pl.BlockSpec(memory_space=pl.ANY)],
         out_shape=[
             jax.ShapeDtypeStruct((2, 2048), jnp.bfloat16),
@@ -242,15 +236,17 @@
         scratch_shapes=[
             pltpu.VMEM((8, 24, 128), jnp.float32),
             pltpu.VMEM((8, 2, 1536), jnp.bfloat16),
+            pltpu.VMEM((24, 32, 1024), jnp.bfloat16),
             pltpu.SemaphoreType.DMA((16,)),
+            pltpu.SemaphoreType.DMA,
         ],
         compiler_params=limit(16),
-    )(table, lengths, parts, k_pool, v_pool, touch)
-
-
-def spread_kernel(place, mine, theirs, own, near_a, near_b, out):
-    near = jnp.concatenate([near_a[...], near_b[...]], axis=0)
-    for weight, to in ((own[...], place[0]), (near, 1 - place[0])):
+    )(table, lengths, parts, k_pool, in_hbm(v_pool), touch)
+
+
+def spread_kernel(place, mine, theirs, own, near, out):
+    for piece, to in ((own, place[0]), (near, 1 - place[0])):
+        weight = piece[...]
         first = lax.dot_general(mine[...], weight, NT, preferred_element_type=jnp.float32)
         second = lax.dot_general(theirs[...], weight, NT, preferred_element_type=jnp.float32)
         first, second = first.astype(jnp.bfloat16), second.astype(jnp.bfloat16)
@@ -265,7 +261,7 @@
 def spread(place, mine, theirs, pieces):
     return pl.pallas_call(
         spread_kernel,
-        in_specs=[SMEM] + [VMEM] * 5,
+        in_specs=[SMEM] + [VMEM] * 4,
         out_specs=VMEM,
         out_shape=jax.ShapeDtypeStruct((8, 2, 96, 128), jnp.bfloat16),
         compiler_params=limit(16),
@@ -309,34 +305,24 @@
     place = jnp.stack([lax.axis_index("zp"), lax.axis_index("c")])
     place = place.astype(jnp.int32)
 
-    own = join(q_weight.T, kv_weight.T)
-    near = lax.ppermute(own, "zp", OTHER)
-    pieces = (own, near, lax.ppermute(own, "c", OTHER), lax.ppermute(near, "c", OTHER))
-
-    rows = [
-        lax.ppermute(
-            part,
-            G + ("zq", "zp", "c"),
-            [
-                ((g * 8 + z) * 2 + c, (z * 8 + g) * 2 + (c ^ flip))
-                for g in range(8)
-                for z in range(8)
-                for c in range(2)
-            ],
-        )
-        for flip, part in enumerate(split(place, hidden.T))
-    ]
-    rows = a2a(copies(place, *rows, near[:16, :128]), ("zq", "zp", "yh")).reshape(8, 4, 32, 384)
+    swap = [(g * 8 + z, z * 8 + g) for g in range(8) for z in range(8)]
+    own, other = split(place, lax.ppermute(hidden.T, G + ("zq", "zp"), swap))
+    other = lax.ppermute(other, "c", OTHER)
+
+    piece = join(q_weight.T, kv_weight.T)
+    near = lax.ppermute(piece, "zp", OTHER)
+    pieces = (piece, near, lax.ppermute(piece, "c", OTHER), lax.ppermute(near, "c", OTHER))
+
+    rows = a2a(copies(place, own, other, near[:16, :128]), ("zq", "zp", "yh")).reshape(8, 4, 32, 384)
     o_own = o_weight.T
-    o_near = [lax.ppermute(half, "zp", OTHER) for half in (o_own[:96], o_own[96:])]
-
-    parts = a2a(project(rows, gather(place, pieces)).reshape(8, 32, 1024), G)
-    parts = a2a(add(parts, o_near[0][:16, :128]), ("zq", "yh"))
-    kv_rows, send = attend(page_table, lengths, parts, k_pool, v_pool, o_near[1][:16, :128])
+    o_near = lax.ppermute(o_own, "zp", OTHER)
+
+    parts = a2a(project(place, rows, pieces), G + ("zq", "yh")).reshape(8, 16, 2, 1024)
+    kv_rows, send = attend(page_table, lengths, parts, k_pool, v_pool, o_near[:16, :128])
 
     mine = a2a(send.reshape(128, 2, 1536), G + ("zq", "yh")).reshape(256, 1536)
     theirs = lax.ppermute(mine, "c", OTHER)
-    out = spread(place, mine, theirs, (o_own, *o_near))
+    out = spread(place, mine, theirs, (o_own, o_near))
     back = a2a(out.reshape(16, 96, 128), G + ("zp",)).reshape(8, 2, 96, 128)
     return (collect(place, back).T, kv_rows)
 

time: 169 us -> 180 us (1.065)
  waiting for transfers between devices: 31.5 us -> 46.5 us
  blocking collectives: 40.1 us -> 50.7 us
  starting transfers between devices: 71.7 us -> 63.7 us
  local copies, waits for them, and re-layouts: 6.99 us -> 0.33 us
    ppermute x6 -> x5, waiting for transfers between devices: 9.04 us -> 27.2 us  [the longest x1 24 us: per_device(): o_near = lax.ppermute(o_own, 'zp', OTHER)]
    all_to_all x2, blocking collectives: 40.1 us -> 50.7 us  [a2a(): return lax.all_to_all(a, axes, split_axis=0, concat_axis=0, tiled=True)]
    unnamed x18 -> x14, local copies, waits for them, and re-layouts: 5.94 us -> 0.03 us
    ppermute x1, starting transfers between devices: 8.66 us -> 4.74 us  [per_device(): theirs = lax.ppermute(mine, 'c', OTHER)]
    ppermute x6 -> x5, starting transfers between devices: 20.4 us -> 16.8 us  [the longest x1 5.88 us: per_device(): other = lax.ppermute(other, 'c', OTHER)]
    all_to_all x3 -> x2, waiting for transfers between devices: 18.5 us -> 15.2 us  [a2a(): return lax.all_to_all(a, axes, split_axis=0, concat_axis=0, tiled=True)]
    pallas_call x1, Pallas kernels: 0.05 us -> 2 us  [join(): pl.pallas_call(join_kernel, in_specs=[VMEM] * 2, out_specs=VMEM, compiler...]
    pallas_call x5 -> x3, Pallas kernels: 12.9 us -> 11.3 us  [the longest x1 5.03 us: project(): pl.pallas_call(project_kernel, in_specs=[SMEM, VMEM] + [pl.BlockSpec(memo...]
  transfers between devices with their start and end apart: 11 -> 9, of which waited for: 7 -> 5; matrix products, arithmetic and copies ran while one was open for 0% -> 0% of each run, Pallas kernels for 2% -> 0%
where the time goes in v4:
time: 180 us; the launch traced here: 179 us
  starting transfers between devices  63.7 us (35%)
  blocking collectives  50.7 us (28%)
  waiting for transfers between devices  46.5 us (26%)
  Pallas kernels  17 us (9%)
    all_to_all x2, blocking collectives, a2a(): return lax.all_to_all(a, axes, split_axis=0, concat_axis=0, tiled=True)  50.7 us
    all_to_all x2, starting transfers between devices, a2a(): return lax.all_to_all(a, axes, split_axis=0, concat_axis=0, tiled=True)  40.2 us
    ppermute x1, waiting for transfers between devices, per_device(): o_near = lax.ppermute(o_own, 'zp', OTHER)  24 us
    all_to_all x2, waiting for transfers between devices, a2a(): return lax.all_to_all(a, axes, split_axis=0, concat_axis=0, tiled=True)  15.2 us
    ppermute x1, starting transfers between devices, per_device(): other = lax.ppermute(other, 'c', OTHER)  5.88 us
    pallas_call x1, Pallas kernels, project(): pl.pallas_call(project_kernel, in_specs=[SMEM, VMEM] + [pl.BlockSpec(memo...  5.03 us
    ppermute x1, starting transfers between devices, per_device(): near = lax.ppermute(piece, 'zp', OTHER)  4.95 us
    ppermute x1, starting transfers between devices, per_device(): theirs = lax.ppermute(mine, 'c', OTHER)  4.74 us
  transfers between devices with their start and end apart: 9, of which 5 were waited for; matrix products, arithmetic and copies ran while one was open for 0% of the time, Pallas kernels for 0%

profile of v4, /device:TPU:1, one launch (start us, length us, event | category | flops | bytes accessed | tf_op | source)
XLA Modules:
  0.0 179.1 jit_solution(15261322961289992771)
XLA Ops:
  0.6 2.0 %shard_map.96.own = bf16[224,1536]{1,0:T(8,128)(2,1)} custom-call(bf16[192,1536]{1,0:T(8,128)(2,1)} %bitcast.19, bf16[32,1536]{1,0:T(8,128)(2,1)} %bitcast.20), custom_call_target="tpu_custom_call" | custom-call | tf_op jit(solution)/shard_map/pallas_call | solution.py:83
  2.6 4.9 %collective-permute-start.2 = (bf16[224,1536]{1,0:T(8,128)(2,1)}, bf16[224,1536]{1,0:T(8,128)(2,1)S(1)}, u32[]{:S(2)}, u32[]{:S(2)}) collective-permute-start(bf16[224,1536]{1,0:T(8,128)(2,1)} %shard_map.96.own), channel_id=1, source_target_pairs={{0,8},{8,0},{1,9},{9,1},{2,10},{10,2},{3,11},{11,3},{4,12},{12,4},... | collective-permute-start | bytes 2064392 | tf_op jit(solution)/shard_map/ppermute | solution.py:313
  7.6 1.5 collective-permute-start
  9.1 0.7 shard_map.95
  9.9 5.9 %collective-permute-start.1 = (bf16[64,192]{1,0:T(8,128)(2,1)S(1)}, bf16[64,192]{1,0:T(8,128)(2,1)S(1)}, u32[]{:S(2)}, u32[]{:S(2)}) collective-permute-start(bf16[64,192]{1,0:T(8,128)(2,1)S(1)} %get-tuple-element.7), channel_id=1, source_target_pairs={{0,1},{1,0},{2,3},{3,2},{4,5},{5,4},{6,7},{7,6},{8,9},{9,8},{10,11... | collective-permute-start | bytes 73736 | tf_op jit(solution)/shard_map/ppermute | solution.py:310
  15.7 3.2 %collective-permute-done.2.near = bf16[224,1536]{1,0:T(8,128)(2,1)S(1)} collective-permute-done((bf16[224,1536]{1,0:T(8,128)(2,1)}, bf16[224,1536]{1,0:T(8,128)(2,1)S(1)}, u32[]{:S(2)}, u32[]{:S(2)}) %collective-permute-start.2) | collective-permute-done | bytes 688160 | tf_op jit(solution)/shard_map/ppermute | solution.py:313
  18.9 1.6 shard_map.97
  20.5 22.3 %all-to-all-start = ((bf16[32,32,384]{2,1,0:T(8,128)(2,1)}), bf16[32,32,384]{2,1,0:T(8,128)(2,1)S(1)}, u32[]{:S(2)}, u32[]{:S(2)}) async-start(bf16[32,32,384]{2,1,0:T(8,128)(2,1)} %shard_map.97), calls=%async_computation | async-start | bytes 1572864 | tf_op jit(solution)/shard_map/all_to_all | solution.py:18
  42.8 2.5 %collective-permute-start.3 = (bf16[224,1536]{1,0:T(8,128)(2,1)S(1)}, bf16[224,1536]{1,0:T(8,128)(2,1)S(1)}, u32[]{:S(2)}, u32[]{:S(2)}) collective-permute-start(bf16[224,1536]{1,0:T(8,128)(2,1)S(1)} %copy-done.4), channel_id=1, source_target_pairs={{0,1},{1,0},{2,3},{3,2},{4,5},{5,4},{6,7},{7,6},{8,9},{9,8},{10,11... | collective-permute-start | bytes 2064392 | tf_op jit(solution)/shard_map/ppermute | solution.py:314
  45.3 1.9 %collective-permute-start.4 = (bf16[224,1536]{1,0:T(8,128)(2,1)S(1)}, bf16[224,1536]{1,0:T(8,128)(2,1)}, u32[]{:S(2)}, u32[]{:S(2)}) collective-permute-start(bf16[224,1536]{1,0:T(8,128)(2,1)S(1)} %collective-permute-done.2.near), channel_id=1, source_target_pairs={{0,1},{1,0},{2,3},{3,2},{4,5},{5,4},{6,7},{7,6},{8,9},{9,8},{10,11... | collective-permute-start | bytes 2064392 | tf_op jit(solution)/shard_map/ppermute | solution.py:314
  47.3 2.2 %collective-permute-done.4.near_other = bf16[224,1536]{1,0:T(8,128)(2,1)} collective-permute-done((bf16[224,1536]{1,0:T(8,128)(2,1)S(1)}, bf16[224,1536]{1,0:T(8,128)(2,1)}, u32[]{:S(2)}, u32[]{:S(2)}) %collective-permute-start.4) | collective-permute-done | bytes 688160 | tf_op jit(solution)/shard_map/ppermute | solution.py:314
  49.5 15.2 %all-to-all-done = bf16[32,32,384]{2,1,0:T(8,128)(2,1)S(1)} async-done(((bf16[32,32,384]{2,1,0:T(8,128)(2,1)}), bf16[32,32,384]{2,1,0:T(8,128)(2,1)S(1)}, u32[]{:S(2)}, u32[]{:S(2)}) %all-to-all-start) | async-done | bytes 786464 | tf_op jit(solution)/shard_map/all_to_all | solution.py:18
  64.7 5.0 %shard_map.98 = bf16[128,2,1024]{2,1,0:T(2,128)(2,1)} custom-call(s32[2]{0:T(128)S(1)} %pad_add_fusion.place, bf16[8,4,32,384]{3,2,1,0:T(8,128)(2,1)S(1)} %bitcast.12, bf16[224,1536]{1,0:T(8,128)(2,1)} %shard_map.96.own, bf16[224,1536]{1,0:T(8,128)(2,1)} %copy-done.5, bf16[224,1536]{1,0:T(8,128)(2,1)} %copy-done.6, ...), custom_call_target="tpu_custom_call" | custom-call | flops 704643072 | bytes 4194304 | tf_op jit(solution)/shard_map/pallas_call | solution.py:141
  69.7 17.9 %all-to-all-start.1 = ((bf16[128,2,1024]{2,1,0:T(2,128)(2,1)}), bf16[128,2,1024]{2,1,0:T(2,128)(2,1)S(1)}, u32[]{:S(2)}, u32[]{:S(2)}) async-start(bf16[128,2,1024]{2,1,0:T(2,128)(2,1)} %shard_map.98), calls=%async_computation.1 | async-start | bytes 1048576 | tf_op jit(solution)/shard_map/all_to_all | solution.py:18
  87.7 2.0 %collective-permute-start.5 = (bf16[192,1536]{1,0:T(8,128)(2,1)S(1)}, bf16[192,1536]{1,0:T(8,128)(2,1)S(1)}, u32[]{:S(2)}, u32[]{:S(2)}) collective-permute-start(bf16[192,1536]{1,0:T(8,128)(2,1)S(1)} %bitcast.16), channel_id=1, source_target_pairs={{0,8},{8,0},{1,9},{9,1},{2,10},{10,2},{3,11},{11,3},{4,12},{12,4},... | collective-permute-start | bytes 1769480 | tf_op jit(solution)/shard_map/ppermute | solution.py:318
  89.7 24.0 %collective-permute-done.5.near = bf16[192,1536]{1,0:T(8,128)(2,1)S(1)} collective-permute-done((bf16[192,1536]{1,0:T(8,128)(2,1)S(1)}, bf16[192,1536]{1,0:T(8,128)(2,1)S(1)}, u32[]{:S(2)}, u32[]{:S(2)}) %collective-permute-start.5) | collective-permute-done | bytes 589856 | tf_op jit(solution)/shard_map/ppermute | solution.py:318
  113.7 4.7 %shard_map.99 = (bf16[2,2048]{1,0:T(2,128)(2,1)}, bf16[8,16,2,1536]{3,2,1,0:T(2,128)(2,1)}) custom-call(s32[2,12]{1,0:T(2,128)S(1)} %copy-done.2, s32[2]{0:T(128)S(1)} %copy-done.3, bf16[8,16,2,1024]{3,2,1,0:T(2,128)(2,1)S(1)} %bitcast.13, bf16[24,32,1024]{2,1,0:T(8,128)(2,1)S(1)} %copy-done, bf16[24,32,1024]{2,1,0:T(8,128)(2,1)} %v_pool.1, ...), custom_call_target="tpu_custom_call" | custom-call | tf_op jit(solution)/shard_map/pallas_call | solution.py:228
  118.4 37.2 %all_to_all.20 = bf16[128,2,1536]{2,1,0:T(2,128)(2,1)S(1)} all-to-all(bf16[128,2,1536]{2,1,0:T(2,128)(2,1)} %bitcast.18), channel_id=1, replica_groups=mesh['yl'=2,'x'=4,'zq'=4,'zp'=2,'yh'=4,'c'=2] {'yl','x','zq','yh'}, dimensions={0} | all-to-all | bytes 1572864 | tf_op jit(solution)/shard_map/all_to_all | solution.py:18
  155.7 0.3 reshape.25.mine
  156.0 4.7 %collective-permute-start.6 = (bf16[256,1536]{1,0:T(8,128)(2,1)S(1)}, bf16[256,1536]{1,0:T(8,128)(2,1)S(1)}, u32[]{:S(2)}, u32[]{:S(2)}) collective-permute-start(bf16[256,1536]{1,0:T(8,128)(2,1)S(1)} %reshape.25.mine), channel_id=1, source_target_pairs={{0,1},{1,0},{2,3},{3,2},{4,5},{5,4},{6,7},{7,6},{8,9},{9,8},{10,11... | collective-permute-start | bytes 2359304 | tf_op jit(solution)/shard_map/ppermute | solution.py:324
  160.7 1.9 %collective-permute-done.6.theirs = bf16[256,1536]{1,0:T(8,128)(2,1)S(1)} collective-permute-done((bf16[256,1536]{1,0:T(8,128)(2,1)S(1)}, bf16[256,1536]{1,0:T(8,128)(2,1)S(1)}, u32[]{:S(2)}, u32[]{:S(2)}) %collective-permute-start.6) | collective-permute-done | bytes 786464 | tf_op jit(solution)/shard_map/ppermute | solution.py:324
  162.6 1.6 shard_map.100
  164.2 13.4 %all_to_all.21 = bf16[16,96,128]{2,1,0:T(8,128)(2,1)S(1)} all-to-all(bf16[16,96,128]{2,1,0:T(8,128)(2,1)S(1)} %bitcast.15), channel_id=1, replica_groups=mesh['yl'=2,'x'=4,'zq'=4,'zp'=2,'yh'=4,'c'=2] {'yl','x','zp'}, dimensions={0} | all-to-all | bytes 786432 | tf_op jit(solution)/shard_map/all_to_all | solution.py:18
  177.7 1.4 shard_map.101
  (21 shorter events, 0.1 us)
Async XLA Ops:
  2.6 40.1 %copy-start.4 = (bf16[224,1536]{1,0:T(8,128)(2,1)S(1)}, bf16[224,1536]{1,0:T(8,128)(2,1)}, u32[]{:S(2)}) copy-start(bf16[224,1536]{1,0:T(8,128)(2,1)} %shard_map.96.own) | copy-start | bytes 2064388
  2.6 16.3 %collective-permute-start.2 = (bf16[224,1536]{1,0:T(8,128)(2,1)}, bf16[224,1536]{1,0:T(8,128)(2,1)S(1)}, u32[]{:S(2)}, u32[]{:S(2)}) collective-permute-start(bf16[224,1536]{1,0:T(8,128)(2,1)} %shard_map.96.own), channel_id=1, source_target_pairs={{0,8},{8,0},{1,9},{9,1},{2,10},{10,2},{3,11},{11,3},{4,12},{12,4},... | collective-permute-start | bytes 2064392 | tf_op jit(solution)/shard_map/ppermute | solution.py:313
  7.6 1.5 collective-permute-start
  9.9 9.1 %collective-permute-start.1 = (bf16[64,192]{1,0:T(8,128)(2,1)S(1)}, bf16[64,192]{1,0:T(8,128)(2,1)S(1)}, u32[]{:S(2)}, u32[]{:S(2)}) collective-permute-start(bf16[64,192]{1,0:T(8,128)(2,1)S(1)} %get-tuple-element.7), channel_id=1, source_target_pairs={{0,1},{1,0},{2,3},{3,2},{4,5},{5,4},{6,7},{7,6},{8,9},{9,8},{10,11... | collective-permute-start | bytes 73736 | tf_op jit(solution)/shard_map/ppermute | solution.py:310
  18.9 45.7 %copy-start.5 = (bf16[224,1536]{1,0:T(8,128)(2,1)}, bf16[224,1536]{1,0:T(8,128)(2,1)S(1)}, u32[]{:S(2)}) copy-start(bf16[224,1536]{1,0:T(8,128)(2,1)S(1)} %collective-permute-done.2.near) | copy-start | bytes 2064388
  20.5 44.2 %all-to-all-start = ((bf16[32,32,384]{2,1,0:T(8,128)(2,1)}), bf16[32,32,384]{2,1,0:T(8,128)(2,1)S(1)}, u32[]{:S(2)}, u32[]{:S(2)}) async-start(bf16[32,32,384]{2,1,0:T(8,128)(2,1)} %shard_map.97), calls=%async_computation | async-start | bytes 1572864 | tf_op jit(solution)/shard_map/all_to_all | solution.py:18
  42.8 4.5 %collective-permute-start.3 = (bf16[224,1536]{1,0:T(8,128)(2,1)S(1)}, bf16[224,1536]{1,0:T(8,128)(2,1)S(1)}, u32[]{:S(2)}, u32[]{:S(2)}) collective-permute-start(bf16[224,1536]{1,0:T(8,128)(2,1)S(1)} %copy-done.4), channel_id=1, source_target_pairs={{0,1},{1,0},{2,3},{3,2},{4,5},{5,4},{6,7},{7,6},{8,9},{9,8},{10,11... | collective-permute-start | bytes 2064392 | tf_op jit(solution)/shard_map/ppermute | solution.py:314
  45.3 4.2 %collective-permute-start.4 = (bf16[224,1536]{1,0:T(8,128)(2,1)S(1)}, bf16[224,1536]{1,0:T(8,128)(2,1)}, u32[]{:S(2)}, u32[]{:S(2)}) collective-permute-start(bf16[224,1536]{1,0:T(8,128)(2,1)S(1)} %collective-permute-done.2.near), channel_id=1, source_target_pairs={{0,1},{1,0},{2,3},{3,2},{4,5},{5,4},{6,7},{7,6},{8,9},{9,8},{10,11... | collective-permute-start | bytes 2064392 | tf_op jit(solution)/shard_map/ppermute | solution.py:314
  47.3 17.4 %copy-start.6 = (bf16[224,1536]{1,0:T(8,128)(2,1)}, bf16[224,1536]{1,0:T(8,128)(2,1)S(1)}, u32[]{:S(2)}) copy-start(bf16[224,1536]{1,0:T(8,128)(2,1)S(1)} %collective-permute-done.3.own_other) | copy-start | bytes 2064388
  64.7 23.0 %copy-start.1 = (bf16[1536,192]{0,1:T(8,128)(2,1)S(1)}, bf16[1536,192]{0,1:T(8,128)(2,1)}, u32[]{:S(2)}) copy-start(bf16[1536,192]{0,1:T(8,128)(2,1)} %param.11) | copy-start | bytes 1769476
  64.7 49.0 %copy-start = (bf16[24,32,1024]{2,1,0:T(8,128)(2,1)S(1)}, bf16[24,32,1024]{2,1,0:T(8,128)(2,1)}, u32[]{:S(2)}) copy-start(bf16[24,32,1024]{2,1,0:T(8,128)(2,1)} %k_pool.1) | copy-start | bytes 4718596
  64.7 49.0 %copy-start.2 = (s32[2,12]{1,0:T(2,128)S(1)}, s32[2,12]{1,0:T(2,128)}, u32[]{:S(2)}) copy-start(s32[2,12]{1,0:T(2,128)} %table.1) | copy-start | bytes 292
  64.7 49.0 %copy-start.3 = (s32[2]{0:T(128)S(1)}, s32[2]{0:T(128)}, u32[]{:S(2)}) copy-start(s32[2]{0:T(128)} %lengths.1) | copy-start | bytes 28
  69.7 44.0 %all-to-all-start.1 = ((bf16[128,2,1024]{2,1,0:T(2,128)(2,1)}), bf16[128,2,1024]{2,1,0:T(2,128)(2,1)S(1)}, u32[]{:S(2)}, u32[]{:S(2)}) async-start(bf16[128,2,1024]{2,1,0:T(2,128)(2,1)} %shard_map.98), calls=%async_computation.1 | async-start | bytes 1048576 | tf_op jit(solution)/shard_map/all_to_all | solution.py:18
  87.7 26.0 %collective-permute-start.5 = (bf16[192,1536]{1,0:T(8,128)(2,1)S(1)}, bf16[192,1536]{1,0:T(8,128)(2,1)S(1)}, u32[]{:S(2)}, u32[]{:S(2)}) collective-permute-start(bf16[192,1536]{1,0:T(8,128)(2,1)S(1)} %bitcast.16), channel_id=1, source_target_pairs={{0,8},{8,0},{1,9},{9,1},{2,10},{10,2},{3,11},{11,3},{4,12},{12,4},... | collective-permute-start | bytes 1769480 | tf_op jit(solution)/shard_map/ppermute | solution.py:318
  156.0 6.6 %collective-permute-start.6 = (bf16[256,1536]{1,0:T(8,128)(2,1)S(1)}, bf16[256,1536]{1,0:T(8,128)(2,1)S(1)}, u32[]{:S(2)}, u32[]{:S(2)}) collective-permute-start(bf16[256,1536]{1,0:T(8,128)(2,1)S(1)} %reshape.25.mine), channel_id=1, source_target_pairs={{0,1},{1,0},{2,3},{3,2},{4,5},{5,4},{6,7},{7,6},{8,9},{9,8},{10,11... | collective-permute-start | bytes 2359304 | tf_op jit(solution)/shard_map/ppermute | solution.py:324

commit v5 on v3

--- a/solution.py
+++ b/solution.py
@@ -74,84 +74,77 @@
     )(place, own, other, touch)
 
 
-def join_kernel(q, kv, first, second):
-    first[...] = q[:112]
-    second[:80] = q[112:]
-    second[80:] = kv[...]
+def join_kernel(q, kv, out):
+    out[:192] = q[...]
+    out[192:] = kv[...]
 
 
 def join(q, kv):
     return pl.pallas_call(
         join_kernel,
         in_specs=[VMEM] * 2,
-        out_specs=[VMEM] * 2,
-        compiler_params=limit(4),
-        out_shape=[jax.ShapeDtypeStruct((112, 1536), jnp.bfloat16)] * 2,
+        out_specs=VMEM,
+        compiler_params=limit(4),
+        out_shape=jax.ShapeDtypeStruct((224, 1536), jnp.bfloat16),
     )(in_hbm(q), in_hbm(kv))
 
 
-def gather_kernel(place, *refs):
+def project_kernel(place, rows, own, near, own_other, near_other, out, weight, sem):
     zp, core = place[0], place[1]
-    weight = refs[8]
-    for k, (z, c) in enumerate(((zp, core), (1 - zp, core), (zp, 1 - core), (1 - zp, 1 - core))):
-        first, second = refs[2 * k], refs[2 * k + 1]
-        at = pl.multiple_of((z * 2 + c) * 192, 64)
-        weight[pl.ds(at, 112), :] = first[...]
-        weight[pl.ds(pl.multiple_of(at + 112, 16), 80), :] = second[:80]
-        at = 768 + (z * 2 + c) * 32
-        weight[pl.ds(pl.multiple_of(at, 32), 32), :] = second[80:]
-
-
-def gather(place, pieces):
-    return pl.pallas_call(
-        gather_kernel,
-        in_specs=[SMEM] + [VMEM] * 8,
-        out_specs=VMEM,
-        out_shape=pltpu.HBM((896, 1536), jnp.bfloat16),
-        compiler_params=limit(8),
-    )(place, *pieces)
-
-
-def project_kernel(rows, weight, out, total, squares):
-    step = pl.program_id(0)
-
-    @pl.when(step == 0)
-    def _():
-        total[...] = jnp.zeros_like(total)
-        squares[...] = jnp.zeros_like(squares)
-
-    a = rows[:, 0].reshape(256, 384)
-    total[...] += lax.dot_general(a, weight[...], NT, preferred_element_type=jnp.float32)
-    wide = a.astype(jnp.float32)
-    wide = wide * wide
-    squares[...] += wide[:, :128] + wide[:, 128:256] + wide[:, 256:]
-
-    @pl.when(step == 3)
-    def _():
-        out[:, :896] = total[...].astype(jnp.bfloat16)
-        sums = jnp.sum(squares[...], axis=1, keepdims=True)
+    fetches = []
+    for k, (piece, z, c) in enumerate(
+        (
+            (own, zp, core),
+            (near, 1 - zp, core),
+            (own_other, zp, 1 - core),
+            (near_other, 1 - zp, 1 - core),
+        )
+    ):
+        at = z * 2 + c
+        q_rows = pl.ds(pl.multiple_of(at * 192, 64), 192)
+        kv_rows = pl.ds(pl.multiple_of(768 + at * 32, 32), 32)
+        fetches.append(pltpu.make_async_copy(piece.at[:192], weight.at[q_rows], sem.at[2 * k]))
+        fetches.append(
+            pltpu.make_async_copy(piece.at[192:], weight.at[kv_rows], sem.at[2 * k + 1])
+        )
+    for fetch in fetches:
+        fetch.start()
+    lane = lax.broadcasted_iota(jnp.int32, (128, 128), 1)
+    for half in range(2):
+        wide = 0
+        for y in range(4):
+            a = rows[half * 4 : half * 4 + 4, y].reshape(128, 384).astype(jnp.float32)
+            a = a * a
+            wide += a[:, :128] + a[:, 128:256] + a[:, 256:]
+        sums = jnp.sum(wide, axis=1, keepdims=True)
         high = sums.astype(jnp.bfloat16).astype(jnp.float32)
-        lane = lax.broadcasted_iota(jnp.int32, (256, 128), 1)
         extra = jnp.where(lane == 0, high, jnp.where(lane == 1, sums - high, 0.0))
-        out[:, 896:] = extra.astype(jnp.bfloat16)
-
-
-def project(rows, weight):
+        out[half * 128 : half * 128 + 128, 896:] = extra.astype(jnp.bfloat16)
+    for fetch in fetches:
+        fetch.wait()
+    total = 0
+    for y in range(4):
+        total += lax.dot_general(
+            rows[:, y].reshape(256, 384),
+            weight[:, y * 384 : y * 384 + 384],
+            NT,
+            preferred_element_type=jnp.float32,
+        )
+    out[:, :896] = total.astype(jnp.bfloat16)
+
+
+def project(place, rows, pieces):
     return pl.pallas_call(
         project_kernel,
-        grid=(4,),
-        in_specs=[
-            pl.BlockSpec((8, 1, 32, 384), lambda i: (0, i, 0, 0)),
-            pl.BlockSpec((896, 384), lambda i: (0, i)),
-        ],
-        out_specs=pl.BlockSpec((256, 1024), lambda i: (0, 0)),
+        in_specs=[SMEM, VMEM] + [pl.BlockSpec(memory_space=pl.ANY)] * 4,
+        out_specs=VMEM,
         out_shape=pltpu.HBM((256, 1024), jnp.bfloat16),
-        scratch_shapes=[pltpu.VMEM((256, 896), jnp.float32), pltpu.VMEM((256, 128), jnp.float32)],
-        compiler_params=limit(12),
+        scratch_shapes=[pltpu.VMEM((896, 1536), jnp.bfloat16), pltpu.SemaphoreType.DMA((8,))],
+        compiler_params=limit(16),
         cost_estimate=pl.CostEstimate(
             flops=2 * 256 * 1536 * 896, bytes_accessed=4 * 2**20, transcendentals=0
         ),
-    )(rows, in_hbm(weight))
+    )(place, rows, *(in_hbm(piece) for piece in pieces))
 
 
 def add_kernel(parts, out):
@@ -175,8 +168,8 @@
     )(parts)
 
 
-def attend_kernel(table, lengths, parts, k_pool, v_pool, touch, new_kv, send, query, mixed, v_held, sem, v_sem):
-    del touch
+def attend_kernel(table, lengths, parts, k_pool, v_pool, first, second, new_kv, send, query, mixed, v_held, sem, v_sem):
+    del first, second
     fetch = pltpu.make_async_copy(v_pool, v_held, v_sem)
     fetch.start()
     row = lax.broadcasted_iota(jnp.int32, (24, 768), 0) % 2
@@ -245,10 +238,10 @@
         copy.wait()
 
 
-def attend(table, lengths, parts, k_pool, v_pool, touch):
+def attend(table, lengths, parts, k_pool, v_pool, first, second):
     return pl.pallas_call(
         attend_kernel,
-        in_specs=[SMEM] * 2 + [VMEM] * 2 + [pl.BlockSpec(memory_space=pl.ANY), VMEM],
+        in_specs=[SMEM] * 2 + [VMEM] * 2 + [pl.BlockSpec(memory_space=pl.ANY)] + [VMEM] * 2,
         out_specs=[VMEM, pl.BlockSpec(memory_space=pl.ANY)],
         out_shape=[
             jax.ShapeDtypeStruct((2, 2048), jnp.bfloat16),
@@ -262,15 +255,14 @@
             pltpu.SemaphoreType.DMA,
         ],
         compiler_params=limit(16),
-    )(table, lengths, parts, k_pool, in_hbm(v_pool), touch)
+    )(table, lengths, parts, k_pool, in_hbm(v_pool), first, second)
 
 
 def spread_kernel(place, rows, *refs):
     zp, core = place[0], place[1]
-    out = refs[6]
-    pieces = [refs[0][...], jnp.concatenate([refs[1][...], refs[2][...]], axis=0)]
-    pieces += [refs[3][...], jnp.concatenate([refs[4][...], refs[5][...]], axis=0)]
-    for k, weight in enumerate(pieces):
+    out = refs[4]
+    for k in range(4):
+        weight = refs[k][...]
         z = zp if k % 2 == 0 else 1 - zp
         c = core if k < 2 else 1 - core
         part = lax.dot_general(rows[...], weight, NT, preferred_element_type=jnp.float32)
@@ -286,7 +278,7 @@
 def spread(place, rows, pieces):
     return pl.pallas_call(
         spread_kernel,
-        in_specs=[SMEM] + [VMEM] * 7,
+        in_specs=[SMEM] + [VMEM] * 5,
         out_specs=VMEM,
         out_shape=jax.ShapeDtypeStruct((8, 4, 48, 128), jnp.bfloat16),
         compiler_params=limit(16),
@@ -330,8 +322,11 @@
     place = place.astype(jnp.int32)
 
     own = join(q_weight.T, kv_weight.T)
-    near = [lax.ppermute(part, "zp", OTHER) for part in own]
-    pieces = (*own, *near, *(lax.ppermute(part, "c", OTHER) for part in (*own, *near)))
+    near = lax.ppermute(own, "zp", OTHER)
+    pieces = (own, near, lax.ppermute(own, "c", OTHER), lax.ppermute(near, "c", OTHER))
+    o_own = o_weight.T
+    o_near = lax.ppermute(o_own, "zp", OTHER)
+    o_pieces = (o_own, o_near, lax.ppermute(o_own, "c", OTHER), lax.ppermute(o_near, "c", OTHER))
 
     rows = [
         lax.ppermute(
@@ -346,17 +341,15 @@
         )
         for flip, part in enumerate(split(place, hidden.T))
     ]
-    rows = a2a(copies(place, *rows, near[0][:16, :128]), ("zq", "zp", "yh")).reshape(8, 4, 32, 384)
-    o_own = o_weight.T
-    o_near = [lax.ppermute(half, "zp", OTHER) for half in (o_own[:96], o_own[96:])]
-    o_pieces = (o_own, *o_near)
-
-    parts = a2a(project(rows, gather(place, pieces)).reshape(8, 32, 1024), G)
+    rows = a2a(copies(place, *rows, near[:16, :128]), ("zq", "zp", "yh")).reshape(8, 4, 32, 384)
+
+    parts = a2a(project(place, rows, pieces).reshape(8, 32, 1024), G)
     parts = a2a(add(parts), ("zq", "yh"))
-    kv_rows, send = attend(page_table, lengths, parts, k_pool, v_pool, o_near[0][:16, :128])
+    first, second = (piece[:16, :128] for piece in o_pieces[2:])
+    kv_rows, send = attend(page_table, lengths, parts, k_pool, v_pool, first, second)
 
     mine = a2a(send.reshape(128, 2, 1536), G + ("zq", "yh")).reshape(256, 1536)
-    out = spread(place, mine, (*o_pieces, *(lax.ppermute(part, "c", OTHER) for part in o_pieces)))
+    out = spread(place, mine, o_pieces)
     back = a2a(out.reshape(32, 48, 128), G + ("zp", "c")).reshape(8, 4, 48, 128)
     return (collect(back).T, kv_rows)
 

time: 174 us -> 162 us (0.931)
  blocking collectives: 15.1 us -> 49.7 us
  waiting for transfers between devices: 50.6 us -> 27.6 us
  starting transfers between devices: 84.5 us -> 65.9 us
  local copies, waits for them, and re-layouts: 3.06 us -> 0.34 us
  Pallas kernels: 19 us -> 17.1 us
    all_to_all x1 -> x2, blocking collectives: 15.1 us -> 49.7 us  [a2a(): return lax.all_to_all(a, axes, split_axis=0, concat_axis=0, tiled=True)]
    ppermute x11 -> x6, waiting for transfers between devices: 33.5 us -> 3.4 us  [the longest x1 3.39 us: per_device(): near = lax.ppermute(own, 'zp', OTHER)]
    ppermute x11 -> x6, starting transfers between devices: 32.1 us -> 18.7 us  [the longest x1 4.83 us: per_device(): near = lax.ppermute(own, 'zp', OTHER)]
    all_to_all x4 -> x3, waiting for transfers between devices: 16.3 us -> 24.2 us  [a2a(): return lax.all_to_all(a, axes, split_axis=0, concat_axis=0, tiled=True)]
    all_to_all x4 -> x3, starting transfers between devices: 45.9 us -> 40.7 us  [a2a(): return lax.all_to_all(a, axes, split_axis=0, concat_axis=0, tiled=True)]
    reshape x1, local copies, waits for them, and re-layouts: 2.27 us -> 0.3 us  [per_device(): mine = a2a(send.reshape(128, 2, 1536), G + ('zq', 'yh')).reshape(256, 1536)]
    pallas_call x4 -> x3, Pallas kernels: 9.72 us -> 7.86 us  [the longest x1 4.42 us: project(): pl.pallas_call(project_kernel, in_specs=[SMEM, VMEM] + [pl.BlockSpec(memo...]
  transfers between devices with their start and end apart: 17 -> 11, of which waited for: 6 -> 4; matrix products, arithmetic and copies ran while one was open for 2% -> 0% of each run, Pallas kernels for 2% -> 4%
where the time goes in v5:
time: 162 us
  starting transfers between devices  65.9 us (41%)
  blocking collectives  49.7 us (31%)
  waiting for transfers between devices  27.6 us (17%)
  Pallas kernels  17.1 us (11%)
    all_to_all x2, blocking collectives, a2a(): return lax.all_to_all(a, axes, split_axis=0, concat_axis=0, tiled=True)  49.7 us
    all_to_all x3, starting transfers between devices, a2a(): return lax.all_to_all(a, axes, split_axis=0, concat_axis=0, tiled=True)  40.7 us
    all_to_all x3, waiting for transfers between devices, a2a(): return lax.all_to_all(a, axes, split_axis=0, concat_axis=0, tiled=True)  24.2 us
    ppermute x2, starting transfers between devices, per_device(): lax.ppermute(part, G + ('zq', 'zp', 'c'), [((g * 8 + z) * 2 + c, (z * 8 +...  6.54 us
    pallas_call x1, Pallas kernels, attend(): pl.pallas_call(attend_kernel, in_specs=[SMEM] * 2 + [VMEM] * 2 + [pl.Bloc...  4.93 us
    ppermute x1, starting transfers between devices, per_device(): near = lax.ppermute(own, 'zp', OTHER)  4.83 us
    pallas_call x1, Pallas kernels, project(): pl.pallas_call(project_kernel, in_specs=[SMEM, VMEM] + [pl.BlockSpec(memo...  4.42 us
    ppermute x1, starting transfers between devices, per_device(): lax.ppermute(own, 'c', OTHER)  3.74 us
  transfers between devices with their start and end apart: 11, of which 4 were waited for; matrix products, arithmetic and copies ran while one was open for 0% of the time, Pallas kernels for 4%

profile of v5, /device:TPU:1, one launch (start us, length us, event | category | flops | bytes accessed | tf_op | source)
XLA Modules:
  0.0 161.5 jit_solution(4652379768908759008)
XLA Ops:
  0.6 1.1 shard_map.96.own
  1.8 4.8 %collective-permute-start.2 = (bf16[224,1536]{1,0:T(8,128)(2,1)S(1)}, bf16[224,1536]{1,0:T(8,128)(2,1)S(1)}, u32[]{:S(2)}, u32[]{:S(2)}) collective-permute-start(bf16[224,1536]{1,0:T(8,128)(2,1)S(1)} %shard_map.96.own), channel_id=1, source_target_pairs={{0,8},{8,0},{1,9},{9,1},{2,10},{10,2},{3,11},{11,3},{4,12},{12,4},... | collective-permute-start | bytes 2064392 | tf_op jit(solution)/shard_map/ppermute | solution.py:325
  6.7 1.0 shard_map.95
  8.3 5.9 %collective-permute-start.1 = (bf16[64,192]{1,0:T(8,128)(2,1)S(1)}, bf16[64,192]{1,0:T(8,128)(2,1)S(1)}, u32[]{:S(2)}, u32[]{:S(2)}) collective-permute-start(bf16[64,192]{1,0:T(8,128)(2,1)S(1)} %get-tuple-element.7), channel_id=1, source_target_pairs={{0,1},{1,0},{8,65},{9,64},{16,129},{17,128},{24,193},{25,192},{32,... | collective-permute-start | bytes 73736 | tf_op jit(solution)/shard_map/ppermute | solution.py:332
  14.2 3.4 %collective-permute-done.2.near = bf16[224,1536]{1,0:T(8,128)(2,1)S(1)} collective-permute-done((bf16[224,1536]{1,0:T(8,128)(2,1)S(1)}, bf16[224,1536]{1,0:T(8,128)(2,1)S(1)}, u32[]{:S(2)}, u32[]{:S(2)}) %collective-permute-start.2) | collective-permute-done | bytes 688160 | tf_op jit(solution)/shard_map/ppermute | solution.py:325
  17.6 1.6 shard_map.97
  19.2 20.0 %all-to-all-start = ((bf16[32,32,384]{2,1,0:T(8,128)(2,1)}), bf16[32,32,384]{2,1,0:T(8,128)(2,1)S(1)}, u32[]{:S(2)}, u32[]{:S(2)}) async-start(bf16[32,32,384]{2,1,0:T(8,128)(2,1)} %shard_map.97), calls=%async_computation | async-start | bytes 1572864 | tf_op jit(solution)/shard_map/all_to_all | solution.py:18
  39.2 3.7 %collective-permute-start.3 = (bf16[224,1536]{1,0:T(8,128)(2,1)S(1)}, bf16[224,1536]{1,0:T(8,128)(2,1)S(1)}, u32[]{:S(2)}, u32[]{:S(2)}) collective-permute-start(bf16[224,1536]{1,0:T(8,128)(2,1)S(1)} %shard_map.96.own), channel_id=1, source_target_pairs={{0,1},{1,0},{2,3},{3,2},{4,5},{5,4},{6,7},{7,6},{8,9},{9,8},{10,11... | collective-permute-start | bytes 2064392 | tf_op jit(solution)/shard_map/ppermute | solution.py:326
  43.0 1.9 %collective-permute-start.4 = (bf16[224,1536]{1,0:T(8,128)(2,1)S(1)}, bf16[224,1536]{1,0:T(8,128)(2,1)S(1)}, u32[]{:S(2)}, u32[]{:S(2)}) collective-permute-start(bf16[224,1536]{1,0:T(8,128)(2,1)S(1)} %collective-permute-done.2.near), channel_id=1, source_target_pairs={{0,1},{1,0},{2,3},{3,2},{4,5},{5,4},{6,7},{7,6},{8,9},{9,8},{10,11... | collective-permute-start | bytes 2064392 | tf_op jit(solution)/shard_map/ppermute | solution.py:326
  44.9 3.4 %collective-permute-start.6 = (bf16[192,1536]{1,0:T(8,128)(2,1)}, bf16[192,1536]{1,0:T(8,128)(2,1)}, u32[]{:S(2)}, u32[]{:S(2)}) collective-permute-start(bf16[192,1536]{1,0:T(8,128)(2,1)} %bitcast.7.refs_0_), channel_id=1, source_target_pairs={{0,8},{8,0},{1,9},{9,1},{2,10},{10,2},{3,11},{11,3},{4,12},{12,4},... | collective-permute-start | bytes 1769480 | tf_op jit(solution)/shard_map/ppermute | solution.py:328
  48.4 10.0 %all-to-all-done = bf16[32,32,384]{2,1,0:T(8,128)(2,1)S(1)} async-done(((bf16[32,32,384]{2,1,0:T(8,128)(2,1)}), bf16[32,32,384]{2,1,0:T(8,128)(2,1)S(1)}, u32[]{:S(2)}, u32[]{:S(2)}) %all-to-all-start) | async-done | bytes 786464 | tf_op jit(solution)/shard_map/all_to_all | solution.py:18
  58.4 4.4 %shard_map.98 = bf16[256,1024]{1,0:T(8,128)(2,1)} custom-call(s32[2]{0:T(128)S(1)} %pad_add_fusion.place, bf16[8,4,32,384]{3,2,1,0:T(8,128)(2,1)S(1)} %bitcast.12, bf16[224,1536]{1,0:T(8,128)(2,1)} %copy-done, bf16[224,1536]{1,0:T(8,128)(2,1)} %copy-done.4, bf16[224,1536]{1,0:T(8,128)(2,1)} %copy-done.5, bf16[224,1536]{1,0:T(8,128)(2,1)} %copy-done.6), custom_call_target="tpu_custom_call" | custom-call | flops 704643072 | bytes 4194304 | tf_op jit(solution)/shard_map/pallas_call | solution.py:137
  62.9 17.2 %all-to-all-start.1 = ((bf16[8,32,1024]{2,1,0:T(8,128)(2,1)}), bf16[8,32,1024]{2,1,0:T(8,128)(2,1)S(1)}, u32[]{:S(2)}, u32[]{:S(2)}) async-start(bf16[8,32,1024]{2,1,0:T(8,128)(2,1)} %bitcast.15), calls=%async_computation.1 | async-start | bytes 1048576 | tf_op jit(solution)/shard_map/all_to_all | solution.py:18
  80.0 2.8 %collective-permute-start.5 = (bf16[192,1536]{1,0:T(8,128)(2,1)}, bf16[192,1536]{1,0:T(8,128)(2,1)S(1)}, u32[]{:S(2)}, u32[]{:S(2)}) collective-permute-start(bf16[192,1536]{1,0:T(8,128)(2,1)} %bitcast.7.refs_0_), channel_id=1, source_target_pairs={{0,1},{1,0},{2,3},{3,2},{4,5},{5,4},{6,7},{7,6},{8,9},{9,8},{10,11... | collective-permute-start | bytes 1769480 | tf_op jit(solution)/shard_map/ppermute | solution.py:329
  82.9 1.9 %collective-permute-start.7 = (bf16[192,1536]{1,0:T(8,128)(2,1)}, bf16[192,1536]{1,0:T(8,128)(2,1)S(1)}, u32[]{:S(2)}, u32[]{:S(2)}) collective-permute-start(bf16[192,1536]{1,0:T(8,128)(2,1)} %collective-permute-done.6.refs_1_), channel_id=1, source_target_pairs={{0,1},{1,0},{2,3},{3,2},{4,5},{5,4},{6,7},{7,6},{8,9},{9,8},{10,11... | collective-permute-start | bytes 1769480 | tf_op jit(solution)/shard_map/ppermute | solution.py:329
  84.8 3.0 %all-to-all-done.1.parts = bf16[8,32,1024]{2,1,0:T(8,128)(2,1)S(1)} async-done(((bf16[8,32,1024]{2,1,0:T(8,128)(2,1)}), bf16[8,32,1024]{2,1,0:T(8,128)(2,1)S(1)}, u32[]{:S(2)}, u32[]{:S(2)}) %all-to-all-start.1) | async-done | bytes 524320 | tf_op jit(solution)/shard_map/all_to_all | solution.py:18
  87.8 0.9 shard_map.99
  88.7 3.5 %all-to-all-start.2 = ((bf16[16,2,896]{2,1,0:T(2,128)(2,1)}), bf16[16,2,896]{2,1,0:T(2,128)(2,1)S(1)}, u32[]{:S(2)}, u32[]{:S(2)}) async-start(bf16[16,2,896]{2,1,0:T(2,128)(2,1)} %shard_map.99), calls=%async_computation.2 | async-start | bytes 114688 | tf_op jit(solution)/shard_map/all_to_all | solution.py:18
  92.2 11.2 %all-to-all-done.2.parts = bf16[16,2,896]{2,1,0:T(2,128)(2,1)S(1)} async-done(((bf16[16,2,896]{2,1,0:T(2,128)(2,1)}), bf16[16,2,896]{2,1,0:T(2,128)(2,1)S(1)}, u32[]{:S(2)}, u32[]{:S(2)}) %all-to-all-start.2) | async-done | bytes 57376 | tf_op jit(solution)/shard_map/all_to_all | solution.py:18
  103.4 4.9 %shard_map.100 = (bf16[2,2048]{1,0:T(2,128)(2,1)}, bf16[8,16,2,1536]{3,2,1,0:T(2,128)(2,1)}) custom-call(s32[2,12]{1,0:T(2,128)S(1)} %copy-done.2, s32[2]{0:T(128)S(1)} %copy-done.3, bf16[16,2,896]{2,1,0:T(2,128)(2,1)S(1)} %all-to-all-done.2.parts, bf16[24,32,1024]{2,1,0:T(8,128)(2,1)S(1)} %copy-done.1, bf16[24,32,1024]{2,1,0:T(8,128)(2,1)} %v_pool.1, ...), custom_call_target="tpu_custom_call" | custom-call | tf_op jit(solution)/shard_map/pallas_call | solution.py:242
  108.4 31.2 %all_to_all.25 = bf16[128,2,1536]{2,1,0:T(2,128)(2,1)S(1)} all-to-all(bf16[128,2,1536]{2,1,0:T(2,128)(2,1)} %bitcast.16), channel_id=1, replica_groups=mesh['yl'=2,'x'=4,'zq'=4,'zp'=2,'yh'=4,'c'=2] {'yl','x','zq','yh'}, dimensions={0} | all-to-all | bytes 1572864 | tf_op jit(solution)/shard_map/all_to_all | solution.py:18
  139.9 2.3 %shard_map.101 = bf16[8,4,48,128]{3,2,1,0:T(8,128)(2,1)S(1)} custom-call(s32[2]{0:T(128)S(1)} %pad_add_fusion.place, bf16[256,1536]{1,0:T(8,128)(2,1)S(1)} %reshape.25.rows, bf16[192,1536]{1,0:T(8,128)(2,1)} %bitcast.7.refs_0_, bf16[192,1536]{1,0:T(8,128)(2,1)} %collective-permute-done.6.refs_1_, bf16[192,1536]{1,0:T(8,128)(2,1)S(1)} %collective-permute-done.5.refs_2_, ...), custom_call_target="tpu_custom_call" | custom-call | flops 603979776 | bytes 4194304 | tf_op jit(solution)/shard_map/pallas_call | solution.py:279
  142.2 18.4 %all_to_all.26 = bf16[32,48,128]{2,1,0:T(8,128)(2,1)S(1)} all-to-all(bf16[32,48,128]{2,1,0:T(8,128)(2,1)S(1)} %bitcast.14), channel_id=1, replica_groups=mesh['yl'=2,'x'=4,'zq'=4,'zp'=2,'yh'=4,'c'=2] {'yl','x','zp','c'}, dimensions={0} | all-to-all | bytes 786432 | tf_op jit(solution)/shard_map/all_to_all | solution.py:18
  160.7 0.9 shard_map.102
  (27 shorter events, 1.1 us)
Async XLA Ops:
  1.7 56.6 %copy-start = (bf16[224,1536]{1,0:T(8,128)(2,1)}, bf16[224,1536]{1,0:T(8,128)(2,1)S(1)}, u32[]{:S(2)}) copy-start(bf16[224,1536]{1,0:T(8,128)(2,1)S(1)} %shard_map.96.own) | copy-start | bytes 2064388
  1.8 15.9 %collective-permute-start.2 = (bf16[224,1536]{1,0:T(8,128)(2,1)S(1)}, bf16[224,1536]{1,0:T(8,128)(2,1)S(1)}, u32[]{:S(2)}, u32[]{:S(2)}) collective-permute-start(bf16[224,1536]{1,0:T(8,128)(2,1)S(1)} %shard_map.96.own), channel_id=1, source_target_pairs={{0,8},{8,0},{1,9},{9,1},{2,10},{10,2},{3,11},{11,3},{4,12},{12,4},... | collective-permute-start | bytes 2064392 | tf_op jit(solution)/shard_map/ppermute | solution.py:325
  7.7 10.0 %collective-permute-start = (bf16[64,192]{1,0:T(8,128)(2,1)S(1)}, bf16[64,192]{1,0:T(8,128)(2,1)S(1)}, u32[]{:S(2)}, u32[]{:S(2)}) collective-permute-start(bf16[64,192]{1,0:T(8,128)(2,1)S(1)} %get-tuple-element.6), channel_id=1, source_target_pairs={{0,0},{1,1},{8,64},{9,65},{16,128},{17,129},{24,192},{25,193},{32,... | collective-permute-start | bytes 73736 | tf_op jit(solution)/shard_map/ppermute | solution.py:332
  8.3 9.3 %collective-permute-start.1 = (bf16[64,192]{1,0:T(8,128)(2,1)S(1)}, bf16[64,192]{1,0:T(8,128)(2,1)S(1)}, u32[]{:S(2)}, u32[]{:S(2)}) collective-permute-start(bf16[64,192]{1,0:T(8,128)(2,1)S(1)} %get-tuple-element.7), channel_id=1, source_target_pairs={{0,1},{1,0},{8,65},{9,64},{16,129},{17,128},{24,193},{25,192},{32,... | collective-permute-start | bytes 73736 | tf_op jit(solution)/shard_map/ppermute | solution.py:332
  17.6 40.8 %copy-start.4 = (bf16[224,1536]{1,0:T(8,128)(2,1)}, bf16[224,1536]{1,0:T(8,128)(2,1)S(1)}, u32[]{:S(2)}) copy-start(bf16[224,1536]{1,0:T(8,128)(2,1)S(1)} %collective-permute-done.2.near) | copy-start | bytes 2064388
  19.2 39.2 %all-to-all-start = ((bf16[32,32,384]{2,1,0:T(8,128)(2,1)}), bf16[32,32,384]{2,1,0:T(8,128)(2,1)S(1)}, u32[]{:S(2)}, u32[]{:S(2)}) async-start(bf16[32,32,384]{2,1,0:T(8,128)(2,1)} %shard_map.97), calls=%async_computation | async-start | bytes 1572864 | tf_op jit(solution)/shard_map/all_to_all | solution.py:18
  39.2 9.1 %collective-permute-start.3 = (bf16[224,1536]{1,0:T(8,128)(2,1)S(1)}, bf16[224,1536]{1,0:T(8,128)(2,1)S(1)}, u32[]{:S(2)}, u32[]{:S(2)}) collective-permute-start(bf16[224,1536]{1,0:T(8,128)(2,1)S(1)} %shard_map.96.own), channel_id=1, source_target_pairs={{0,1},{1,0},{2,3},{3,2},{4,5},{5,4},{6,7},{7,6},{8,9},{9,8},{10,11... | collective-permute-start | bytes 2064392 | tf_op jit(solution)/shard_map/ppermute | solution.py:326
  43.0 5.4 %collective-permute-start.4 = (bf16[224,1536]{1,0:T(8,128)(2,1)S(1)}, bf16[224,1536]{1,0:T(8,128)(2,1)S(1)}, u32[]{:S(2)}, u32[]{:S(2)}) collective-permute-start(bf16[224,1536]{1,0:T(8,128)(2,1)S(1)} %collective-permute-done.2.near), channel_id=1, source_target_pairs={{0,1},{1,0},{2,3},{3,2},{4,5},{5,4},{6,7},{7,6},{8,9},{9,8},{10,11... | collective-permute-start | bytes 2064392 | tf_op jit(solution)/shard_map/ppermute | solution.py:326
  44.9 38.0 %collective-permute-start.6 = (bf16[192,1536]{1,0:T(8,128)(2,1)}, bf16[192,1536]{1,0:T(8,128)(2,1)}, u32[]{:S(2)}, u32[]{:S(2)}) collective-permute-start(bf16[192,1536]{1,0:T(8,128)(2,1)} %bitcast.7.refs_0_), channel_id=1, source_target_pairs={{0,8},{8,0},{1,9},{9,1},{2,10},{10,2},{3,11},{11,3},{4,12},{12,4},... | collective-permute-start | bytes 1769480 | tf_op jit(solution)/shard_map/ppermute | solution.py:328
  48.3 10.0 %copy-start.5 = (bf16[224,1536]{1,0:T(8,128)(2,1)}, bf16[224,1536]{1,0:T(8,128)(2,1)S(1)}, u32[]{:S(2)}) copy-start(bf16[224,1536]{1,0:T(8,128)(2,1)S(1)} %collective-permute-done.3.own_other) | copy-start | bytes 2064388
  48.4 10.0 %copy-start.6 = (bf16[224,1536]{1,0:T(8,128)(2,1)}, bf16[224,1536]{1,0:T(8,128)(2,1)S(1)}, u32[]{:S(2)}) copy-start(bf16[224,1536]{1,0:T(8,128)(2,1)S(1)} %collective-permute-done.4.near_other) | copy-start | bytes 2064388
  62.8 40.6 %copy-start.1 = (bf16[24,32,1024]{2,1,0:T(8,128)(2,1)S(1)}, bf16[24,32,1024]{2,1,0:T(8,128)(2,1)}, u32[]{:S(2)}) copy-start(bf16[24,32,1024]{2,1,0:T(8,128)(2,1)} %k_pool.1) | copy-start | bytes 4718596
  62.8 40.6 %copy-start.2 = (s32[2,12]{1,0:T(2,128)S(1)}, s32[2,12]{1,0:T(2,128)}, u32[]{:S(2)}) copy-start(s32[2,12]{1,0:T(2,128)} %table.1) | copy-start | bytes 292
  62.8 40.6 %copy-start.3 = (s32[2]{0:T(128)S(1)}, s32[2]{0:T(128)}, u32[]{:S(2)}) copy-start(s32[2]{0:T(128)} %lengths.1) | copy-start | bytes 28
  62.9 24.9 %all-to-all-start.1 = ((bf16[8,32,1024]{2,1,0:T(8,128)(2,1)}), bf16[8,32,1024]{2,1,0:T(8,128)(2,1)S(1)}, u32[]{:S(2)}, u32[]{:S(2)}) async-start(bf16[8,32,1024]{2,1,0:T(8,128)(2,1)} %bitcast.15), calls=%async_computation.1 | async-start | bytes 1048576 | tf_op jit(solution)/shard_map/all_to_all | solution.py:18
  80.0 12.2 %collective-permute-start.5 = (bf16[192,1536]{1,0:T(8,128)(2,1)}, bf16[192,1536]{1,0:T(8,128)(2,1)S(1)}, u32[]{:S(2)}, u32[]{:S(2)}) collective-permute-start(bf16[192,1536]{1,0:T(8,128)(2,1)} %bitcast.7.refs_0_), channel_id=1, source_target_pairs={{0,1},{1,0},{2,3},{3,2},{4,5},{5,4},{6,7},{7,6},{8,9},{9,8},{10,11... | collective-permute-start | bytes 1769480 | tf_op jit(solution)/shard_map/ppermute | solution.py:329
  82.9 9.3 %collective-permute-start.7 = (bf16[192,1536]{1,0:T(8,128)(2,1)}, bf16[192,1536]{1,0:T(8,128)(2,1)S(1)}, u32[]{:S(2)}, u32[]{:S(2)}) collective-permute-start(bf16[192,1536]{1,0:T(8,128)(2,1)} %collective-permute-done.6.refs_1_), channel_id=1, source_target_pairs={{0,1},{1,0},{2,3},{3,2},{4,5},{5,4},{6,7},{7,6},{8,9},{9,8},{10,11... | collective-permute-start | bytes 1769480 | tf_op jit(solution)/shard_map/ppermute | solution.py:329
  88.7 14.7 %all-to-all-start.2 = ((bf16[16,2,896]{2,1,0:T(2,128)(2,1)}), bf16[16,2,896]{2,1,0:T(2,128)(2,1)S(1)}, u32[]{:S(2)}, u32[]{:S(2)}) async-start(bf16[16,2,896]{2,1,0:T(2,128)(2,1)} %shard_map.99), calls=%async_computation.2 | async-start | bytes 114688 | tf_op jit(solution)/shard_map/all_to_all | solution.py:18

commit v6 on v5

--- a/solution.py
+++ b/solution.py
@@ -110,6 +110,7 @@
     for fetch in fetches:
         fetch.start()
     lane = lax.broadcasted_iota(jnp.int32, (128, 128), 1)
+    extras = []
     for half in range(2):
         wide = 0
         for y in range(4):
@@ -118,19 +119,22 @@
             wide += a[:, :128] + a[:, 128:256] + a[:, 256:]
         sums = jnp.sum(wide, axis=1, keepdims=True)
         high = sums.astype(jnp.bfloat16).astype(jnp.float32)
-        extra = jnp.where(lane == 0, high, jnp.where(lane == 1, sums - high, 0.0))
-        out[half * 128 : half * 128 + 128, 896:] = extra.astype(jnp.bfloat16)
+        extras.append(jnp.where(lane == 0, high, jnp.where(lane == 1, sums - high, 0.0)))
     for fetch in fetches:
         fetch.wait()
-    total = 0
-    for y in range(4):
-        total += lax.dot_general(
-            rows[:, y].reshape(256, 384),
-            weight[:, y * 384 : y * 384 + 384],
-            NT,
-            preferred_element_type=jnp.float32,
-        )
-    out[:, :896] = total.astype(jnp.bfloat16)
+    for half in range(2):
+        total = 0
+        for y in range(4):
+            total += lax.dot_general(
+                rows[half * 4 : half * 4 + 4, y].reshape(128, 384),
+                weight[:, y * 384 : y * 384 + 384],
+                NT,
+                preferred_element_type=jnp.float32,
+            )
+        for r in range(64):
+            at = slice(2 * r, 2 * r + 2)
+            out[half * 64 + r, :, :896] = total[at].astype(jnp.bfloat16)
+            out[half * 64 + r, :, 896:] = extras[half][at].astype(jnp.bfloat16)
 
 
 def project(place, rows, pieces):
@@ -138,34 +142,13 @@
         project_kernel,
         in_specs=[SMEM, VMEM] + [pl.BlockSpec(memory_space=pl.ANY)] * 4,
         out_specs=VMEM,
-        out_shape=pltpu.HBM((256, 1024), jnp.bfloat16),
+        out_shape=pltpu.HBM((128, 2, 1024), jnp.bfloat16),
         scratch_shapes=[pltpu.VMEM((896, 1536), jnp.bfloat16), pltpu.SemaphoreType.DMA((8,))],
         compiler_params=limit(16),
         cost_estimate=pl.CostEstimate(
             flops=2 * 256 * 1536 * 896, bytes_accessed=4 * 2**20, transcendentals=0
         ),
     )(place, rows, *(in_hbm(piece) for piece in pieces))
-
-
-def add_kernel(parts, out):
-    total = jnp.sum(parts[...].astype(jnp.float32), axis=0)
-    squares = jnp.sum(total[:, 896:], axis=1, keepdims=True)
-    normed = total[:, :896] * lax.rsqrt(squares / D + eps)
-    for r in range(8):
-        out[r] = normed[2 * r : 2 * r + 2].astype(jnp.bfloat16)
-
-
-def add(parts):
-    return pl.pallas_call(
-        add_kernel,
-        grid=(2,),
-        in_specs=[
-            pl.BlockSpec((8, 16, 1024), lambda i: (0, i, 0)),
-        ],
-        out_specs=pl.BlockSpec((8, 2, 896), lambda i: (i, 0, 0)),
-        compiler_params=limit(4),
-        out_shape=pltpu.HBM((16, 2, 896), jnp.bfloat16),
-    )(parts)
 
 
 def attend_kernel(table, lengths, parts, k_pool, v_pool, first, second, new_kv, send, query, mixed, v_held, sem, v_sem):
@@ -184,21 +167,24 @@
         masks.append(mask)
     valid = jnp.where(row == 0, masks[0], masks[1]) == 1
 
+    normed = []
+    for k in range(16):
+        total = jnp.sum(parts[:, k].astype(jnp.float32), axis=0)
+        if k == 0:
+            squares = jnp.sum(total[:, 896:], axis=1, keepdims=True)
+            inv_rms = lax.rsqrt(squares / D + eps)
+        normed.append((total[:, :896] * inv_rms).astype(jnp.bfloat16).astype(jnp.float32))
     for z in range(8):
         zq, zp = z // 2, z % 2
         for y in range(4):
             for k in range(3):
                 at, h = zp * 384 + k * 128, y * 3 + k
-                query[z, 2 * h : 2 * h + 2, :] = parts[zq * 4 + y, :, at : at + 128].astype(
-                    jnp.float32
-                )
+                query[z, 2 * h : 2 * h + 2, :] = normed[zq * 4 + y][:, at : at + 128]
     fresh = []
     for z in range(8):
         at = 768 + (z % 2) * 64
         for y in range(0, 4, 2):
-            pair = [
-                parts[(z // 2) * 4 + y + k, :, at : at + 64].astype(jnp.float32) for k in range(2)
-            ]
+            pair = [normed[(z // 2) * 4 + y + k][:, at : at + 64] for k in range(2)]
             fresh.append(jnp.concatenate(pair, axis=1))
             to = z * 256 + y * 64
             new_kv[:, to : to + 128] = fresh[-1].astype(jnp.bfloat16)
@@ -222,6 +208,7 @@
         weights = (scores / total).astype(jnp.bfloat16)
         found.append((weights, (own / total).astype(jnp.bfloat16).astype(jnp.float32)))
     fetch.wait()
+    copies = []
     for g, (weights, own) in enumerate(found):
         values = v_held[:, :, g * 128 : g * 128 + 128].reshape(768, 128)
         own_value = jnp.where(odd, fresh[8 + g][1:2], fresh[8 + g][0:1])
@@ -231,9 +218,15 @@
         out = out + own * own_value
         for h in range(12):
             mixed[g, :, h * 128 : h * 128 + 128] = out[2 * h : 2 * h + 2].astype(jnp.bfloat16)
-    copies = [pltpu.make_async_copy(mixed, send.at[:, k], sem.at[k]) for k in range(16)]
-    for copy in copies:
-        copy.start()
+        if g % 4 == 3:
+            part = pl.ds(g - 3, 4)
+            for k in range(16):
+                copies.append(
+                    pltpu.make_async_copy(
+                        mixed.at[part], send.at[part, k], sem.at[g // 4 * 16 + k]
+                    )
+                )
+                copies[-1].start()
     for copy in copies:
         copy.wait()
 
@@ -251,7 +244,7 @@
             pltpu.VMEM((8, 24, 128), jnp.float32),
             pltpu.VMEM((8, 2, 1536), jnp.bfloat16),
             pltpu.VMEM((24, 32, 1024), jnp.bfloat16),
-            pltpu.SemaphoreType.DMA((16,)),
+            pltpu.SemaphoreType.DMA((32,)),
             pltpu.SemaphoreType.DMA,
         ],
         compiler_params=limit(16),
@@ -343,8 +336,7 @@
     ]
     rows = a2a(copies(place, *rows, near[:16, :128]), ("zq", "zp", "yh")).reshape(8, 4, 32, 384)
 
-    parts = a2a(project(place, rows, pieces).reshape(8, 32, 1024), G)
-    parts = a2a(add(parts), ("zq", "yh"))
+    parts = a2a(project(place, rows, pieces), G + ("zq", "yh")).reshape(8, 16, 2, 1024)
     first, second = (piece[:16, :128] for piece in o_pieces[2:])
     kv_rows, send = attend(page_table, lengths, parts, k_pool, v_pool, first, second)
 

time: 162 us -> 161 us (level)
  waiting for transfers between devices: 27.6 us -> 21.6 us
  blocking collectives: 49.7 us -> 52.9 us
    all_to_all x3 -> x2, waiting for transfers between devices: 24.2 us -> 16.1 us  [a2a(): return lax.all_to_all(a, axes, split_axis=0, concat_axis=0, tiled=True)]
    all_to_all x2, blocking collectives: 49.7 us -> 52.9 us  [a2a(): return lax.all_to_all(a, axes, split_axis=0, concat_axis=0, tiled=True)]
    ppermute x1, starting transfers between devices: 2.83 us -> 5.05 us  [per_device(): lax.ppermute(o_own, 'c', OTHER)]
    ppermute x1, waiting for transfers between devices: 0.01 us -> 2.16 us  [per_device(): lax.ppermute(o_near, 'c', OTHER)]
    all_to_all x3 -> x2, starting transfers between devices: 40.7 us -> 39.8 us  [a2a(): return lax.all_to_all(a, axes, split_axis=0, concat_axis=0, tiled=True)]
  transfers between devices with their start and end apart: 11 -> 10, of which waited for: 4 -> 4; matrix products, arithmetic and copies ran while one was open for 0% -> 0% of each run, Pallas kernels for 4% -> 4%
where the time goes in v6:
time: 161 us; the launch traced here: 160 us
  starting transfers between devices  67.2 us (42%)
  blocking collectives  52.9 us (33%)
  waiting for transfers between devices  21.6 us (13%)
  Pallas kernels  16.5 us (10%)
    all_to_all x2, blocking collectives, a2a(): return lax.all_to_all(a, axes, split_axis=0, concat_axis=0, tiled=True)  52.9 us
    all_to_all x2, starting transfers between devices, a2a(): return lax.all_to_all(a, axes, split_axis=0, concat_axis=0, tiled=True)  39.8 us
    all_to_all x2, waiting for transfers between devices, a2a(): return lax.all_to_all(a, axes, split_axis=0, concat_axis=0, tiled=True)  16.1 us
    ppermute x2, starting transfers between devices, per_device(): lax.ppermute(part, G + ('zq', 'zp', 'c'), [((g * 8 + z) * 2 + c, (z * 8 +...  6.54 us
    ppermute x1, starting transfers between devices, per_device(): lax.ppermute(o_own, 'c', OTHER)  5.05 us
    pallas_call x1, Pallas kernels, project(): pl.pallas_call(project_kernel, in_specs=[SMEM, VMEM] + [pl.BlockSpec(memo...  4.93 us
    ppermute x1, starting transfers between devices, per_device(): near = lax.ppermute(own, 'zp', OTHER)  4.83 us
    pallas_call x1, Pallas kernels, attend(): pl.pallas_call(attend_kernel, in_specs=[SMEM] * 2 + [VMEM] * 2 + [pl.Bloc...  4.68 us
  transfers between devices with their start and end apart: 10, of which 4 were waited for; matrix products, arithmetic and copies ran while one was open for 0% of the time, Pallas kernels for 4%

profile of v6, /device:TPU:1, one launch (start us, length us, event | category | flops | bytes accessed | tf_op | source)
XLA Modules:
  0.0 160.3 jit_solution(13591084054733455624)
XLA Ops:
  0.6 1.1 shard_map.96.own
  1.8 4.8 %collective-permute-start.2 = (bf16[224,1536]{1,0:T(8,128)(2,1)S(1)}, bf16[224,1536]{1,0:T(8,128)(2,1)S(1)}, u32[]{:S(2)}, u32[]{:S(2)}) collective-permute-start(bf16[224,1536]{1,0:T(8,128)(2,1)S(1)} %shard_map.96.own), channel_id=1, source_target_pairs={{0,8},{8,0},{1,9},{9,1},{2,10},{10,2},{3,11},{11,3},{4,12},{12,4},... | collective-permute-start | bytes 2064392 | tf_op jit(solution)/shard_map/ppermute | solution.py:318
  6.7 1.0 shard_map.95
  7.7 0.7 collective-permute-start
  8.3 5.9 %collective-permute-start.1 = (bf16[64,192]{1,0:T(8,128)(2,1)S(1)}, bf16[64,192]{1,0:T(8,128)(2,1)S(1)}, u32[]{:S(2)}, u32[]{:S(2)}) collective-permute-start(bf16[64,192]{1,0:T(8,128)(2,1)S(1)} %get-tuple-element.7), channel_id=1, source_target_pairs={{0,1},{1,0},{8,65},{9,64},{16,129},{17,128},{24,193},{25,192},{32,... | collective-permute-start | bytes 73736 | tf_op jit(solution)/shard_map/ppermute | solution.py:325
  14.2 3.4 %collective-permute-done.2.near = bf16[224,1536]{1,0:T(8,128)(2,1)S(1)} collective-permute-done((bf16[224,1536]{1,0:T(8,128)(2,1)S(1)}, bf16[224,1536]{1,0:T(8,128)(2,1)S(1)}, u32[]{:S(2)}, u32[]{:S(2)}) %collective-permute-start.2) | collective-permute-done | bytes 688160 | tf_op jit(solution)/shard_map/ppermute | solution.py:318
  17.6 1.6 shard_map.97
  19.2 20.0 %all-to-all-start = ((bf16[32,32,384]{2,1,0:T(8,128)(2,1)}), bf16[32,32,384]{2,1,0:T(8,128)(2,1)S(1)}, u32[]{:S(2)}, u32[]{:S(2)}) async-start(bf16[32,32,384]{2,1,0:T(8,128)(2,1)} %shard_map.97), calls=%async_computation | async-start | bytes 1572864 | tf_op jit(solution)/shard_map/all_to_all | solution.py:18
  39.2 3.7 %collective-permute-start.3 = (bf16[224,1536]{1,0:T(8,128)(2,1)S(1)}, bf16[224,1536]{1,0:T(8,128)(2,1)S(1)}, u32[]{:S(2)}, u32[]{:S(2)}) collective-permute-start(bf16[224,1536]{1,0:T(8,128)(2,1)S(1)} %shard_map.96.own), channel_id=1, source_target_pairs={{0,1},{1,0},{2,3},{3,2},{4,5},{5,4},{6,7},{7,6},{8,9},{9,8},{10,11... | collective-permute-start | bytes 2064392 | tf_op jit(solution)/shard_map/ppermute | solution.py:319
  43.0 1.9 %collective-permute-start.4 = (bf16[224,1536]{1,0:T(8,128)(2,1)S(1)}, bf16[224,1536]{1,0:T(8,128)(2,1)}, u32[]{:S(2)}, u32[]{:S(2)}) collective-permute-start(bf16[224,1536]{1,0:T(8,128)(2,1)S(1)} %collective-permute-done.2.near), channel_id=1, source_target_pairs={{0,1},{1,0},{2,3},{3,2},{4,5},{5,4},{6,7},{7,6},{8,9},{9,8},{10,11... | collective-permute-start | bytes 2064392 | tf_op jit(solution)/shard_map/ppermute | solution.py:319
  44.9 3.4 %collective-permute-start.6 = (bf16[192,1536]{1,0:T(8,128)(2,1)}, bf16[192,1536]{1,0:T(8,128)(2,1)}, u32[]{:S(2)}, u32[]{:S(2)}) collective-permute-start(bf16[192,1536]{1,0:T(8,128)(2,1)} %bitcast.7.refs_0_), channel_id=1, source_target_pairs={{0,8},{8,0},{1,9},{9,1},{2,10},{10,2},{3,11},{11,3},{4,12},{12,4},... | collective-permute-start | bytes 1769480 | tf_op jit(solution)/shard_map/ppermute | solution.py:321
  48.4 10.0 %all-to-all-done = bf16[32,32,384]{2,1,0:T(8,128)(2,1)S(1)} async-done(((bf16[32,32,384]{2,1,0:T(8,128)(2,1)}), bf16[32,32,384]{2,1,0:T(8,128)(2,1)S(1)}, u32[]{:S(2)}, u32[]{:S(2)}) %all-to-all-start) | async-done | bytes 786464 | tf_op jit(solution)/shard_map/all_to_all | solution.py:18
  58.4 4.9 %shard_map.98 = bf16[128,2,1024]{2,1,0:T(2,128)(2,1)} custom-call(s32[2]{0:T(128)S(1)} %pad_add_fusion.place, bf16[8,4,32,384]{3,2,1,0:T(8,128)(2,1)S(1)} %bitcast.12, bf16[224,1536]{1,0:T(8,128)(2,1)} %copy-done, bf16[224,1536]{1,0:T(8,128)(2,1)} %copy-done.6, bf16[224,1536]{1,0:T(8,128)(2,1)} %copy-done.7, bf16[224,1536]{1,0:T(8,128)(2,1)} %collective-permute-done.4.near_other), custom_call_target="tpu_custom_call" | custom-call | flops 704643072 | bytes 4194304 | tf_op jit(solution)/shard_map/pallas_call | solution.py:141
  63.3 19.8 %all-to-all-start.1 = ((bf16[128,2,1024]{2,1,0:T(2,128)(2,1)}), bf16[128,2,1024]{2,1,0:T(2,128)(2,1)S(1)}, u32[]{:S(2)}, u32[]{:S(2)}) async-start(bf16[128,2,1024]{2,1,0:T(2,128)(2,1)} %shard_map.98), calls=%async_computation.1 | async-start | bytes 1048576 | tf_op jit(solution)/shard_map/all_to_all | solution.py:18
  83.1 5.1 %collective-permute-start.5 = (bf16[192,1536]{1,0:T(8,128)(2,1)}, bf16[192,1536]{1,0:T(8,128)(2,1)S(1)}, u32[]{:S(2)}, u32[]{:S(2)}) collective-permute-start(bf16[192,1536]{1,0:T(8,128)(2,1)} %bitcast.7.refs_0_), channel_id=1, source_target_pairs={{0,1},{1,0},{2,3},{3,2},{4,5},{5,4},{6,7},{7,6},{8,9},{9,8},{10,11... | collective-permute-start | bytes 1769480 | tf_op jit(solution)/shard_map/ppermute | solution.py:322
  88.2 1.9 %collective-permute-start.7 = (bf16[192,1536]{1,0:T(8,128)(2,1)}, bf16[192,1536]{1,0:T(8,128)(2,1)S(1)}, u32[]{:S(2)}, u32[]{:S(2)}) collective-permute-start(bf16[192,1536]{1,0:T(8,128)(2,1)} %collective-permute-done.6.refs_1_), channel_id=1, source_target_pairs={{0,1},{1,0},{2,3},{3,2},{4,5},{5,4},{6,7},{7,6},{8,9},{9,8},{10,11... | collective-permute-start | bytes 1769480 | tf_op jit(solution)/shard_map/ppermute | solution.py:322
  90.2 2.2 %collective-permute-done.7.refs_3_ = bf16[192,1536]{1,0:T(8,128)(2,1)S(1)} collective-permute-done((bf16[192,1536]{1,0:T(8,128)(2,1)}, bf16[192,1536]{1,0:T(8,128)(2,1)S(1)}, u32[]{:S(2)}, u32[]{:S(2)}) %collective-permute-start.7) | collective-permute-done | bytes 589856 | tf_op jit(solution)/shard_map/ppermute | solution.py:322
  92.3 0.8 copy-done.2
  93.2 6.1 %all-to-all-done.1 = bf16[128,2,1024]{2,1,0:T(2,128)(2,1)S(1)} async-done(((bf16[128,2,1024]{2,1,0:T(2,128)(2,1)}), bf16[128,2,1024]{2,1,0:T(2,128)(2,1)S(1)}, u32[]{:S(2)}, u32[]{:S(2)}) %all-to-all-start.1) | async-done | bytes 524320 | tf_op jit(solution)/shard_map/all_to_all | solution.py:18
  99.3 4.7 %shard_map.99 = (bf16[2,2048]{1,0:T(2,128)(2,1)}, bf16[8,16,2,1536]{3,2,1,0:T(2,128)(2,1)}) custom-call(s32[2,12]{1,0:T(2,128)S(1)} %copy-done.4, s32[2]{0:T(128)S(1)} %copy-done.5, bf16[8,16,2,1024]{3,2,1,0:T(2,128)(2,1)S(1)} %bitcast.13, bf16[24,32,1024]{2,1,0:T(8,128)(2,1)S(1)} %copy-done.1, bf16[24,32,1024]{2,1,0:T(8,128)(2,1)} %v_pool.1, ...), custom_call_target="tpu_custom_call" | custom-call | tf_op jit(solution)/shard_map/pallas_call | solution.py:235
  104.0 31.4 %all_to_all.20 = bf16[128,2,1536]{2,1,0:T(2,128)(2,1)S(1)} all-to-all(bf16[128,2,1536]{2,1,0:T(2,128)(2,1)} %bitcast.16), channel_id=1, replica_groups=mesh['yl'=2,'x'=4,'zq'=4,'zp'=2,'yh'=4,'c'=2] {'yl','x','zq','yh'}, dimensions={0} | all-to-all | bytes 1572864 | tf_op jit(solution)/shard_map/all_to_all | solution.py:18
  135.7 2.3 %shard_map.100 = bf16[8,4,48,128]{3,2,1,0:T(8,128)(2,1)S(1)} custom-call(s32[2]{0:T(128)S(1)} %pad_add_fusion.place, bf16[256,1536]{1,0:T(8,128)(2,1)S(1)} %reshape.25.rows, bf16[192,1536]{1,0:T(8,128)(2,1)} %bitcast.7.refs_0_, bf16[192,1536]{1,0:T(8,128)(2,1)} %collective-permute-done.6.refs_1_, bf16[192,1536]{1,0:T(8,128)(2,1)S(1)} %collective-permute-done.5.refs_2_, ...), custom_call_target="tpu_custom_call" | custom-call | flops 603979776 | bytes 4194304 | tf_op jit(solution)/shard_map/pallas_call | solution.py:272
  138.0 21.4 %all_to_all.21 = bf16[32,48,128]{2,1,0:T(8,128)(2,1)S(1)} all-to-all(bf16[32,48,128]{2,1,0:T(8,128)(2,1)S(1)} %bitcast.15), channel_id=1, replica_groups=mesh['yl'=2,'x'=4,'zq'=4,'zp'=2,'yh'=4,'c'=2] {'yl','x','zp','c'}, dimensions={0} | all-to-all | bytes 786432 | tf_op jit(solution)/shard_map/all_to_all | solution.py:18
  159.5 0.9 shard_map.101
  (26 shorter events, 0.4 us)
Async XLA Ops:
  1.7 56.6 %copy-start = (bf16[224,1536]{1,0:T(8,128)(2,1)}, bf16[224,1536]{1,0:T(8,128)(2,1)S(1)}, u32[]{:S(2)}) copy-start(bf16[224,1536]{1,0:T(8,128)(2,1)S(1)} %shard_map.96.own) | copy-start | bytes 2064388
  1.8 15.9 %collective-permute-start.2 = (bf16[224,1536]{1,0:T(8,128)(2,1)S(1)}, bf16[224,1536]{1,0:T(8,128)(2,1)S(1)}, u32[]{:S(2)}, u32[]{:S(2)}) collective-permute-start(bf16[224,1536]{1,0:T(8,128)(2,1)S(1)} %shard_map.96.own), channel_id=1, source_target_pairs={{0,8},{8,0},{1,9},{9,1},{2,10},{10,2},{3,11},{11,3},{4,12},{12,4},... | collective-permute-start | bytes 2064392 | tf_op jit(solution)/shard_map/ppermute | solution.py:318
  7.7 10.0 %collective-permute-start = (bf16[64,192]{1,0:T(8,128)(2,1)S(1)}, bf16[64,192]{1,0:T(8,128)(2,1)S(1)}, u32[]{:S(2)}, u32[]{:S(2)}) collective-permute-start(bf16[64,192]{1,0:T(8,128)(2,1)S(1)} %get-tuple-element.6), channel_id=1, source_target_pairs={{0,0},{1,1},{8,64},{9,65},{16,128},{17,129},{24,192},{25,193},{32,... | collective-permute-start | bytes 73736 | tf_op jit(solution)/shard_map/ppermute | solution.py:325
  8.3 9.3 %collective-permute-start.1 = (bf16[64,192]{1,0:T(8,128)(2,1)S(1)}, bf16[64,192]{1,0:T(8,128)(2,1)S(1)}, u32[]{:S(2)}, u32[]{:S(2)}) collective-permute-start(bf16[64,192]{1,0:T(8,128)(2,1)S(1)} %get-tuple-element.7), channel_id=1, source_target_pairs={{0,1},{1,0},{8,65},{9,64},{16,129},{17,128},{24,193},{25,192},{32,... | collective-permute-start | bytes 73736 | tf_op jit(solution)/shard_map/ppermute | solution.py:325
  17.6 40.8 %copy-start.6 = (bf16[224,1536]{1,0:T(8,128)(2,1)}, bf16[224,1536]{1,0:T(8,128)(2,1)S(1)}, u32[]{:S(2)}) copy-start(bf16[224,1536]{1,0:T(8,128)(2,1)S(1)} %collective-permute-done.2.near) | copy-start | bytes 2064388
  19.2 39.2 %all-to-all-start = ((bf16[32,32,384]{2,1,0:T(8,128)(2,1)}), bf16[32,32,384]{2,1,0:T(8,128)(2,1)S(1)}, u32[]{:S(2)}, u32[]{:S(2)}) async-start(bf16[32,32,384]{2,1,0:T(8,128)(2,1)} %shard_map.97), calls=%async_computation | async-start | bytes 1572864 | tf_op jit(solution)/shard_map/all_to_all | solution.py:18
  39.2 9.1 %collective-permute-start.3 = (bf16[224,1536]{1,0:T(8,128)(2,1)S(1)}, bf16[224,1536]{1,0:T(8,128)(2,1)S(1)}, u32[]{:S(2)}, u32[]{:S(2)}) collective-permute-start(bf16[224,1536]{1,0:T(8,128)(2,1)S(1)} %shard_map.96.own), channel_id=1, source_target_pairs={{0,1},{1,0},{2,3},{3,2},{4,5},{5,4},{6,7},{7,6},{8,9},{9,8},{10,11... | collective-permute-start | bytes 2064392 | tf_op jit(solution)/shard_map/ppermute | solution.py:319
  43.0 5.4 %collective-permute-start.4 = (bf16[224,1536]{1,0:T(8,128)(2,1)S(1)}, bf16[224,1536]{1,0:T(8,128)(2,1)}, u32[]{:S(2)}, u32[]{:S(2)}) collective-permute-start(bf16[224,1536]{1,0:T(8,128)(2,1)S(1)} %collective-permute-done.2.near), channel_id=1, source_target_pairs={{0,1},{1,0},{2,3},{3,2},{4,5},{5,4},{6,7},{7,6},{8,9},{9,8},{10,11... | collective-permute-start | bytes 2064392 | tf_op jit(solution)/shard_map/ppermute | solution.py:319
  44.9 43.3 %collective-permute-start.6 = (bf16[192,1536]{1,0:T(8,128)(2,1)}, bf16[192,1536]{1,0:T(8,128)(2,1)}, u32[]{:S(2)}, u32[]{:S(2)}) collective-permute-start(bf16[192,1536]{1,0:T(8,128)(2,1)} %bitcast.7.refs_0_), channel_id=1, source_target_pairs={{0,8},{8,0},{1,9},{9,1},{2,10},{10,2},{3,11},{11,3},{4,12},{12,4},... | collective-permute-start | bytes 1769480 | tf_op jit(solution)/shard_map/ppermute | solution.py:321
  48.3 10.0 %copy-start.7 = (bf16[224,1536]{1,0:T(8,128)(2,1)}, bf16[224,1536]{1,0:T(8,128)(2,1)S(1)}, u32[]{:S(2)}) copy-start(bf16[224,1536]{1,0:T(8,128)(2,1)S(1)} %collective-permute-done.3.own_other) | copy-start | bytes 2064388
  58.4 40.9 %copy-start.1 = (bf16[24,32,1024]{2,1,0:T(8,128)(2,1)S(1)}, bf16[24,32,1024]{2,1,0:T(8,128)(2,1)}, u32[]{:S(2)}) copy-start(bf16[24,32,1024]{2,1,0:T(8,128)(2,1)} %k_pool.1) | copy-start | bytes 4718596
  58.4 40.9 %copy-start.4 = (s32[2,12]{1,0:T(2,128)S(1)}, s32[2,12]{1,0:T(2,128)}, u32[]{:S(2)}) copy-start(s32[2,12]{1,0:T(2,128)} %table.1) | copy-start | bytes 292
  58.4 40.9 %copy-start.5 = (s32[2]{0:T(128)S(1)}, s32[2]{0:T(128)}, u32[]{:S(2)}) copy-start(s32[2]{0:T(128)} %lengths.1) | copy-start | bytes 28
  63.3 35.9 %all-to-all-start.1 = ((bf16[128,2,1024]{2,1,0:T(2,128)(2,1)}), bf16[128,2,1024]{2,1,0:T(2,128)(2,1)S(1)}, u32[]{:S(2)}, u32[]{:S(2)}) async-start(bf16[128,2,1024]{2,1,0:T(2,128)(2,1)} %shard_map.98), calls=%async_computation.1 | async-start | bytes 1048576 | tf_op jit(solution)/shard_map/all_to_all | solution.py:18
  83.1 7.0 %collective-permute-start.5 = (bf16[192,1536]{1,0:T(8,128)(2,1)}, bf16[192,1536]{1,0:T(8,128)(2,1)S(1)}, u32[]{:S(2)}, u32[]{:S(2)}) collective-permute-start(bf16[192,1536]{1,0:T(8,128)(2,1)} %bitcast.7.refs_0_), channel_id=1, source_target_pairs={{0,1},{1,0},{2,3},{3,2},{4,5},{5,4},{6,7},{7,6},{8,9},{9,8},{10,11... | collective-permute-start | bytes 1769480 | tf_op jit(solution)/shard_map/ppermute | solution.py:322
  88.2 4.1 %collective-permute-start.7 = (bf16[192,1536]{1,0:T(8,128)(2,1)}, bf16[192,1536]{1,0:T(8,128)(2,1)S(1)}, u32[]{:S(2)}, u32[]{:S(2)}) collective-permute-start(bf16[192,1536]{1,0:T(8,128)(2,1)} %collective-permute-done.6.refs_1_), channel_id=1, source_target_pairs={{0,1},{1,0},{2,3},{3,2},{4,5},{5,4},{6,7},{7,6},{8,9},{9,8},{10,11... | collective-permute-start | bytes 1769480 | tf_op jit(solution)/shard_map/ppermute | solution.py:322
  92.3 0.8 copy-start.2
  103.9 31.7 %copy-start.3 = (bf16[192,1536]{1,0:T(8,128)(2,1)S(1)}, bf16[192,1536]{1,0:T(8,128)(2,1)}, u32[]{:S(2)}) copy-start(bf16[192,1536]{1,0:T(8,128)(2,1)} %copy-done.2) | copy-start | bytes 1769476

commit v7 on v6

--- a/solution.py
+++ b/solution.py
@@ -52,8 +52,8 @@
     )(place, in_hbm(hidden))
 
 
-def copies_kernel(place, own, other, touch, out):
-    del touch
+def copies_kernel(place, own, other, first, second, out):
+    del first, second
     flip = place[1] == 1
     first = jnp.where(flip, other[...], own[...])
     second = jnp.where(flip, own[...], other[...])
@@ -64,51 +64,37 @@
                 out[zq * 8 + zp * 4 + y] = both[zp * 32 : zp * 32 + 32]
 
 
-def copies(place, own, other, touch):
+def copies(place, own, other, first, second):
     return pl.pallas_call(
         copies_kernel,
-        in_specs=[SMEM] + [VMEM] * 3,
+        in_specs=[SMEM] + [VMEM] * 4,
         out_specs=VMEM,
         compiler_params=limit(4),
         out_shape=pltpu.HBM((32, 32, 384), jnp.bfloat16),
-    )(place, own, other, touch)
-
-
-def join_kernel(q, kv, out):
-    out[:192] = q[...]
-    out[192:] = kv[...]
-
-
-def join(q, kv):
-    return pl.pallas_call(
-        join_kernel,
-        in_specs=[VMEM] * 2,
-        out_specs=VMEM,
-        compiler_params=limit(4),
-        out_shape=jax.ShapeDtypeStruct((224, 1536), jnp.bfloat16),
-    )(in_hbm(q), in_hbm(kv))
-
-
-def project_kernel(place, rows, own, near, own_other, near_other, out, weight, sem):
+    )(place, own, other, first, second)
+
+
+def project_kernel(place, rows, *refs):
     zp, core = place[0], place[1]
+    out, weight, sem = refs[8:]
     fetches = []
-    for k, (piece, z, c) in enumerate(
-        (
-            (own, zp, core),
-            (near, 1 - zp, core),
-            (own_other, zp, 1 - core),
-            (near_other, 1 - zp, 1 - core),
-        )
-    ):
-        at = z * 2 + c
-        q_rows = pl.ds(pl.multiple_of(at * 192, 64), 192)
-        kv_rows = pl.ds(pl.multiple_of(768 + at * 32, 32), 32)
-        fetches.append(pltpu.make_async_copy(piece.at[:192], weight.at[q_rows], sem.at[2 * k]))
-        fetches.append(
-            pltpu.make_async_copy(piece.at[192:], weight.at[kv_rows], sem.at[2 * k + 1])
-        )
-    for fetch in fetches:
-        fetch.start()
+    for y in range(4):
+        part = slice(y * 384, y * 384 + 384)
+        for k, (z, c) in enumerate(
+            ((zp, core), (1 - zp, core), (zp, 1 - core), (1 - zp, 1 - core))
+        ):
+            at = z * 2 + c
+            q_rows = pl.ds(pl.multiple_of(at * 192, 64), 192)
+            kv_rows = pl.ds(pl.multiple_of(768 + at * 32, 32), 32)
+            for j, to in enumerate((q_rows, kv_rows)):
+                fetches.append(
+                    pltpu.make_async_copy(
+                        refs[2 * k + j].at[:, part],
+                        weight.at[to, part],
+                        sem.at[y * 8 + 2 * k + j],
+                    )
+                )
+                fetches[-1].start()
     lane = lax.broadcasted_iota(jnp.int32, (128, 128), 1)
     extras = []
     for half in range(2):
@@ -120,30 +106,31 @@
         sums = jnp.sum(wide, axis=1, keepdims=True)
         high = sums.astype(jnp.bfloat16).astype(jnp.float32)
         extras.append(jnp.where(lane == 0, high, jnp.where(lane == 1, sums - high, 0.0)))
-    for fetch in fetches:
-        fetch.wait()
-    for half in range(2):
-        total = 0
-        for y in range(4):
-            total += lax.dot_general(
+    total = [0, 0]
+    for y in range(4):
+        for fetch in fetches[y * 8 : y * 8 + 8]:
+            fetch.wait()
+        for half in range(2):
+            total[half] += lax.dot_general(
                 rows[half * 4 : half * 4 + 4, y].reshape(128, 384),
                 weight[:, y * 384 : y * 384 + 384],
                 NT,
                 preferred_element_type=jnp.float32,
             )
+    for half in range(2):
         for r in range(64):
             at = slice(2 * r, 2 * r + 2)
-            out[half * 64 + r, :, :896] = total[at].astype(jnp.bfloat16)
+            out[half * 64 + r, :, :896] = total[half][at].astype(jnp.bfloat16)
             out[half * 64 + r, :, 896:] = extras[half][at].astype(jnp.bfloat16)
 
 
 def project(place, rows, pieces):
     return pl.pallas_call(
         project_kernel,
-        in_specs=[SMEM, VMEM] + [pl.BlockSpec(memory_space=pl.ANY)] * 4,
+        in_specs=[SMEM, VMEM] + [pl.BlockSpec(memory_space=pl.ANY)] * 8,
         out_specs=VMEM,
         out_shape=pltpu.HBM((128, 2, 1024), jnp.bfloat16),
-        scratch_shapes=[pltpu.VMEM((896, 1536), jnp.bfloat16), pltpu.SemaphoreType.DMA((8,))],
+        scratch_shapes=[pltpu.VMEM((896, 1536), jnp.bfloat16), pltpu.SemaphoreType.DMA((32,))],
         compiler_params=limit(16),
         cost_estimate=pl.CostEstimate(
             flops=2 * 256 * 1536 * 896, bytes_accessed=4 * 2**20, transcendentals=0
@@ -314,9 +301,9 @@
     place = jnp.stack([lax.axis_index("zp"), lax.axis_index("c")])
     place = place.astype(jnp.int32)
 
-    own = join(q_weight.T, kv_weight.T)
-    near = lax.ppermute(own, "zp", OTHER)
-    pieces = (own, near, lax.ppermute(own, "c", OTHER), lax.ppermute(near, "c", OTHER))
+    own = (q_weight.T, kv_weight.T)
+    near = [lax.ppermute(part, "zp", OTHER) for part in own]
+    pieces = (*own, *near, *(lax.ppermute(part, "c", OTHER) for part in (*own, *near)))
     o_own = o_weight.T
     o_near = lax.ppermute(o_own, "zp", OTHER)
     o_pieces = (o_own, o_near, lax.ppermute(o_own, "c", OTHER), lax.ppermute(o_near, "c", OTHER))
@@ -334,7 +321,7 @@
         )
         for flip, part in enumerate(split(place, hidden.T))
     ]
-    rows = a2a(copies(place, *rows, near[:16, :128]), ("zq", "zp", "yh")).reshape(8, 4, 32, 384)
+    rows = a2a(copies(place, *rows, near[0][:16, :128], near[1][:16, :128]), ("zq", "zp", "yh")).reshape(8, 4, 32, 384)
 
     parts = a2a(project(place, rows, pieces), G + ("zq", "yh")).reshape(8, 16, 2, 1024)
     first, second = (piece[:16, :128] for piece in o_pieces[2:])

time: 161 us -> 160 us (level)
  starting transfers between devices: 67.2 us -> 71.3 us
  waiting for transfers between devices: 21.6 us -> 18.7 us
    ppermute x3 -> x6, starting transfers between devices: 10.5 us -> 15.8 us  [the longest x4 8.87 us: per_device(): lax.ppermute(part, 'c', OTHER)]
    ppermute x3 -> x6, waiting for transfers between devices: 3.39 us -> 0.02 us  [the longest x4 0.01 us: per_device(): lax.ppermute(part, 'c', OTHER)]
    all_to_all x2, starting transfers between devices: 39.8 us -> 36.6 us  [a2a(): return lax.all_to_all(a, axes, split_axis=0, concat_axis=0, tiled=True)]
    ppermute x2, starting transfers between devices: 6.54 us -> 8.54 us  [per_device(): lax.ppermute(part, G + ('zq', 'zp', 'c'), [((g * 8 + z) * 2 + c, (z * 8 +...]
  transfers between devices with their start and end apart: 10 -> 13, of which waited for: 4 -> 4; matrix products, arithmetic and copies ran while one was open for 0% -> 0% of each run, Pallas kernels for 4% -> 4%
where the time goes in v7:
time: 160 us; the launch traced here: 159 us
  starting transfers between devices  71.3 us (45%)
  blocking collectives  52.2 us (33%)
  waiting for transfers between devices  18.7 us (12%)
  Pallas kernels  15.6 us (10%)
    all_to_all x2, blocking collectives, a2a(): return lax.all_to_all(a, axes, split_axis=0, concat_axis=0, tiled=True)  52.2 us
    all_to_all x2, starting transfers between devices, a2a(): return lax.all_to_all(a, axes, split_axis=0, concat_axis=0, tiled=True)  36.6 us
    all_to_all x2, waiting for transfers between devices, a2a(): return lax.all_to_all(a, axes, split_axis=0, concat_axis=0, tiled=True)  15.7 us
    ppermute x4, starting transfers between devices, per_device(): lax.ppermute(part, 'c', OTHER)  8.87 us
    ppermute x2, starting transfers between devices, per_device(): lax.ppermute(part, G + ('zq', 'zp', 'c'), [((g * 8 + z) * 2 + c, (z * 8 +...  8.54 us
    ppermute x2, starting transfers between devices, per_device(): near = [lax.ppermute(part, 'zp', OTHER) for part in own]  6.89 us
    pallas_call x1, Pallas kernels, project(): pl.pallas_call(project_kernel, in_specs=[SMEM, VMEM] + [pl.BlockSpec(memo...  5.13 us
    ppermute x1, starting transfers between devices, per_device(): lax.ppermute(o_own, 'c', OTHER)  5.01 us
  transfers between devices with their start and end apart: 13, of which 4 were waited for; matrix products, arithmetic and copies ran while one was open for 0% of the time, Pallas kernels for 4%

profile of v7, /device:TPU:1, one launch (start us, length us, event | category | flops | bytes accessed | tf_op | source)
XLA Modules:
  0.0 159.2 jit_solution(7510510490464831779)
XLA Ops:
  0.7 5.0 %collective-permute-start.2 = (bf16[192,1536]{1,0:T(8,128)(2,1)}, bf16[192,1536]{1,0:T(8,128)(2,1)S(1)}, u32[]{:S(2)}, u32[]{:S(2)}) collective-permute-start(bf16[192,1536]{1,0:T(8,128)(2,1)} %bitcast.17), channel_id=1, source_target_pairs={{0,8},{8,0},{1,9},{9,1},{2,10},{10,2},{3,11},{11,3},{4,12},{12,4},... | collective-permute-start | bytes 1769480 | tf_op jit(solution)/shard_map/ppermute | solution.py:305
  5.6 1.9 %collective-permute-start.3 = (bf16[32,1536]{1,0:T(8,128)(2,1)}, bf16[32,1536]{1,0:T(8,128)(2,1)S(1)}, u32[]{:S(2)}, u32[]{:S(2)}) collective-permute-start(bf16[32,1536]{1,0:T(8,128)(2,1)} %bitcast.20), channel_id=1, source_target_pairs={{0,8},{8,0},{1,9},{9,1},{2,10},{10,2},{3,11},{11,3},{4,12},{12,4},... | collective-permute-start | bytes 294920 | tf_op jit(solution)/shard_map/ppermute | solution.py:305
  7.6 1.0 shard_map.95
  9.3 7.9 %collective-permute-start.1 = (bf16[64,192]{1,0:T(8,128)(2,1)S(1)}, bf16[64,192]{1,0:T(8,128)(2,1)S(1)}, u32[]{:S(2)}, u32[]{:S(2)}) collective-permute-start(bf16[64,192]{1,0:T(8,128)(2,1)S(1)} %get-tuple-element.7), channel_id=1, source_target_pairs={{0,1},{1,0},{8,65},{9,64},{16,129},{17,128},{24,193},{25,192},{32,... | collective-permute-start | bytes 73736 | tf_op jit(solution)/shard_map/ppermute | solution.py:312
  17.3 0.8 collective-permute-done.1.other
  18.0 1.6 shard_map.96
  19.6 20.0 %all-to-all-start = ((bf16[32,32,384]{2,1,0:T(8,128)(2,1)}), bf16[32,32,384]{2,1,0:T(8,128)(2,1)S(1)}, u32[]{:S(2)}, u32[]{:S(2)}) async-start(bf16[32,32,384]{2,1,0:T(8,128)(2,1)} %shard_map.96), calls=%async_computation | async-start | bytes 1572864 | tf_op jit(solution)/shard_map/all_to_all | solution.py:18
  39.6 2.6 %collective-permute-start.4 = (bf16[192,1536]{1,0:T(8,128)(2,1)S(1)}, bf16[192,1536]{1,0:T(8,128)(2,1)S(1)}, u32[]{:S(2)}, u32[]{:S(2)}) collective-permute-start(bf16[192,1536]{1,0:T(8,128)(2,1)S(1)} %bitcast.19), channel_id=1, source_target_pairs={{0,1},{1,0},{2,3},{3,2},{4,5},{5,4},{6,7},{7,6},{8,9},{9,8},{10,11... | collective-permute-start | bytes 1769480 | tf_op jit(solution)/shard_map/ppermute | solution.py:306
  42.2 1.9 %collective-permute-start.6 = (bf16[192,1536]{1,0:T(8,128)(2,1)S(1)}, bf16[192,1536]{1,0:T(8,128)(2,1)S(1)}, u32[]{:S(2)}, u32[]{:S(2)}) collective-permute-start(bf16[192,1536]{1,0:T(8,128)(2,1)S(1)} %collective-permute-done.2.refs_2_), channel_id=1, source_target_pairs={{0,1},{1,0},{2,3},{3,2},{4,5},{5,4},{6,7},{7,6},{8,9},{9,8},{10,11... | collective-permute-start | bytes 1769480 | tf_op jit(solution)/shard_map/ppermute | solution.py:306
  44.2 2.4 %collective-permute-start.5 = (bf16[32,1536]{1,0:T(8,128)(2,1)S(1)}, bf16[32,1536]{1,0:T(8,128)(2,1)S(1)}, u32[]{:S(2)}, u32[]{:S(2)}) collective-permute-start(bf16[32,1536]{1,0:T(8,128)(2,1)S(1)} %bitcast.22), channel_id=1, source_target_pairs={{0,1},{1,0},{2,3},{3,2},{4,5},{5,4},{6,7},{7,6},{8,9},{9,8},{10,11... | collective-permute-start | bytes 294920 | tf_op jit(solution)/shard_map/ppermute | solution.py:306
  46.6 1.9 %collective-permute-start.7 = (bf16[32,1536]{1,0:T(8,128)(2,1)S(1)}, bf16[32,1536]{1,0:T(8,128)(2,1)S(1)}, u32[]{:S(2)}, u32[]{:S(2)}) collective-permute-start(bf16[32,1536]{1,0:T(8,128)(2,1)S(1)} %collective-permute-done.3.refs_3_), channel_id=1, source_target_pairs={{0,1},{1,0},{2,3},{3,2},{4,5},{5,4},{6,7},{7,6},{8,9},{9,8},{10,11... | collective-permute-start | bytes 294920 | tf_op jit(solution)/shard_map/ppermute | solution.py:306
  48.5 3.4 %collective-permute-start.9 = (bf16[192,1536]{1,0:T(8,128)(2,1)}, bf16[192,1536]{1,0:T(8,128)(2,1)}, u32[]{:S(2)}, u32[]{:S(2)}) collective-permute-start(bf16[192,1536]{1,0:T(8,128)(2,1)} %bitcast.7.refs_0_), channel_id=1, source_target_pairs={{0,8},{8,0},{1,9},{9,1},{2,10},{10,2},{3,11},{11,3},{4,12},{12,4},... | collective-permute-start | bytes 1769480 | tf_op jit(solution)/shard_map/ppermute | solution.py:308
  52.0 8.8 %all-to-all-done = bf16[32,32,384]{2,1,0:T(8,128)(2,1)S(1)} async-done(((bf16[32,32,384]{2,1,0:T(8,128)(2,1)}), bf16[32,32,384]{2,1,0:T(8,128)(2,1)S(1)}, u32[]{:S(2)}, u32[]{:S(2)}) %all-to-all-start) | async-done | bytes 786464 | tf_op jit(solution)/shard_map/all_to_all | solution.py:18
  60.9 5.1 %shard_map.97 = bf16[128,2,1024]{2,1,0:T(2,128)(2,1)} custom-call(s32[2]{0:T(128)S(1)} %pad_add_fusion.place, bf16[8,4,32,384]{3,2,1,0:T(8,128)(2,1)S(1)} %bitcast.12, bf16[192,1536]{1,0:T(8,128)(2,1)} %bitcast.18, bf16[32,1536]{1,0:T(8,128)(2,1)} %bitcast.21, bf16[192,1536]{1,0:T(8,128)(2,1)} %copy-done.3, bf16[32,1536]{1,0:T(8,128)(2,1)} %copy-done.7, ...), custom_call_target="tpu_custom_call" | custom-call | flops 704643072 | bytes 4194304 | tf_op jit(solution)/shard_map/pallas_call | solution.py:128
  66.0 16.6 %all-to-all-start.1 = ((bf16[128,2,1024]{2,1,0:T(2,128)(2,1)}), bf16[128,2,1024]{2,1,0:T(2,128)(2,1)S(1)}, u32[]{:S(2)}, u32[]{:S(2)}) async-start(bf16[128,2,1024]{2,1,0:T(2,128)(2,1)} %shard_map.97), calls=%async_computation.1 | async-start | bytes 1048576 | tf_op jit(solution)/shard_map/all_to_all | solution.py:18
  82.7 5.0 %collective-permute-start.8 = (bf16[192,1536]{1,0:T(8,128)(2,1)}, bf16[192,1536]{1,0:T(8,128)(2,1)S(1)}, u32[]{:S(2)}, u32[]{:S(2)}) collective-permute-start(bf16[192,1536]{1,0:T(8,128)(2,1)} %bitcast.7.refs_0_), channel_id=1, source_target_pairs={{0,1},{1,0},{2,3},{3,2},{4,5},{5,4},{6,7},{7,6},{8,9},{9,8},{10,11... | collective-permute-start | bytes 1769480 | tf_op jit(solution)/shard_map/ppermute | solution.py:309
  87.7 1.9 %collective-permute-start.10 = (bf16[192,1536]{1,0:T(8,128)(2,1)}, bf16[192,1536]{1,0:T(8,128)(2,1)S(1)}, u32[]{:S(2)}, u32[]{:S(2)}) collective-permute-start(bf16[192,1536]{1,0:T(8,128)(2,1)} %collective-permute-done.9.refs_1_), channel_id=1, source_target_pairs={{0,1},{1,0},{2,3},{3,2},{4,5},{5,4},{6,7},{7,6},{8,9},{9,8},{10,11... | collective-permute-start | bytes 1769480 | tf_op jit(solution)/shard_map/ppermute | solution.py:309
  89.6 2.2 %collective-permute-done.10.refs_3_ = bf16[192,1536]{1,0:T(8,128)(2,1)S(1)} collective-permute-done((bf16[192,1536]{1,0:T(8,128)(2,1)}, bf16[192,1536]{1,0:T(8,128)(2,1)S(1)}, u32[]{:S(2)}, u32[]{:S(2)}) %collective-permute-start.10) | collective-permute-done | bytes 589856 | tf_op jit(solution)/shard_map/ppermute | solution.py:309
  91.8 6.9 %all-to-all-done.1 = bf16[128,2,1024]{2,1,0:T(2,128)(2,1)S(1)} async-done(((bf16[128,2,1024]{2,1,0:T(2,128)(2,1)}), bf16[128,2,1024]{2,1,0:T(2,128)(2,1)S(1)}, u32[]{:S(2)}, u32[]{:S(2)}) %all-to-all-start.1) | async-done | bytes 524320 | tf_op jit(solution)/shard_map/all_to_all | solution.py:18
  98.8 4.7 %shard_map.98 = (bf16[2,2048]{1,0:T(2,128)(2,1)}, bf16[8,16,2,1536]{3,2,1,0:T(2,128)(2,1)}) custom-call(s32[2,12]{1,0:T(2,128)S(1)} %copy-done.1, s32[2]{0:T(128)S(1)} %copy-done.2, bf16[8,16,2,1024]{3,2,1,0:T(2,128)(2,1)S(1)} %bitcast.13, bf16[24,32,1024]{2,1,0:T(8,128)(2,1)S(1)} %copy-done, bf16[24,32,1024]{2,1,0:T(8,128)(2,1)} %v_pool.1, ...), custom_call_target="tpu_custom_call" | custom-call | tf_op jit(solution)/shard_map/pallas_call | solution.py:222
  103.5 31.2 %all_to_all.20 = bf16[128,2,1536]{2,1,0:T(2,128)(2,1)S(1)} all-to-all(bf16[128,2,1536]{2,1,0:T(2,128)(2,1)} %bitcast.16), channel_id=1, replica_groups=mesh['yl'=2,'x'=4,'zq'=4,'zp'=2,'yh'=4,'c'=2] {'yl','x','zq','yh'}, dimensions={0} | all-to-all | bytes 1572864 | tf_op jit(solution)/shard_map/all_to_all | solution.py:18
  135.0 2.3 %shard_map.99 = bf16[8,4,48,128]{3,2,1,0:T(8,128)(2,1)S(1)} custom-call(s32[2]{0:T(128)S(1)} %pad_add_fusion.place, bf16[256,1536]{1,0:T(8,128)(2,1)S(1)} %reshape.25.rows, bf16[192,1536]{1,0:T(8,128)(2,1)} %bitcast.7.refs_0_, bf16[192,1536]{1,0:T(8,128)(2,1)} %collective-permute-done.9.refs_1_, bf16[192,1536]{1,0:T(8,128)(2,1)S(1)} %collective-permute-done.8.refs_2_, ...), custom_call_target="tpu_custom_call" | custom-call | flops 603979776 | bytes 4194304 | tf_op jit(solution)/shard_map/pallas_call | solution.py:259
  137.3 21.0 %all_to_all.21 = bf16[32,48,128]{2,1,0:T(8,128)(2,1)S(1)} all-to-all(bf16[32,48,128]{2,1,0:T(8,128)(2,1)S(1)} %bitcast.15), channel_id=1, replica_groups=mesh['yl'=2,'x'=4,'zq'=4,'zp'=2,'yh'=4,'c'=2] {'yl','x','zp','c'}, dimensions={0} | all-to-all | bytes 786432 | tf_op jit(solution)/shard_map/all_to_all | solution.py:18
  158.3 0.9 shard_map.100
  (38 shorter events, 1.1 us)
Async XLA Ops:
  0.6 39.0 %copy-start.4 = (bf16[1536,192]{0,1:T(8,128)(2,1)S(1)}, bf16[1536,192]{0,1:T(8,128)(2,1)}, u32[]{:S(2)}) copy-start(bf16[1536,192]{0,1:T(8,128)(2,1)} %param.9) | copy-start | bytes 1769476
  0.6 43.5 %copy-start.8 = (bf16[1536,32]{0,1:T(8,128)(2,1)S(1)}, bf16[1536,32]{0,1:T(8,128)(2,1)}, u32[]{:S(2)}) copy-start(bf16[1536,32]{0,1:T(8,128)(2,1)} %param.10) | copy-start | bytes 294916
  0.7 16.6 %collective-permute-start.2 = (bf16[192,1536]{1,0:T(8,128)(2,1)}, bf16[192,1536]{1,0:T(8,128)(2,1)S(1)}, u32[]{:S(2)}, u32[]{:S(2)}) collective-permute-start(bf16[192,1536]{1,0:T(8,128)(2,1)} %bitcast.17), channel_id=1, source_target_pairs={{0,8},{8,0},{1,9},{9,1},{2,10},{10,2},{3,11},{11,3},{4,12},{12,4},... | collective-permute-start | bytes 1769480 | tf_op jit(solution)/shard_map/ppermute | solution.py:305
  5.6 11.6 %collective-permute-start.3 = (bf16[32,1536]{1,0:T(8,128)(2,1)}, bf16[32,1536]{1,0:T(8,128)(2,1)S(1)}, u32[]{:S(2)}, u32[]{:S(2)}) collective-permute-start(bf16[32,1536]{1,0:T(8,128)(2,1)} %bitcast.20), channel_id=1, source_target_pairs={{0,8},{8,0},{1,9},{9,1},{2,10},{10,2},{3,11},{11,3},{4,12},{12,4},... | collective-permute-start | bytes 294920 | tf_op jit(solution)/shard_map/ppermute | solution.py:305
  8.6 8.6 %collective-permute-start = (bf16[64,192]{1,0:T(8,128)(2,1)S(1)}, bf16[64,192]{1,0:T(8,128)(2,1)S(1)}, u32[]{:S(2)}, u32[]{:S(2)}) collective-permute-start(bf16[64,192]{1,0:T(8,128)(2,1)S(1)} %get-tuple-element.6), channel_id=1, source_target_pairs={{0,0},{1,1},{8,64},{9,65},{16,128},{17,129},{24,192},{25,193},{32,... | collective-permute-start | bytes 73736 | tf_op jit(solution)/shard_map/ppermute | solution.py:312
  9.3 8.7 %collective-permute-start.1 = (bf16[64,192]{1,0:T(8,128)(2,1)S(1)}, bf16[64,192]{1,0:T(8,128)(2,1)S(1)}, u32[]{:S(2)}, u32[]{:S(2)}) collective-permute-start(bf16[64,192]{1,0:T(8,128)(2,1)S(1)} %get-tuple-element.7), channel_id=1, source_target_pairs={{0,1},{1,0},{8,65},{9,64},{16,129},{17,128},{24,193},{25,192},{32,... | collective-permute-start | bytes 73736 | tf_op jit(solution)/shard_map/ppermute | solution.py:312
  17.2 43.6 %copy-start.7 = (bf16[32,1536]{1,0:T(8,128)(2,1)}, bf16[32,1536]{1,0:T(8,128)(2,1)S(1)}, u32[]{:S(2)}) copy-start(bf16[32,1536]{1,0:T(8,128)(2,1)S(1)} %collective-permute-done.3.refs_3_) | copy-start | bytes 294916
  17.2 43.6 %copy-start.3 = (bf16[192,1536]{1,0:T(8,128)(2,1)}, bf16[192,1536]{1,0:T(8,128)(2,1)S(1)}, u32[]{:S(2)}) copy-start(bf16[192,1536]{1,0:T(8,128)(2,1)S(1)} %collective-permute-done.2.refs_2_) | copy-start | bytes 1769476
  19.6 41.2 %all-to-all-start = ((bf16[32,32,384]{2,1,0:T(8,128)(2,1)}), bf16[32,32,384]{2,1,0:T(8,128)(2,1)S(1)}, u32[]{:S(2)}, u32[]{:S(2)}) async-start(bf16[32,32,384]{2,1,0:T(8,128)(2,1)} %shard_map.96), calls=%async_computation | async-start | bytes 1572864 | tf_op jit(solution)/shard_map/all_to_all | solution.py:18
  39.6 12.4 %collective-permute-start.4 = (bf16[192,1536]{1,0:T(8,128)(2,1)S(1)}, bf16[192,1536]{1,0:T(8,128)(2,1)S(1)}, u32[]{:S(2)}, u32[]{:S(2)}) collective-permute-start(bf16[192,1536]{1,0:T(8,128)(2,1)S(1)} %bitcast.19), channel_id=1, source_target_pairs={{0,1},{1,0},{2,3},{3,2},{4,5},{5,4},{6,7},{7,6},{8,9},{9,8},{10,11... | collective-permute-start | bytes 1769480 | tf_op jit(solution)/shard_map/ppermute | solution.py:306
  42.2 9.8 %collective-permute-start.6 = (bf16[192,1536]{1,0:T(8,128)(2,1)S(1)}, bf16[192,1536]{1,0:T(8,128)(2,1)S(1)}, u32[]{:S(2)}, u32[]{:S(2)}) collective-permute-start(bf16[192,1536]{1,0:T(8,128)(2,1)S(1)} %collective-permute-done.2.refs_2_), channel_id=1, source_target_pairs={{0,1},{1,0},{2,3},{3,2},{4,5},{5,4},{6,7},{7,6},{8,9},{9,8},{10,11... | collective-permute-start | bytes 1769480 | tf_op jit(solution)/shard_map/ppermute | solution.py:306
  44.2 7.8 %collective-permute-start.5 = (bf16[32,1536]{1,0:T(8,128)(2,1)S(1)}, bf16[32,1536]{1,0:T(8,128)(2,1)S(1)}, u32[]{:S(2)}, u32[]{:S(2)}) collective-permute-start(bf16[32,1536]{1,0:T(8,128)(2,1)S(1)} %bitcast.22), channel_id=1, source_target_pairs={{0,1},{1,0},{2,3},{3,2},{4,5},{5,4},{6,7},{7,6},{8,9},{9,8},{10,11... | collective-permute-start | bytes 294920 | tf_op jit(solution)/shard_map/ppermute | solution.py:306
  46.6 5.4 %collective-permute-start.7 = (bf16[32,1536]{1,0:T(8,128)(2,1)S(1)}, bf16[32,1536]{1,0:T(8,128)(2,1)S(1)}, u32[]{:S(2)}, u32[]{:S(2)}) collective-permute-start(bf16[32,1536]{1,0:T(8,128)(2,1)S(1)} %collective-permute-done.3.refs_3_), channel_id=1, source_target_pairs={{0,1},{1,0},{2,3},{3,2},{4,5},{5,4},{6,7},{7,6},{8,9},{9,8},{10,11... | collective-permute-start | bytes 294920 | tf_op jit(solution)/shard_map/ppermute | solution.py:306
  48.5 39.2 %collective-permute-start.9 = (bf16[192,1536]{1,0:T(8,128)(2,1)}, bf16[192,1536]{1,0:T(8,128)(2,1)}, u32[]{:S(2)}, u32[]{:S(2)}) collective-permute-start(bf16[192,1536]{1,0:T(8,128)(2,1)} %bitcast.7.refs_0_), channel_id=1, source_target_pairs={{0,8},{8,0},{1,9},{9,1},{2,10},{10,2},{3,11},{11,3},{4,12},{12,4},... | collective-permute-start | bytes 1769480 | tf_op jit(solution)/shard_map/ppermute | solution.py:308
  52.0 8.8 %copy-start.9 = (bf16[32,1536]{1,0:T(8,128)(2,1)}, bf16[32,1536]{1,0:T(8,128)(2,1)S(1)}, u32[]{:S(2)}) copy-start(bf16[32,1536]{1,0:T(8,128)(2,1)S(1)} %collective-permute-done.5.refs_5_) | copy-start | bytes 294916
  52.0 8.8 %copy-start.10 = (bf16[32,1536]{1,0:T(8,128)(2,1)}, bf16[32,1536]{1,0:T(8,128)(2,1)S(1)}, u32[]{:S(2)}) copy-start(bf16[32,1536]{1,0:T(8,128)(2,1)S(1)} %collective-permute-done.7.refs_7_) | copy-start | bytes 294916
  52.0 8.8 %copy-start.5 = (bf16[192,1536]{1,0:T(8,128)(2,1)}, bf16[192,1536]{1,0:T(8,128)(2,1)S(1)}, u32[]{:S(2)}) copy-start(bf16[192,1536]{1,0:T(8,128)(2,1)S(1)} %collective-permute-done.4.refs_4_) | copy-start | bytes 1769476
  52.0 8.8 %copy-start.6 = (bf16[192,1536]{1,0:T(8,128)(2,1)}, bf16[192,1536]{1,0:T(8,128)(2,1)S(1)}, u32[]{:S(2)}) copy-start(bf16[192,1536]{1,0:T(8,128)(2,1)S(1)} %collective-permute-done.6.refs_6_) | copy-start | bytes 1769476
  60.9 37.9 %copy-start = (bf16[24,32,1024]{2,1,0:T(8,128)(2,1)S(1)}, bf16[24,32,1024]{2,1,0:T(8,128)(2,1)}, u32[]{:S(2)}) copy-start(bf16[24,32,1024]{2,1,0:T(8,128)(2,1)} %k_pool.1) | copy-start | bytes 4718596
  60.9 37.9 %copy-start.1 = (s32[2,12]{1,0:T(2,128)S(1)}, s32[2,12]{1,0:T(2,128)}, u32[]{:S(2)}) copy-start(s32[2,12]{1,0:T(2,128)} %table.1) | copy-start | bytes 292
  60.9 37.9 %copy-start.2 = (s32[2]{0:T(128)S(1)}, s32[2]{0:T(128)}, u32[]{:S(2)}) copy-start(s32[2]{0:T(128)} %lengths.1) | copy-start | bytes 28
  66.0 32.7 %all-to-all-start.1 = ((bf16[128,2,1024]{2,1,0:T(2,128)(2,1)}), bf16[128,2,1024]{2,1,0:T(2,128)(2,1)S(1)}, u32[]{:S(2)}, u32[]{:S(2)}) async-start(bf16[128,2,1024]{2,1,0:T(2,128)(2,1)} %shard_map.97), calls=%async_computation.1 | async-start | bytes 1048576 | tf_op jit(solution)/shard_map/all_to_all | solution.py:18
  82.7 7.0 %collective-permute-start.8 = (bf16[192,1536]{1,0:T(8,128)(2,1)}, bf16[192,1536]{1,0:T(8,128)(2,1)S(1)}, u32[]{:S(2)}, u32[]{:S(2)}) collective-permute-start(bf16[192,1536]{1,0:T(8,128)(2,1)} %bitcast.7.refs_0_), channel_id=1, source_target_pairs={{0,1},{1,0},{2,3},{3,2},{4,5},{5,4},{6,7},{7,6},{8,9},{9,8},{10,11... | collective-permute-start | bytes 1769480 | tf_op jit(solution)/shard_map/ppermute | solution.py:309
  87.7 4.1 %collective-permute-start.10 = (bf16[192,1536]{1,0:T(8,128)(2,1)}, bf16[192,1536]{1,0:T(8,128)(2,1)S(1)}, u32[]{:S(2)}, u32[]{:S(2)}) collective-permute-start(bf16[192,1536]{1,0:T(8,128)(2,1)} %collective-permute-done.9.refs_1_), channel_id=1, source_target_pairs={{0,1},{1,0},{2,3},{3,2},{4,5},{5,4},{6,7},{7,6},{8,9},{9,8},{10,11... | collective-permute-start | bytes 1769480 | tf_op jit(solution)/shard_map/ppermute | solution.py:309

commit v8 on v7

--- a/solution.py
+++ b/solution.py
@@ -118,10 +118,12 @@
                 preferred_element_type=jnp.float32,
             )
     for half in range(2):
+        rounded = total[half].astype(jnp.bfloat16)
+        extra = extras[half].astype(jnp.bfloat16)
         for r in range(64):
             at = slice(2 * r, 2 * r + 2)
-            out[half * 64 + r, :, :896] = total[half][at].astype(jnp.bfloat16)
-            out[half * 64 + r, :, 896:] = extras[half][at].astype(jnp.bfloat16)
+            out[half * 64 + r, :, :896] = rounded[at]
+            out[half * 64 + r, :, 896:] = extra[at]
 
 
 def project(place, rows, pieces):
@@ -192,8 +194,9 @@
         scores = jnp.exp(scores - top)
         own = jnp.exp(own - top)
         total = jnp.sum(scores, axis=1, keepdims=True) + own
-        weights = (scores / total).astype(jnp.bfloat16)
-        found.append((weights, (own / total).astype(jnp.bfloat16).astype(jnp.float32)))
+        inverse = 1.0 / total
+        weights = (scores * inverse).astype(jnp.bfloat16)
+        found.append((weights, (own * inverse).astype(jnp.bfloat16).astype(jnp.float32)))
     fetch.wait()
     copies = []
     for g, (weights, own) in enumerate(found):
@@ -202,9 +205,9 @@
         out = lax.dot_general(
             weights, values, (((1,), (0,)), ((), ())), preferred_element_type=jnp.float32
         )
-        out = out + own * own_value
+        out = (out + own * own_value).astype(jnp.bfloat16)
         for h in range(12):
-            mixed[g, :, h * 128 : h * 128 + 128] = out[2 * h : 2 * h + 2].astype(jnp.bfloat16)
+            mixed[g, :, h * 128 : h * 128 + 128] = out[2 * h : 2 * h + 2]
         if g % 4 == 3:
             part = pl.ds(g - 3, 4)
             for k in range(16):

time: 160 us -> 160 us (level)
  no operation moved by 1% of the time
where the time goes in v8:
time: 160 us; the launch traced here: 159 us
  starting transfers between devices  71.3 us (45%)
  blocking collectives  52.2 us (33%)
  waiting for transfers between devices  18.7 us (12%)
  Pallas kernels  15.6 us (10%)
    all_to_all x2, blocking collectives, a2a(): return lax.all_to_all(a, axes, split_axis=0, concat_axis=0, tiled=True)  52.2 us
    all_to_all x2, starting transfers between devices, a2a(): return lax.all_to_all(a, axes, split_axis=0, concat_axis=0, tiled=True)  36.6 us
    all_to_all x2, waiting for transfers between devices, a2a(): return lax.all_to_all(a, axes, split_axis=0, concat_axis=0, tiled=True)  15.7 us
    ppermute x4, starting transfers between devices, per_device(): lax.ppermute(part, 'c', OTHER)  8.87 us
    ppermute x2, starting transfers between devices, per_device(): lax.ppermute(part, G + ('zq', 'zp', 'c'), [((g * 8 + z) * 2 + c, (z * 8 +...  8.54 us
    ppermute x2, starting transfers between devices, per_device(): near = [lax.ppermute(part, 'zp', OTHER) for part in own]  6.89 us
    pallas_call x1, Pallas kernels, project(): pl.pallas_call(project_kernel, in_specs=[SMEM, VMEM] + [pl.BlockSpec(memo...  5.13 us
    ppermute x1, starting transfers between devices, per_device(): lax.ppermute(o_own, 'c', OTHER)  5.01 us
  transfers between devices with their start and end apart: 13, of which 4 were waited for; matrix products, arithmetic and copies ran while one was open for 0% of the time, Pallas kernels for 4%

profile of v8, /device:TPU:1, one launch (start us, length us, event | category | flops | bytes accessed | tf_op | source)
XLA Modules:
  0.0 159.2 jit_solution(4208399093984934626)
XLA Ops:
  0.7 5.0 %collective-permute-start.2 = (bf16[192,1536]{1,0:T(8,128)(2,1)}, bf16[192,1536]{1,0:T(8,128)(2,1)S(1)}, u32[]{:S(2)}, u32[]{:S(2)}) collective-permute-start(bf16[192,1536]{1,0:T(8,128)(2,1)} %bitcast.17), channel_id=1, source_target_pairs={{0,8},{8,0},{1,9},{9,1},{2,10},{10,2},{3,11},{11,3},{4,12},{12,4},... | collective-permute-start | bytes 1769480 | tf_op jit(solution)/shard_map/ppermute | solution.py:308
  5.6 1.9 %collective-permute-start.3 = (bf16[32,1536]{1,0:T(8,128)(2,1)}, bf16[32,1536]{1,0:T(8,128)(2,1)S(1)}, u32[]{:S(2)}, u32[]{:S(2)}) collective-permute-start(bf16[32,1536]{1,0:T(8,128)(2,1)} %bitcast.20), channel_id=1, source_target_pairs={{0,8},{8,0},{1,9},{9,1},{2,10},{10,2},{3,11},{11,3},{4,12},{12,4},... | collective-permute-start | bytes 294920 | tf_op jit(solution)/shard_map/ppermute | solution.py:308
  7.6 1.0 shard_map.95
  9.3 7.9 %collective-permute-start.1 = (bf16[64,192]{1,0:T(8,128)(2,1)S(1)}, bf16[64,192]{1,0:T(8,128)(2,1)S(1)}, u32[]{:S(2)}, u32[]{:S(2)}) collective-permute-start(bf16[64,192]{1,0:T(8,128)(2,1)S(1)} %get-tuple-element.7), channel_id=1, source_target_pairs={{0,1},{1,0},{8,65},{9,64},{16,129},{17,128},{24,193},{25,192},{32,... | collective-permute-start | bytes 73736 | tf_op jit(solution)/shard_map/ppermute | solution.py:315
  17.3 0.8 collective-permute-done.1.other
  18.0 1.6 shard_map.96
  19.6 20.0 %all-to-all-start = ((bf16[32,32,384]{2,1,0:T(8,128)(2,1)}), bf16[32,32,384]{2,1,0:T(8,128)(2,1)S(1)}, u32[]{:S(2)}, u32[]{:S(2)}) async-start(bf16[32,32,384]{2,1,0:T(8,128)(2,1)} %shard_map.96), calls=%async_computation | async-start | bytes 1572864 | tf_op jit(solution)/shard_map/all_to_all | solution.py:18
  39.6 2.6 %collective-permute-start.4 = (bf16[192,1536]{1,0:T(8,128)(2,1)S(1)}, bf16[192,1536]{1,0:T(8,128)(2,1)S(1)}, u32[]{:S(2)}, u32[]{:S(2)}) collective-permute-start(bf16[192,1536]{1,0:T(8,128)(2,1)S(1)} %bitcast.19), channel_id=1, source_target_pairs={{0,1},{1,0},{2,3},{3,2},{4,5},{5,4},{6,7},{7,6},{8,9},{9,8},{10,11... | collective-permute-start | bytes 1769480 | tf_op jit(solution)/shard_map/ppermute | solution.py:309
  42.2 1.9 %collective-permute-start.6 = (bf16[192,1536]{1,0:T(8,128)(2,1)S(1)}, bf16[192,1536]{1,0:T(8,128)(2,1)S(1)}, u32[]{:S(2)}, u32[]{:S(2)}) collective-permute-start(bf16[192,1536]{1,0:T(8,128)(2,1)S(1)} %collective-permute-done.2.refs_2_), channel_id=1, source_target_pairs={{0,1},{1,0},{2,3},{3,2},{4,5},{5,4},{6,7},{7,6},{8,9},{9,8},{10,11... | collective-permute-start | bytes 1769480 | tf_op jit(solution)/shard_map/ppermute | solution.py:309
  44.2 2.4 %collective-permute-start.5 = (bf16[32,1536]{1,0:T(8,128)(2,1)S(1)}, bf16[32,1536]{1,0:T(8,128)(2,1)S(1)}, u32[]{:S(2)}, u32[]{:S(2)}) collective-permute-start(bf16[32,1536]{1,0:T(8,128)(2,1)S(1)} %bitcast.22), channel_id=1, source_target_pairs={{0,1},{1,0},{2,3},{3,2},{4,5},{5,4},{6,7},{7,6},{8,9},{9,8},{10,11... | collective-permute-start | bytes 294920 | tf_op jit(solution)/shard_map/ppermute | solution.py:309
  46.6 1.9 %collective-permute-start.7 = (bf16[32,1536]{1,0:T(8,128)(2,1)S(1)}, bf16[32,1536]{1,0:T(8,128)(2,1)S(1)}, u32[]{:S(2)}, u32[]{:S(2)}) collective-permute-start(bf16[32,1536]{1,0:T(8,128)(2,1)S(1)} %collective-permute-done.3.refs_3_), channel_id=1, source_target_pairs={{0,1},{1,0},{2,3},{3,2},{4,5},{5,4},{6,7},{7,6},{8,9},{9,8},{10,11... | collective-permute-start | bytes 294920 | tf_op jit(solution)/shard_map/ppermute | solution.py:309
  48.5 3.4 %collective-permute-start.9 = (bf16[192,1536]{1,0:T(8,128)(2,1)}, bf16[192,1536]{1,0:T(8,128)(2,1)}, u32[]{:S(2)}, u32[]{:S(2)}) collective-permute-start(bf16[192,1536]{1,0:T(8,128)(2,1)} %bitcast.7.refs_0_), channel_id=1, source_target_pairs={{0,8},{8,0},{1,9},{9,1},{2,10},{10,2},{3,11},{11,3},{4,12},{12,4},... | collective-permute-start | bytes 1769480 | tf_op jit(solution)/shard_map/ppermute | solution.py:311
  52.0 8.8 %all-to-all-done = bf16[32,32,384]{2,1,0:T(8,128)(2,1)S(1)} async-done(((bf16[32,32,384]{2,1,0:T(8,128)(2,1)}), bf16[32,32,384]{2,1,0:T(8,128)(2,1)S(1)}, u32[]{:S(2)}, u32[]{:S(2)}) %all-to-all-start) | async-done | bytes 786464 | tf_op jit(solution)/shard_map/all_to_all | solution.py:18
  60.9 5.1 %shard_map.97 = bf16[128,2,1024]{2,1,0:T(2,128)(2,1)} custom-call(s32[2]{0:T(128)S(1)} %pad_add_fusion.place, bf16[8,4,32,384]{3,2,1,0:T(8,128)(2,1)S(1)} %bitcast.12, bf16[192,1536]{1,0:T(8,128)(2,1)} %bitcast.18, bf16[32,1536]{1,0:T(8,128)(2,1)} %bitcast.21, bf16[192,1536]{1,0:T(8,128)(2,1)} %copy-done.3, bf16[32,1536]{1,0:T(8,128)(2,1)} %copy-done.7, ...), custom_call_target="tpu_custom_call" | custom-call | flops 704643072 | bytes 4194304 | tf_op jit(solution)/shard_map/pallas_call | solution.py:130
  66.0 16.6 %all-to-all-start.1 = ((bf16[128,2,1024]{2,1,0:T(2,128)(2,1)}), bf16[128,2,1024]{2,1,0:T(2,128)(2,1)S(1)}, u32[]{:S(2)}, u32[]{:S(2)}) async-start(bf16[128,2,1024]{2,1,0:T(2,128)(2,1)} %shard_map.97), calls=%async_computation.1 | async-start | bytes 1048576 | tf_op jit(solution)/shard_map/all_to_all | solution.py:18
  82.7 5.0 %collective-permute-start.8 = (bf16[192,1536]{1,0:T(8,128)(2,1)}, bf16[192,1536]{1,0:T(8,128)(2,1)S(1)}, u32[]{:S(2)}, u32[]{:S(2)}) collective-permute-start(bf16[192,1536]{1,0:T(8,128)(2,1)} %bitcast.7.refs_0_), channel_id=1, source_target_pairs={{0,1},{1,0},{2,3},{3,2},{4,5},{5,4},{6,7},{7,6},{8,9},{9,8},{10,11... | collective-permute-start | bytes 1769480 | tf_op jit(solution)/shard_map/ppermute | solution.py:312
  87.7 1.9 %collective-permute-start.10 = (bf16[192,1536]{1,0:T(8,128)(2,1)}, bf16[192,1536]{1,0:T(8,128)(2,1)S(1)}, u32[]{:S(2)}, u32[]{:S(2)}) collective-permute-start(bf16[192,1536]{1,0:T(8,128)(2,1)} %collective-permute-done.9.refs_1_), channel_id=1, source_target_pairs={{0,1},{1,0},{2,3},{3,2},{4,5},{5,4},{6,7},{7,6},{8,9},{9,8},{10,11... | collective-permute-start | bytes 1769480 | tf_op jit(solution)/shard_map/ppermute | solution.py:312
  89.6 2.2 %collective-permute-done.10.refs_3_ = bf16[192,1536]{1,0:T(8,128)(2,1)S(1)} collective-permute-done((bf16[192,1536]{1,0:T(8,128)(2,1)}, bf16[192,1536]{1,0:T(8,128)(2,1)S(1)}, u32[]{:S(2)}, u32[]{:S(2)}) %collective-permute-start.10) | collective-permute-done | bytes 589856 | tf_op jit(solution)/shard_map/ppermute | solution.py:312
  91.8 6.9 %all-to-all-done.1 = bf16[128,2,1024]{2,1,0:T(2,128)(2,1)S(1)} async-done(((bf16[128,2,1024]{2,1,0:T(2,128)(2,1)}), bf16[128,2,1024]{2,1,0:T(2,128)(2,1)S(1)}, u32[]{:S(2)}, u32[]{:S(2)}) %all-to-all-start.1) | async-done | bytes 524320 | tf_op jit(solution)/shard_map/all_to_all | solution.py:18
  98.8 4.7 %shard_map.98 = (bf16[2,2048]{1,0:T(2,128)(2,1)}, bf16[8,16,2,1536]{3,2,1,0:T(2,128)(2,1)}) custom-call(s32[2,12]{1,0:T(2,128)S(1)} %copy-done.1, s32[2]{0:T(128)S(1)} %copy-done.2, bf16[8,16,2,1024]{3,2,1,0:T(2,128)(2,1)S(1)} %bitcast.13, bf16[24,32,1024]{2,1,0:T(8,128)(2,1)S(1)} %copy-done, bf16[24,32,1024]{2,1,0:T(8,128)(2,1)} %v_pool.1, ...), custom_call_target="tpu_custom_call" | custom-call | tf_op jit(solution)/shard_map/pallas_call | solution.py:225
  103.5 31.2 %all_to_all.20 = bf16[128,2,1536]{2,1,0:T(2,128)(2,1)S(1)} all-to-all(bf16[128,2,1536]{2,1,0:T(2,128)(2,1)} %bitcast.16), channel_id=1, replica_groups=mesh['yl'=2,'x'=4,'zq'=4,'zp'=2,'yh'=4,'c'=2] {'yl','x','zq','yh'}, dimensions={0} | all-to-all | bytes 1572864 | tf_op jit(solution)/shard_map/all_to_all | solution.py:18
  135.0 2.3 %shard_map.99 = bf16[8,4,48,128]{3,2,1,0:T(8,128)(2,1)S(1)} custom-call(s32[2]{0:T(128)S(1)} %pad_add_fusion.place, bf16[256,1536]{1,0:T(8,128)(2,1)S(1)} %reshape.25.rows, bf16[192,1536]{1,0:T(8,128)(2,1)} %bitcast.7.refs_0_, bf16[192,1536]{1,0:T(8,128)(2,1)} %collective-permute-done.9.refs_1_, bf16[192,1536]{1,0:T(8,128)(2,1)S(1)} %collective-permute-done.8.refs_2_, ...), custom_call_target="tpu_custom_call" | custom-call | flops 603979776 | bytes 4194304 | tf_op jit(solution)/shard_map/pallas_call | solution.py:262
  137.3 21.0 %all_to_all.21 = bf16[32,48,128]{2,1,0:T(8,128)(2,1)S(1)} all-to-all(bf16[32,48,128]{2,1,0:T(8,128)(2,1)S(1)} %bitcast.15), channel_id=1, replica_groups=mesh['yl'=2,'x'=4,'zq'=4,'zp'=2,'yh'=4,'c'=2] {'yl','x','zp','c'}, dimensions={0} | all-to-all | bytes 786432 | tf_op jit(solution)/shard_map/all_to_all | solution.py:18
  158.3 0.9 shard_map.100
  (38 shorter events, 1.1 us)
Async XLA Ops:
  0.6 39.0 %copy-start.4 = (bf16[1536,192]{0,1:T(8,128)(2,1)S(1)}, bf16[1536,192]{0,1:T(8,128)(2,1)}, u32[]{:S(2)}) copy-start(bf16[1536,192]{0,1:T(8,128)(2,1)} %param.9) | copy-start | bytes 1769476
  0.6 43.5 %copy-start.8 = (bf16[1536,32]{0,1:T(8,128)(2,1)S(1)}, bf16[1536,32]{0,1:T(8,128)(2,1)}, u32[]{:S(2)}) copy-start(bf16[1536,32]{0,1:T(8,128)(2,1)} %param.10) | copy-start | bytes 294916
  0.7 16.6 %collective-permute-start.2 = (bf16[192,1536]{1,0:T(8,128)(2,1)}, bf16[192,1536]{1,0:T(8,128)(2,1)S(1)}, u32[]{:S(2)}, u32[]{:S(2)}) collective-permute-start(bf16[192,1536]{1,0:T(8,128)(2,1)} %bitcast.17), channel_id=1, source_target_pairs={{0,8},{8,0},{1,9},{9,1},{2,10},{10,2},{3,11},{11,3},{4,12},{12,4},... | collective-permute-start | bytes 1769480 | tf_op jit(solution)/shard_map/ppermute | solution.py:308
  5.6 11.6 %collective-permute-start.3 = (bf16[32,1536]{1,0:T(8,128)(2,1)}, bf16[32,1536]{1,0:T(8,128)(2,1)S(1)}, u32[]{:S(2)}, u32[]{:S(2)}) collective-permute-start(bf16[32,1536]{1,0:T(8,128)(2,1)} %bitcast.20), channel_id=1, source_target_pairs={{0,8},{8,0},{1,9},{9,1},{2,10},{10,2},{3,11},{11,3},{4,12},{12,4},... | collective-permute-start | bytes 294920 | tf_op jit(solution)/shard_map/ppermute | solution.py:308
  8.6 8.6 %collective-permute-start = (bf16[64,192]{1,0:T(8,128)(2,1)S(1)}, bf16[64,192]{1,0:T(8,128)(2,1)S(1)}, u32[]{:S(2)}, u32[]{:S(2)}) collective-permute-start(bf16[64,192]{1,0:T(8,128)(2,1)S(1)} %get-tuple-element.6), channel_id=1, source_target_pairs={{0,0},{1,1},{8,64},{9,65},{16,128},{17,129},{24,192},{25,193},{32,... | collective-permute-start | bytes 73736 | tf_op jit(solution)/shard_map/ppermute | solution.py:315
  9.3 8.7 %collective-permute-start.1 = (bf16[64,192]{1,0:T(8,128)(2,1)S(1)}, bf16[64,192]{1,0:T(8,128)(2,1)S(1)}, u32[]{:S(2)}, u32[]{:S(2)}) collective-permute-start(bf16[64,192]{1,0:T(8,128)(2,1)S(1)} %get-tuple-element.7), channel_id=1, source_target_pairs={{0,1},{1,0},{8,65},{9,64},{16,129},{17,128},{24,193},{25,192},{32,... | collective-permute-start | bytes 73736 | tf_op jit(solution)/shard_map/ppermute | solution.py:315
  17.2 43.6 %copy-start.7 = (bf16[32,1536]{1,0:T(8,128)(2,1)}, bf16[32,1536]{1,0:T(8,128)(2,1)S(1)}, u32[]{:S(2)}) copy-start(bf16[32,1536]{1,0:T(8,128)(2,1)S(1)} %collective-permute-done.3.refs_3_) | copy-start | bytes 294916
  17.2 43.6 %copy-start.3 = (bf16[192,1536]{1,0:T(8,128)(2,1)}, bf16[192,1536]{1,0:T(8,128)(2,1)S(1)}, u32[]{:S(2)}) copy-start(bf16[192,1536]{1,0:T(8,128)(2,1)S(1)} %collective-permute-done.2.refs_2_) | copy-start | bytes 1769476
  19.6 41.2 %all-to-all-start = ((bf16[32,32,384]{2,1,0:T(8,128)(2,1)}), bf16[32,32,384]{2,1,0:T(8,128)(2,1)S(1)}, u32[]{:S(2)}, u32[]{:S(2)}) async-start(bf16[32,32,384]{2,1,0:T(8,128)(2,1)} %shard_map.96), calls=%async_computation | async-start | bytes 1572864 | tf_op jit(solution)/shard_map/all_to_all | solution.py:18
  39.6 12.4 %collective-permute-start.4 = (bf16[192,1536]{1,0:T(8,128)(2,1)S(1)}, bf16[192,1536]{1,0:T(8,128)(2,1)S(1)}, u32[]{:S(2)}, u32[]{:S(2)}) collective-permute-start(bf16[192,1536]{1,0:T(8,128)(2,1)S(1)} %bitcast.19), channel_id=1, source_target_pairs={{0,1},{1,0},{2,3},{3,2},{4,5},{5,4},{6,7},{7,6},{8,9},{9,8},{10,11... | collective-permute-start | bytes 1769480 | tf_op jit(solution)/shard_map/ppermute | solution.py:309
  42.2 9.8 %collective-permute-start.6 = (bf16[192,1536]{1,0:T(8,128)(2,1)S(1)}, bf16[192,1536]{1,0:T(8,128)(2,1)S(1)}, u32[]{:S(2)}, u32[]{:S(2)}) collective-permute-start(bf16[192,1536]{1,0:T(8,128)(2,1)S(1)} %collective-permute-done.2.refs_2_), channel_id=1, source_target_pairs={{0,1},{1,0},{2,3},{3,2},{4,5},{5,4},{6,7},{7,6},{8,9},{9,8},{10,11... | collective-permute-start | bytes 1769480 | tf_op jit(solution)/shard_map/ppermute | solution.py:309
  44.2 7.8 %collective-permute-start.5 = (bf16[32,1536]{1,0:T(8,128)(2,1)S(1)}, bf16[32,1536]{1,0:T(8,128)(2,1)S(1)}, u32[]{:S(2)}, u32[]{:S(2)}) collective-permute-start(bf16[32,1536]{1,0:T(8,128)(2,1)S(1)} %bitcast.22), channel_id=1, source_target_pairs={{0,1},{1,0},{2,3},{3,2},{4,5},{5,4},{6,7},{7,6},{8,9},{9,8},{10,11... | collective-permute-start | bytes 294920 | tf_op jit(solution)/shard_map/ppermute | solution.py:309
  46.6 5.4 %collective-permute-start.7 = (bf16[32,1536]{1,0:T(8,128)(2,1)S(1)}, bf16[32,1536]{1,0:T(8,128)(2,1)S(1)}, u32[]{:S(2)}, u32[]{:S(2)}) collective-permute-start(bf16[32,1536]{1,0:T(8,128)(2,1)S(1)} %collective-permute-done.3.refs_3_), channel_id=1, source_target_pairs={{0,1},{1,0},{2,3},{3,2},{4,5},{5,4},{6,7},{7,6},{8,9},{9,8},{10,11... | collective-permute-start | bytes 294920 | tf_op jit(solution)/shard_map/ppermute | solution.py:309
  48.5 39.2 %collective-permute-start.9 = (bf16[192,1536]{1,0:T(8,128)(2,1)}, bf16[192,1536]{1,0:T(8,128)(2,1)}, u32[]{:S(2)}, u32[]{:S(2)}) collective-permute-start(bf16[192,1536]{1,0:T(8,128)(2,1)} %bitcast.7.refs_0_), channel_id=1, source_target_pairs={{0,8},{8,0},{1,9},{9,1},{2,10},{10,2},{3,11},{11,3},{4,12},{12,4},... | collective-permute-start | bytes 1769480 | tf_op jit(solution)/shard_map/ppermute | solution.py:311
  52.0 8.8 %copy-start.9 = (bf16[32,1536]{1,0:T(8,128)(2,1)}, bf16[32,1536]{1,0:T(8,128)(2,1)S(1)}, u32[]{:S(2)}) copy-start(bf16[32,1536]{1,0:T(8,128)(2,1)S(1)} %collective-permute-done.5.refs_5_) | copy-start | bytes 294916
  52.0 8.8 %copy-start.10 = (bf16[32,1536]{1,0:T(8,128)(2,1)}, bf16[32,1536]{1,0:T(8,128)(2,1)S(1)}, u32[]{:S(2)}) copy-start(bf16[32,1536]{1,0:T(8,128)(2,1)S(1)} %collective-permute-done.7.refs_7_) | copy-start | bytes 294916
  52.0 8.8 %copy-start.5 = (bf16[192,1536]{1,0:T(8,128)(2,1)}, bf16[192,1536]{1,0:T(8,128)(2,1)S(1)}, u32[]{:S(2)}) copy-start(bf16[192,1536]{1,0:T(8,128)(2,1)S(1)} %collective-permute-done.4.refs_4_) | copy-start | bytes 1769476
  52.0 8.8 %copy-start.6 = (bf16[192,1536]{1,0:T(8,128)(2,1)}, bf16[192,1536]{1,0:T(8,128)(2,1)S(1)}, u32[]{:S(2)}) copy-start(bf16[192,1536]{1,0:T(8,128)(2,1)S(1)} %collective-permute-done.6.refs_6_) | copy-start | bytes 1769476
  60.9 37.9 %copy-start = (bf16[24,32,1024]{2,1,0:T(8,128)(2,1)S(1)}, bf16[24,32,1024]{2,1,0:T(8,128)(2,1)}, u32[]{:S(2)}) copy-start(bf16[24,32,1024]{2,1,0:T(8,128)(2,1)} %k_pool.1) | copy-start | bytes 4718596
  60.9 37.9 %copy-start.1 = (s32[2,12]{1,0:T(2,128)S(1)}, s32[2,12]{1,0:T(2,128)}, u32[]{:S(2)}) copy-start(s32[2,12]{1,0:T(2,128)} %table.1) | copy-start | bytes 292
  60.9 37.9 %copy-start.2 = (s32[2]{0:T(128)S(1)}, s32[2]{0:T(128)}, u32[]{:S(2)}) copy-start(s32[2]{0:T(128)} %lengths.1) | copy-start | bytes 28
  66.0 32.7 %all-to-all-start.1 = ((bf16[128,2,1024]{2,1,0:T(2,128)(2,1)}), bf16[128,2,1024]{2,1,0:T(2,128)(2,1)S(1)}, u32[]{:S(2)}, u32[]{:S(2)}) async-start(bf16[128,2,1024]{2,1,0:T(2,128)(2,1)} %shard_map.97), calls=%async_computation.1 | async-start | bytes 1048576 | tf_op jit(solution)/shard_map/all_to_all | solution.py:18
  82.7 7.0 %collective-permute-start.8 = (bf16[192,1536]{1,0:T(8,128)(2,1)}, bf16[192,1536]{1,0:T(8,128)(2,1)S(1)}, u32[]{:S(2)}, u32[]{:S(2)}) collective-permute-start(bf16[192,1536]{1,0:T(8,128)(2,1)} %bitcast.7.refs_0_), channel_id=1, source_target_pairs={{0,1},{1,0},{2,3},{3,2},{4,5},{5,4},{6,7},{7,6},{8,9},{9,8},{10,11... | collective-permute-start | bytes 1769480 | tf_op jit(solution)/shard_map/ppermute | solution.py:312
  87.7 4.1 %collective-permute-start.10 = (bf16[192,1536]{1,0:T(8,128)(2,1)}, bf16[192,1536]{1,0:T(8,128)(2,1)S(1)}, u32[]{:S(2)}, u32[]{:S(2)}) collective-permute-start(bf16[192,1536]{1,0:T(8,128)(2,1)} %collective-permute-done.9.refs_1_), channel_id=1, source_target_pairs={{0,1},{1,0},{2,3},{3,2},{4,5},{5,4},{6,7},{7,6},{8,9},{9,8},{10,11... | collective-permute-start | bytes 1769480 | tf_op jit(solution)/shard_map/ppermute | solution.py:312
